TPU v7x, 32 devices: a whole 2x2x4 slice. The times are simulated.
32 devices in a mesh: dp: 8 (over z, x), mp: 4 (over y, core).
Axes of the slice: x: 2, y: 2, z: 4, core: 2. Of those that a mesh axis runs over, the one named last changes fastest.
Arguments:
- rows: bfloat16 [16384, 768], P(('dp', 'mp')), may hold values from -6 to 6
- cotangent: bfloat16 [16384, 768], P(('dp', 'mp')), may hold values from -6 to 6
- group_ids: int32 [64], P(('dp', 'mp')), may hold values from 0 to 7, as said below
- qkv_weight: bfloat16 [3, 768, 768], P(None, None, 'mp'), may hold values from -0.21875 to 0.21875
- out_weight: bfloat16 [768, 768], P('mp'), may hold values from -1.25 to 1.25
- in_weight: bfloat16 [768, 3072], P(None, 'mp'), may hold values from -0.21875 to 0.21875
- down_weight: bfloat16 [3072, 768], P('mp'), may hold values from -0.109375 to 0.109375
- vectors: float32 [6, 768], replicated
- qkv_master: float32 [3, 768, 768], P(None, 'dp', 'mp')
- qkv_first: float32 [3, 768, 768], P(None, 'dp', 'mp'), may hold values from -384 to 384
- qkv_second: float32 [3, 768, 768], P(None, 'dp', 'mp'), may hold values from 4096 to 16384
- out_master: float32 [768, 768], P('mp', 'dp')
- out_first: float32 [768, 768], P('mp', 'dp'), may hold values from -112 to 112
- out_second: float32 [768, 768], P('mp', 'dp'), may hold values from 368.64 to 1474.56
- in_master: float32 [768, 3072], P('dp', 'mp')
- in_first: float32 [768, 3072], P('dp', 'mp'), may hold values from -224 to 224
- in_second: float32 [768, 3072], P('dp', 'mp'), may hold values from 1474.56 to 5898.24
- down_master: float32 [3072, 768], P('mp', 'dp')
- down_first: float32 [3072, 768], P('mp', 'dp'), may hold values from -448 to 448
- down_second: float32 [3072, 768], P('mp', 'dp'), may hold values from 5898.24 to 23592.96
- vec_first: float32 [6, 768], replicated, may hold values from -768 to 768
- vec_second: float32 [6, 768], replicated, may hold values from 16384 to 65536
Outputs:
- out_rows: bfloat16 [16384, 768], P(('dp', 'mp'))
- input_grad: float32 [16384, 768], P(('dp', 'mp'))
- qkv_grad: float32 [3, 768, 768], P(None, 'dp', 'mp')
- out_grad: float32 [768, 768], P('mp', 'dp')
- in_grad: float32 [768, 3072], P('dp', 'mp')
- down_grad: float32 [3072, 768], P('mp', 'dp')
- qkv_first_new: float32 [3, 768, 768], P(None, 'dp', 'mp')
- qkv_second_new: float32 [3, 768, 768], P(None, 'dp', 'mp')
- qkv_new: float32 [3, 768, 768], P(None, 'dp', 'mp')
- out_first_new: float32 [768, 768], P('mp', 'dp')
- out_second_new: float32 [768, 768], P('mp', 'dp')
- out_new: float32 [768, 768], P('mp', 'dp')
- in_first_new: float32 [768, 3072], P('dp', 'mp')
- in_second_new: float32 [768, 3072], P('dp', 'mp')
- in_new: float32 [768, 3072], P('dp', 'mp')
- down_first_new: float32 [3072, 768], P('mp', 'dp')
- down_second_new: float32 [3072, 768], P('mp', 'dp')
- down_new: float32 [3072, 768], P('mp', 'dp')
- vec_grad: float32 [6, 768], replicated
- vec_first_new: float32 [6, 768], replicated
- vec_second_new: float32 [6, 768], replicated
- vec_new: float32 [6, 768], replicated
- matrix_norms: float32 [3, 4], replicated
Inputs may be any that keep to these rules, and one draw needn't show every extreme that they name: group_ids never fall from one image to the next; every group holds at least max(1, 1) images.
All inputs are finite; a program needn't handle non-finite values.
Results may differ from a plain program's by a relative error of at most 0.014.
Values may be sent and summed in bfloat16 or wider, within the bound.
No kernel may reach another device: no remote copies, remote signals or barrier semaphores. Data moves between devices by JAX's collectives and lax.ppermute only.
A program may use at most 128 MiB of HBM per device.

v0:
```python
import math

import jax
import jax.numpy as jnp
from jax import lax
from jax.experimental import pallas as pl
from jax.experimental.pallas import tpu as pltpu
from jax.sharding import PartitionSpec as P

HEAD_DIM = 64
PATCHES = 256
GROUPS = 8
STEP = 5

NORM_EPS = 1e-06
ADAM_EPS = 1e-06
MOMENT_DECAY = 0.5
LEARN_RATE = 0.5
WEIGHT_DECAY = 0.01
SCALE = HEAD_DIM ** (-0.5)

F32 = jnp.float32
BF16 = jnp.bfloat16
MB = 1024 * 1024
BIG = 16


def mm(left, right):
    return jnp.dot(left, right, preferred_element_type=F32)


def mm_nt(left, right):
    return lax.dot_general(left, right, (((1,), (1,)), ((), ())), preferred_element_type=F32)


def mm_tn(left, right):
    return lax.dot_general(left, right, (((0,), (0,)), ((), ())), preferred_element_type=F32)


def layer_stats(values):
    center = values - jnp.mean(values, axis=-1, keepdims=True)
    inverse = lax.rsqrt(jnp.mean(center * center, axis=-1, keepdims=True) + NORM_EPS)
    return center * inverse, inverse


def norm_back(grad_normed, normed, inverse):
    return inverse * (
        grad_normed
        - jnp.mean(grad_normed, axis=-1, keepdims=True)
        - normed * jnp.mean(grad_normed * normed, axis=-1, keepdims=True)
    )


def gelu_pair(t):
    size = jnp.abs(t) * (2.0**-0.5)
    k = 1.0 / (1.0 + 0.3275911 * size)
    bell = jnp.exp(-size * size)
    poly = k * (
        0.254829592
        + k * (-0.284496736 + k * (1.421413741 + k * (-1.453152027 + k * 1.061405429)))
    )
    tail = 0.5 * poly * bell
    cdf = jnp.where(t < 0, tail, 1.0 - tail)
    return t * cdf, cdf + t * bell * (1.0 / math.sqrt(2.0 * math.pi))


def put_turned(out_ref, value, pos_ref, count, start):
    turned = value.T
    part = turned.shape[0] // count
    width = turned.shape[1]
    here = pl.ds(start, width)
    if len(out_ref.shape) == 2:
        out_ref[:, here] = turned
        return
    for j in range(count):
        out_ref[pos_ref[j], :, here] = turned[j * part : (j + 1) * part]


def turned_shape(width, rows, count):
    part = width // count
    if part % 16 == 0:
        return (count, part, rows)
    return (width, rows)


def turned_order(turned, pos, count):
    width = turned.shape[0] if turned.ndim == 2 else turned.shape[0] * turned.shape[1]
    rows = turned.shape[-1]
    if turned.ndim == 2:
        shaped = turned.reshape(count, width // count, rows)
        turned = jnp.zeros_like(shaped).at[pos].set(shaped)
    return turned.reshape(width, rows)


def params(limit, **more):
    return pltpu.CompilerParams(vmem_limit_bytes=limit * MB, **more)


def full(shape):
    return pl.BlockSpec(shape, lambda *_: (0,) * len(shape), pipeline_mode=pl.Buffered(1))


SMEM = pl.BlockSpec(memory_space=pltpu.SMEM)


def start_kernel(pos_ref, pos2_ref, rows_ref, vec_ref, x_ref, xt_ref, xt2_ref, *, count):
    width, rows = rows_ref.shape[1], rows_ref.shape[0]
    for start in range(0, rows, PATCHES):
        normed, _ = layer_stats(rows_ref[start : start + PATCHES].astype(F32))
        low = (normed * vec_ref[0:1] + vec_ref[1:2]).astype(BF16)
        x_ref[start : start + PATCHES] = low
        put_turned(xt_ref, low, pos_ref, count, start)
        put_turned(xt2_ref, low, pos2_ref, count, start)


def run_start(pos, pos2, rows, vectors, count):
    r, d = rows.shape
    return pl.pallas_call(
        lambda *refs: start_kernel(*refs, count=count),
        out_shape=(
            jax.ShapeDtypeStruct((r, d), BF16),
            jax.ShapeDtypeStruct(turned_shape(d, r, count), BF16),
            jax.ShapeDtypeStruct(turned_shape(d, r, count), BF16),
        ),
        in_specs=[SMEM, SMEM, pl.BlockSpec(memory_space=pltpu.VMEM), pl.BlockSpec(memory_space=pltpu.VMEM)],
        compiler_params=params(BIG),
    )(pos, pos2, rows, vectors)


def gout_kernel(pos_ref, weight_ref, cot_ref, g_ref, gt_ref, *, count):
    rows = cot_ref.shape[0]
    for index in range(rows // PATCHES):
        start = index * PATCHES
        low = (cot_ref[start : start + PATCHES].astype(F32) * weight_ref[index]).astype(BF16)
        g_ref[start : start + PATCHES] = low
        put_turned(gt_ref, low, pos_ref, count, start)


def run_gout(pos, weight, cot, count):
    r, d = cot.shape
    return pl.pallas_call(
        lambda *refs: gout_kernel(*refs, count=count),
        out_shape=(
            jax.ShapeDtypeStruct((r, d), BF16),
            jax.ShapeDtypeStruct(turned_shape(d, r, count), BF16),
        ),
        in_specs=[SMEM, SMEM, pl.BlockSpec(memory_space=pltpu.VMEM)],
        compiler_params=params(BIG),
    )(pos, weight, cot)


def attend_shard(x, w_ref, saved_ref, probs_ref):
    cols = w_ref.shape[0] // 4
    qkv = mm_nt(x, w_ref[: 3 * cols]).astype(BF16)
    saved_ref[:, : 3 * cols] = qkv
    mixed = []
    for h in range(cols // HEAD_DIM):
        at = h * HEAD_DIM
        q = qkv[:, at : at + HEAD_DIM] * SCALE
        k = qkv[:, cols + at : cols + at + HEAD_DIM]
        v = qkv[:, 2 * cols + at : 2 * cols + at + HEAD_DIM]
        scores = mm_nt(q, k)
        expo = jnp.exp(scores - jnp.max(scores, axis=-1, keepdims=True))
        probs = (expo * (1.0 / jnp.sum(expo, axis=-1, keepdims=True))).astype(BF16)
        probs_ref[h] = probs
        mixed.append(mm(probs, v).astype(BF16))
    mixed = jnp.concatenate(mixed, axis=1)
    saved_ref[:, 3 * cols :] = mixed
    return mm(mixed, w_ref[3 * cols :])


def attn_one_kernel(x_ref, rows_ref, vec_ref, wa_ref, wb_ref, acc_ref, sa_ref, pa_ref, sb_ref, pb_ref):
    x = x_ref[...]
    term = attend_shard(x, wa_ref, sa_ref, pa_ref)
    term += attend_shard(x, wb_ref, sb_ref, pb_ref)
    acc_ref[...] = rows_ref[...].astype(F32) + term + vec_ref[4:5]


def join_halves(low_ref, own_ref, other_ref, whole_ref):
    half = own_ref.shape[0]

    @pl.when(low_ref[0] == 0)
    def _():
        whole_ref[:half] = own_ref[...]
        whole_ref[half:] = other_ref[...]

    @pl.when(low_ref[0] != 0)
    def _():
        whole_ref[:half] = other_ref[...]
        whole_ref[half:] = own_ref[...]


def join_pair(low_ref, halves, wholes):
    @pl.when(pl.program_id(0) == 0)
    def _():
        for (own, other), whole in zip(halves, wholes):
            join_halves(low_ref, own, other, whole)


def attn_two_kernel(
    pos_ref, low_ref, x_ref, acc_ref, vec_ref, ha_ref, ia_ref, hb_ref, ib_ref,
    first_ref, mid_ref, midt_ref, sa_ref, pa_ref, sb_ref, pb_ref, wa_ref, wb_ref, *, count,
):
    join_pair(low_ref, ((ha_ref, ia_ref), (hb_ref, ib_ref)), (wa_ref, wb_ref))
    x = x_ref[...]
    term = attend_shard(x, wa_ref, sa_ref, pa_ref)
    term += attend_shard(x, wb_ref, sb_ref, pb_ref)
    first = acc_ref[...] + term
    first_ref[...] = first
    normed, _ = layer_stats(first)
    low = (normed * vec_ref[2:3] + vec_ref[3:4]).astype(BF16)
    mid_ref[...] = low
    put_turned(midt_ref, low, pos_ref, count, 0)


def image_block(d):
    return pl.BlockSpec((PATCHES, d), lambda i: (i, 0))


def saved_outputs(r, d, heads):
    images = r // PATCHES
    shapes = (
        jax.ShapeDtypeStruct((r, d), BF16),
        jax.ShapeDtypeStruct((images * heads, PATCHES, PATCHES), BF16),
    )
    specs = [image_block(d), pl.BlockSpec((heads, PATCHES, PATCHES), lambda i: (i, 0, 0))]
    return shapes, specs


def cost(micros):
    return pl.CostEstimate(flops=int(micros * 10 * 1e9), bytes_accessed=int(micros * 10 * 3e6), transcendentals=0)


def run_attn_one(x, rows, vectors, wa, wb):
    r, d = x.shape
    heads = d // 4 // HEAD_DIM
    shapes, specs = saved_outputs(r, d, heads)
    return pl.pallas_call(
        attn_one_kernel,
        grid=(r // PATCHES,),
        out_shape=(jax.ShapeDtypeStruct((r, d), F32),) + shapes * 2,
        in_specs=[image_block(d), image_block(d), full(vectors.shape), full((d, d)), full((d, d))],
        out_specs=[image_block(d)] + specs * 2,
        compiler_params=params(BIG),
        cost_estimate=cost(7),
    )(x, rows, vectors, wa, wb)


def run_attn_two(pos, low, x, acc, vectors, wa, wb, count):
    r, d = x.shape
    heads = d // 4 // HEAD_DIM
    shapes, specs = saved_outputs(r, d, heads)
    tshape = turned_shape(d, r, count)
    tspec = pl.BlockSpec(
        tshape[:-1] + (PATCHES,), lambda i: (0,) * (len(tshape) - 1) + (i,)
    )
    return pl.pallas_call(
        lambda *refs: attn_two_kernel(*refs, count=count),
        grid=(r // PATCHES,),
        out_shape=(
            jax.ShapeDtypeStruct((r, d), F32),
            jax.ShapeDtypeStruct((r, d), BF16),
            jax.ShapeDtypeStruct(tshape, BF16),
        )
        + shapes * 2,
        in_specs=[SMEM, SMEM, image_block(d), image_block(d), full(vectors.shape)]
        + [full((d // 2, d))] * 4,
        out_specs=[image_block(d), image_block(d), tspec] + specs * 2,
        scratch_shapes=[pltpu.VMEM((d, d), BF16)] * 2,
        compiler_params=params(BIG),
        cost_estimate=cost(7),
    )(pos, low, x, acc, vectors, *wa, *wb)


TILES = 3


def ffn_tile(mid_ref, midt_ref, g_ref, gt_ref, w_in, w_down, gi_ref, gd_ref, y_ref, dm_ref):
    pre = mm(mid_ref[...], w_in)
    dact = mm_nt(g_ref[...], w_down)
    activ, slope = gelu_pair(pre)
    activ = activ.astype(BF16)
    dpre = (dact * slope).astype(BF16)
    y_ref[...] += mm(activ, w_down)
    dm_ref[...] += mm_nt(dpre, w_in)
    gd_ref[...] = mm(gt_ref[...], activ).astype(BF16)
    gi_ref[...] = mm(midt_ref[...], dpre).astype(BF16)


def joined(low_ref, own_ref, other_ref, axis):
    own, other = own_ref[...], other_ref[...]
    return jnp.where(
        low_ref[0] == 0,
        jnp.concatenate([own, other], axis=axis),
        jnp.concatenate([other, own], axis=axis),
    )


def ffn_near_kernel(mid_ref, midt_ref, g_ref, gt_ref, in_ref, down_ref, *rest):
    *before, y_ref, dm_ref, gi_ref, gd_ref = rest

    @pl.when(pl.program_id(0) == 0)
    def _():
        y_ref[...] = before[0][...] if before else jnp.zeros_like(y_ref)
        dm_ref[...] = before[1][...] if before else jnp.zeros_like(dm_ref)

    ffn_tile(mid_ref, midt_ref, g_ref, gt_ref, in_ref[...], down_ref[...], gi_ref, gd_ref, y_ref, dm_ref)


def ffn_far_kernel(
    low_ref, mid_ref, midt_ref, g_ref, gt_ref, ia_ref, ib_ref, da_ref, db_ref, y_in_ref, dm_in_ref,
    y_ref, dm_ref, gi_ref, gd_ref,
):
    @pl.when(pl.program_id(0) == 0)
    def _():
        y_ref[...] = y_in_ref[...]
        dm_ref[...] = dm_in_ref[...]

    w_in, w_down = joined(low_ref, ia_ref, ib_ref, 0), joined(low_ref, da_ref, db_ref, 1)
    ffn_tile(mid_ref, midt_ref, g_ref, gt_ref, w_in, w_down, gi_ref, gd_ref, y_ref, dm_ref)


def ffn_last_kernel(
    pos_ref, low_ref, weight_ref, mid_ref, midt_ref, g_ref, gt_ref, ia_ref, ib_ref, da_ref, db_ref,
    y_in_ref, dm_in_ref, first_ref, cot_ref, vec_ref,
    out_ref, gf_ref, gfl_ref, gft_ref, sums_ref, gi_ref, gd_ref, y_ref, dm_ref, *, count,
):
    ffn_far_kernel(
        low_ref, mid_ref, midt_ref, g_ref, gt_ref, ia_ref, ib_ref, da_ref, db_ref, y_in_ref, dm_in_ref,
        y_ref, dm_ref, gi_ref, gd_ref,
    )

    @pl.when(pl.program_id(0) == pl.num_programs(0) - 1)
    def _():
        chunk = 128

        def body(index, sums):
            start = pl.multiple_of(index * chunk, chunk)
            here = pl.ds(start, chunk)
            first = first_ref[here, :]
            normed, inverse = layer_stats(first)
            out_ref[here, :] = (first + y_ref[here, :] + vec_ref[5:6]).astype(BF16)
            dmid = dm_ref[here, :]
            gout = cot_ref[here, :].astype(F32) * weight_ref[start // PATCHES]
            gfirst = gout + norm_back(dmid * vec_ref[2:3], normed, inverse)
            gf_ref[here, :] = gfirst
            low = gfirst.astype(BF16)
            gfl_ref[here, :] = low
            put_turned(gft_ref, low, pos_ref, count, start)
            terms = (dmid * normed, dmid, gfirst, gout)
            return tuple(a + jnp.sum(b, axis=0, keepdims=True) for a, b in zip(sums, terms))

        zero = jnp.zeros((1, first_ref.shape[1]), F32)
        sums = lax.fori_loop(0, first_ref.shape[0] // chunk, body, (zero,) * 4)
        sums_ref[...] = jnp.concatenate(sums + sums, axis=0)


def ffn_specs(d, parts):
    tile = d // TILES
    cols = lambda rows: pl.BlockSpec((rows, tile), lambda i: (0, i))
    w_down = pl.BlockSpec((tile, d // parts), lambda i: (i, 0))
    return [cols(d // parts)] * parts + [w_down] * parts, [cols(d)] * 2


def run_ffn_near(mid, midt, g, gt, w_in, w_down, *before):
    r, d = mid.shape
    w_specs, g_specs = ffn_specs(d, 1)
    grad = jax.ShapeDtypeStruct((d, d), BF16)
    return pl.pallas_call(
        ffn_near_kernel,
        grid=(TILES,),
        out_shape=(jax.ShapeDtypeStruct((r, d), F32),) * 2 + (grad,) * 2,
        in_specs=[full((r, d)), full((d, r)), full((r, d)), full((d, r))] + w_specs + [full((r, d))] * len(before),
        out_specs=[full((r, d))] * 2 + g_specs,
        compiler_params=params(BIG),
        cost_estimate=cost(6),
    )(mid, midt, g, gt, w_in, w_down, *before)


def run_ffn_far(low, mid, midt, g, gt, w_in, w_down, y, dm):
    r, d = mid.shape
    w_specs, g_specs = ffn_specs(d, 2)
    grad = jax.ShapeDtypeStruct((d, d), BF16)
    return pl.pallas_call(
        ffn_far_kernel,
        grid=(TILES,),
        out_shape=(jax.ShapeDtypeStruct((r, d), F32),) * 2 + (grad,) * 2,
        in_specs=[SMEM, full((r, d)), full((d, r)), full((r, d)), full((d, r))] + w_specs + [full((r, d))] * 2,
        out_specs=[full((r, d))] * 2 + g_specs,
        compiler_params=params(BIG),
        cost_estimate=cost(6),
    )(low, mid, midt, g, gt, *w_in, *w_down, y, dm)


def run_ffn_last(pos, low, weight, mid, midt, g, gt, w_in, w_down, y, dm, first, cot, vectors, count):
    r, d = mid.shape
    w_specs, g_specs = ffn_specs(d, 2)
    grad = jax.ShapeDtypeStruct((d, d), BF16)
    tshape = turned_shape(d, r, count)
    return pl.pallas_call(
        lambda *refs: ffn_last_kernel(*refs, count=count),
        grid=(TILES,),
        out_shape=(
            jax.ShapeDtypeStruct((r, d), BF16),
            jax.ShapeDtypeStruct((r, d), F32),
            jax.ShapeDtypeStruct((r, d), BF16),
            jax.ShapeDtypeStruct(tshape, BF16),
            jax.ShapeDtypeStruct((8, d), F32),
        )
        + (grad,) * 2,
        in_specs=[SMEM, SMEM, SMEM, full((r, d)), full((d, r)), full((r, d)), full((d, r))]
        + w_specs
        + [full((r, d))] * 4
        + [full(vectors.shape)],
        out_specs=[full((r, d)), full((r, d)), full((r, d)), full(tshape), full((8, d))] + g_specs,
        scratch_shapes=[pltpu.VMEM((r, d), F32)] * 2,
        compiler_params=params(BIG),
        cost_estimate=cost(8),
    )(pos, low, weight, mid, midt, g, gt, *w_in, *w_down, y, dm, first, cot, vectors)


def attend_back_shard(gf, w_ref, saved_ref, probs_ref, keep_ref):
    cols = w_ref.shape[0] // 4
    start = pl.multiple_of(pl.program_id(0) * PATCHES, PATCHES)
    dmix = mm_nt(gf, w_ref[3 * cols :]).astype(BF16)
    dq, dk, dv = [], [], []
    for h in range(cols // HEAD_DIM):
        at = h * HEAD_DIM
        q = saved_ref[:, at : at + HEAD_DIM]
        k = saved_ref[:, cols + at : cols + at + HEAD_DIM]
        v = saved_ref[:, 2 * cols + at : 2 * cols + at + HEAD_DIM]
        do = dmix[:, at : at + HEAD_DIM]
        probs = probs_ref[h]
        dv.append(mm_tn(probs, do).astype(BF16))
        dp = mm_nt(do, v)
        wide = probs.astype(F32)
        ds = (SCALE * wide * (dp - jnp.sum(wide * dp, axis=-1, keepdims=True))).astype(BF16)
        dq.append(mm(ds, k).astype(BF16))
        dk.append(mm_tn(ds, q).astype(BF16))
    dqkv = jnp.concatenate(dq + dk + dv, axis=1)
    keep_ref[pl.ds(start, PATCHES), : 3 * cols] = dqkv
    keep_ref[pl.ds(start, PATCHES), 3 * cols :] = saved_ref[:, 3 * cols :]
    return mm(dqkv, w_ref[: 3 * cols])


def attn_grad(xt_ref, xt2_ref, gft_ref, keep_ref, g_ref):
    cols = keep_ref.shape[1] // 4
    g_ref[:, : 2 * cols] = mm(xt_ref[...], keep_ref[:, : 2 * cols]).astype(BF16)
    g_ref[:, 2 * cols : 3 * cols] = mm(xt2_ref[...], keep_ref[:, 2 * cols : 3 * cols]).astype(BF16)
    g_ref[:, 3 * cols :] = mm(gft_ref[...], keep_ref[:, 3 * cols :]).astype(BF16)


def back_body(gf_ref, xt_ref, xt2_ref, gft_ref, w_ref, saved_ref, probs_ref, g_ref, keep_ref):
    term = attend_back_shard(gf_ref[...], w_ref, saved_ref, probs_ref, keep_ref)

    @pl.when(pl.program_id(0) == pl.num_programs(0) - 1)
    def _():
        attn_grad(xt_ref, xt2_ref, gft_ref, keep_ref, g_ref)

    return term


def back_far_kernel(
    low_ref, gf_ref, xt_ref, xt2_ref, gft_ref, saved_ref, probs_ref, h_ref, i_ref, *rest
):
    *before, acc_ref, g_ref, keep_ref, w_ref = rest
    join_pair(low_ref, ((h_ref, i_ref),), (w_ref,))
    term = back_body(gf_ref, xt_ref, xt2_ref, gft_ref, w_ref, saved_ref, probs_ref, g_ref, keep_ref)
    if before:
        acc_ref[...] = term + before[0][...]
    else:
        acc_ref[...] = jnp.zeros_like(acc_ref)
        acc_ref[...] += term


def back_near_kernel(
    gf_ref, xt_ref, xt2_ref, gft_ref, saved_ref, probs_ref, w_ref, before_ref, acc_ref, g_ref, keep_ref
):
    term = back_body(gf_ref, xt_ref, xt2_ref, gft_ref, w_ref, saved_ref, probs_ref, g_ref, keep_ref)
    acc_ref[...] = term + before_ref[...]


def back_last_kernel(
    gf_ref, xt_ref, xt2_ref, gft_ref, saved_ref, probs_ref, w_ref, before_ref, rows_ref, gfirst_ref, vec_ref,
    ig_ref, sums_ref, g_ref, keep_ref,
):
    term = back_body(gf_ref, xt_ref, xt2_ref, gft_ref, w_ref, saved_ref, probs_ref, g_ref, keep_ref)
    grad_in = before_ref[...] + term
    normed, inverse = layer_stats(rows_ref[...].astype(F32))
    ig_ref[...] = gfirst_ref[...] + norm_back(grad_in * vec_ref[0:1], normed, inverse)
    one = jnp.sum(grad_in * normed, axis=0, keepdims=True)
    two = jnp.sum(grad_in, axis=0, keepdims=True)
    sums = jnp.concatenate([one, two] * 4, axis=0)

    @pl.when(pl.program_id(0) == 0)
    def _():
        sums_ref[...] = sums

    @pl.when(pl.program_id(0) > 0)
    def _():
        sums_ref[...] += sums


def back_call(kernel, ops, specs, outs, out_specs, far):
    gfl = ops[1] if far else ops[0]
    r, d = gfl.shape
    heads = d // 4 // HEAD_DIM
    _, saved_specs = saved_outputs(r, d, heads)
    keep, whole = pltpu.VMEM((r, d), BF16), pltpu.VMEM((d, d), BF16)
    return pl.pallas_call(
        kernel,
        grid=(r // PATCHES,),
        out_shape=tuple(outs) + (jax.ShapeDtypeStruct((d, d), BF16),),
        in_specs=([SMEM] if far else []) + [image_block(d)] + [full((d, r))] * 3 + saved_specs + specs,
        out_specs=out_specs + [full((d, d))],
        scratch_shapes=[keep, whole] if far else [keep],
        compiler_params=params(BIG),
        cost_estimate=cost(6),
    )(*ops)


def run_back_far(low, gfl, xt, xt2, gft, halves, saved, *acc):
    r, d = gfl.shape
    return back_call(
        back_far_kernel,
        [low, gfl, xt, xt2, gft, *saved, *halves, *acc],
        [full((d // 2, d))] * 2 + [image_block(d)] * len(acc),
        [jax.ShapeDtypeStruct((r, d), F32)], [image_block(d)], True,
    )


def run_back_near(gfl, xt, xt2, gft, weight, saved, acc):
    r, d = gfl.shape
    return back_call(
        back_near_kernel,
        [gfl, xt, xt2, gft, *saved, weight, acc],
        [full((d, d)), image_block(d)],
        [jax.ShapeDtypeStruct((r, d), F32)], [image_block(d)], False,
    )


def run_back_last(gfl, xt, xt2, gft, weight, saved, acc, rows, gfirst, vectors):
    r, d = gfl.shape
    return back_call(
        back_last_kernel,
        [gfl, xt, xt2, gft, *saved, weight, acc, rows, gfirst, vectors],
        [full((d, d))] + [image_block(d)] * 3 + [full(vectors.shape)],
        [jax.ShapeDtypeStruct((r, d), F32), jax.ShapeDtypeStruct((8, d), F32)],
        [image_block(d), full((8, d))], False,
    )


def swap(value, axis, bit):
    size = lax.axis_size(axis)
    return lax.ppermute(value, axis, [(i, i ^ bit) for i in range(size)])


def all_sum(value):
    for axis in ("mp", "dp"):
        bit = 1
        while bit < lax.axis_size(axis):
            value = value + swap(value, axis, bit)
            bit *= 2
    return value


def total(terms, rows=slice(None)):
    return sum(term[rows].astype(F32) for term in terms)


def columns(terms, cut):
    return tuple(term[:, cut] for term in terms)


def meet(own, partner):
    return own, swap(partner, "mp", 1)


def upper(terms):
    return total(terms, slice(terms[0].shape[0] // 2, None)).astype(BF16)


def fold(terms, bit, sent=None):
    half = terms[0].shape[0] // 2
    back = swap(upper(terms) if sent is None else sent, "dp", 1 << bit)
    return tuple(term[:half] for term in terms) + (back,)


def stacked(move, *sums):
    moved = move(jnp.concatenate(sums, axis=0))
    edges = [0]
    for value in sums:
        edges.append(edges[-1] + value.shape[0])
    return [moved[low:high] for low, high in zip(edges, edges[1:])]


def join(near, far, sent=None):
    return near + (swap(total(far).astype(BF16) if sent is None else sent, "mp", 2),)


def join_two(near_a, far_a, near_b, far_b):
    a, b = stacked(
        lambda value: swap(value, "mp", 2), total(far_a).astype(BF16), total(far_b).astype(BF16)
    )
    return near_a + (a,), near_b + (b,)


def fold_two(terms_a, terms_b, bit):
    half_a, half_b = terms_a[0].shape[0] // 2, terms_b[0].shape[0] // 2
    a, b = stacked(lambda value: swap(value, "dp", 1 << bit), upper(terms_a), upper(terms_b))
    return tuple(term[:half_a] for term in terms_a) + (a,), tuple(term[:half_b] for term in terms_b) + (b,)


CORRECTION = 1.0 - MOMENT_DECAY**STEP


def lamb_step(grad, master, first, second):
    first_new = MOMENT_DECAY * first + (1.0 - MOMENT_DECAY) * grad
    second_new = MOMENT_DECAY * second + (1.0 - MOMENT_DECAY) * grad * grad
    update = (
        first_new * (1.0 / CORRECTION) / (jnp.sqrt(second_new * (1.0 / CORRECTION)) + ADAM_EPS)
        + WEIGHT_DECAY * master
    )
    return first_new, second_new, update


def whole_sum(value):
    return jnp.sum(jnp.sum(value, axis=0, keepdims=True), axis=1, keepdims=True)


def spread(parts, width):
    lane = lax.broadcasted_iota(jnp.int32, (1, width), 1)
    return sum(jnp.where(lane == index, part, 0.0) for index, part in enumerate(parts))


def dense_step_kernel(*refs):
    ins, outs = refs[:8], refs[8:]
    parts = []
    for at in range(2):
        grad, master, first, second = (ref[...] for ref in ins[4 * at : 4 * at + 4])
        first_new, second_new, update = lamb_step(grad, master, first, second)
        for ref, value in zip(outs[3 * at : 3 * at + 3], (first_new, second_new, update)):
            ref[...] = value
        parts += [whole_sum(master * master), whole_sum(update * update)]
    outs[6][...] = spread(parts, outs[6].shape[1])


def run_dense_step(in_parts, down_parts):
    shape = jax.ShapeDtypeStruct(in_parts[0].shape, F32)
    width = in_parts[0].shape[1]
    return pl.pallas_call(
        dense_step_kernel,
        out_shape=(shape,) * 6 + (jax.ShapeDtypeStruct((1, width), F32),),
        compiler_params=params(BIG),
    )(*in_parts, *down_parts)


def attn_step_kernel(
    left_ref, right_ref, qm_ref, qf_ref, qs_ref, om_ref, of_ref, os_ref, sums_a_ref, sums_b_ref, squares_ref,
    qg_ref, qf_out, qs_out, qu_ref, og_ref, of_out, os_out, ou_ref, small_ref,
):
    cols = qm_ref.shape[2]
    left, right = left_ref[...], right_ref[...]
    master_square, update_square = 0.0, 0.0
    for index, grad in enumerate((left[:, :cols], left[:, cols:], right[:, :cols])):
        master = qm_ref[index]
        first_new, second_new, update = lamb_step(grad, master, qf_ref[index], qs_ref[index])
        qg_ref[index] = grad
        qf_out[index] = first_new
        qs_out[index] = second_new
        qu_ref[index] = update
        master_square += whole_sum(master * master)
        update_square += whole_sum(update * update)
    grad = right[:, cols:].T
    master = om_ref[...]
    first_new, second_new, update = lamb_step(grad, master, of_ref[...], os_ref[...])
    og_ref[...] = grad
    of_out[...] = first_new
    os_out[...] = second_new
    ou_ref[...] = update
    dense = squares_ref[...]
    parts = [
        master_square, whole_sum(master * master), dense[:, 0:1], dense[:, 2:3],
        update_square, whole_sum(update * update), dense[:, 1:2], dense[:, 3:4],
    ]
    width = small_ref.shape[1]
    small_ref[...] = jnp.concatenate(
        [sums_a_ref[0:2], sums_b_ref[0:4], spread(parts, width), jnp.zeros((1, width), F32)], axis=0
    )


def run_attn_step(left, right, qkv, out, sums_a, sums_b, squares):
    q, o = jax.ShapeDtypeStruct(qkv[0].shape, F32), jax.ShapeDtypeStruct(out[0].shape, F32)
    return pl.pallas_call(
        attn_step_kernel,
        out_shape=(q,) * 4 + (o,) * 4 + (jax.ShapeDtypeStruct(sums_a.shape, F32),),
        compiler_params=params(BIG),
    )(left, right, *qkv, *out, sums_a, sums_b, squares)


def final_kernel(*refs):
    small_ref, vec_ref, vf_ref, vs_ref = refs[:4]
    masters, updates, new = refs[4:8], refs[8:12], refs[12:16]
    vg_out, vf_out, vs_out, v_out, norms_ref = refs[16:]
    norms = jnp.sqrt(small_ref[6:7])
    lane = lax.broadcasted_iota(jnp.int32, norms_ref.shape, 1)
    row = lax.broadcasted_iota(jnp.int32, norms_ref.shape, 0)
    table = jnp.zeros(norms_ref.shape, F32)
    for index in range(4):
        weight, update = norms[:, index : index + 1], norms[:, 4 + index : 5 + index]
        trust = weight / (update + ADAM_EPS)
        new[index][...] = masters[index][...] - LEARN_RATE * trust * updates[index][...]
        for at, value in enumerate((weight, update, trust)):
            table = jnp.where((lane == index) & (row == at), value, table)
    norms_ref[...] = table
    grad = small_ref[0:6]
    first_new = MOMENT_DECAY * vf_ref[...] + (1.0 - MOMENT_DECAY) * grad
    second_new = MOMENT_DECAY * vs_ref[...] + (1.0 - MOMENT_DECAY) * grad * grad
    vg_out[...] = grad
    vf_out[...] = first_new
    vs_out[...] = second_new
    v_out[...] = vec_ref[...] - LEARN_RATE * (first_new * (1.0 / CORRECTION)) / (
        jnp.sqrt(second_new * (1.0 / CORRECTION)) + ADAM_EPS
    )


def run_final(small, vectors, vec_first, vec_second, masters, updates):
    shape = lambda value: jax.ShapeDtypeStruct(value.shape, F32)
    flat = lambda value: value.reshape(-1, value.shape[-1])
    outs = pl.pallas_call(
        final_kernel,
        out_shape=tuple(shape(flat(m)) for m in masters)
        + (shape(vectors),) * 4
        + (jax.ShapeDtypeStruct((3, 4), F32),),
        compiler_params=params(BIG),
    )(small, vectors, vec_first, vec_second, *(flat(m) for m in masters), *(flat(u) for u in updates))
    new = [value.reshape(m.shape) for value, m in zip(outs[:4], masters)]
    return new, outs[4:]


def after(value, *others):
    return lax.optimization_barrier((value,) + others)[0]


def shards(
    rows,
    cotangent,
    group_ids,
    qkv_weight,
    out_weight,
    in_weight,
    down_weight,
    vectors,
    qkv_master,
    qkv_first,
    qkv_second,
    out_master,
    out_first,
    out_second,
    in_master,
    in_first,
    in_second,
    down_master,
    down_first,
    down_second,
    vec_first,
    vec_second,
):
    count = lax.axis_size("dp")
    width = rows.shape[1]
    half = width // 2
    nbits = count.bit_length() - 1
    me = lax.axis_index("dp").astype(jnp.int32)
    rel = jnp.arange(count, dtype=jnp.int32) ^ me
    order1 = tuple(range(nbits))
    order2 = (1, 0) + order1[2:]
    pos, pos2 = (
        sum(((rel >> bit) & 1) << (nbits - 1 - place) for place, bit in enumerate(order))
        for order in (order1, order2)
    )
    low = (me & 1).reshape(1)

    onehot = (group_ids[:, None] == jnp.arange(GROUPS, dtype=jnp.int32)[None, :]).astype(F32)
    counts = jnp.sum(onehot, axis=0)

    attn_w = jnp.concatenate(
        [jnp.swapaxes(qkv_weight, 1, 2).reshape(-1, width), out_weight], axis=0
    )
    pieces = [
        lax.dynamic_slice_in_dim(weight, low[0] * half, half, axis)
        for weight, axis in ((attn_w, 0), (in_weight, 0), (down_weight, 1))
    ]
    counts, pieces[0] = lax.optimization_barrier((counts, pieces[0]))
    attn_far = swap(pieces[0], "mp", 2)
    counts = counts + swap(counts, "mp", 2)
    counts, *pieces = lax.optimization_barrier((counts, *pieces[1:]))
    in_far, down_far = (swap(piece, "mp", 2) for piece in pieces)
    near = [swap(weight, "mp", 1) for weight in (attn_w, in_weight, down_weight)]
    counts, attn_one, in_one, down_one = lax.optimization_barrier((counts, *near))
    counts = counts + swap(counts, "dp", 1)
    x, xt, xt2 = run_start(pos, pos2, rows, vectors, count)
    xt, xt2 = turned_order(xt, pos, count), turned_order(xt2, pos2, count)
    acc, s1, p1, s0, p0 = run_attn_one(x, rows, vectors, attn_one, attn_w)
    attn_far, counts, acc = lax.optimization_barrier((attn_far, counts, acc))
    attn_two = (attn_far, swap(attn_far, "dp", 1))
    counts = counts + swap(counts, "mp", 1)
    for bit in order1[1:]:
        counts = counts + swap(counts, "dp", 1 << bit)
    image_weight = jnp.sqrt(jnp.sum(counts) / (GROUPS * jnp.sum(onehot * counts, axis=1)))
    gout, goutt = run_gout(pos2, image_weight, cotangent, count)
    goutt = turned_order(goutt, pos2, count)
    attn_other, in_far, gout, acc = lax.optimization_barrier((attn_two[1], in_far, gout, acc))
    in_two = (in_far, swap(in_far, "dp", 1))
    attn_two = (attn_far, attn_other)
    attn_three = tuple(swap(piece, "mp", 1) for piece in attn_two)
    first, mid, midt, s3, p3, s2, p2 = run_attn_two(
        pos, low, x, acc, vectors, attn_three, attn_two, count
    )
    midt = turned_order(midt, pos, count)
    y, dm, gi1, gd1 = run_ffn_near(mid, midt, gout, goutt, in_one, down_one)
    gi1, gd1, y, down_far, _ = lax.optimization_barrier((gi1, gd1, y, down_far, in_two[1]))
    down_two = (down_far, swap(down_far, "dp", 1))
    y, dm, gi0, gd0 = run_ffn_near(mid, midt, gout, goutt, in_weight, down_weight, y, dm)
    in_near, down_near = meet(gi0, gi1), meet(gd0, gd1)
    y, down_other, in_sent, down_sent = lax.optimization_barrier(
        (y, down_two[1], upper(in_near), upper(down_near))
    )
    in_near, down_near = fold(in_near, order1[0], in_sent), fold(down_near, order2[0], down_sent)
    down_two = (down_far, down_other)
    in_three, down_three = (
        tuple(swap(piece, "mp", 1) for piece in pieces) for pieces in (in_two, down_two)
    )
    y, dm, gi3, gd3 = run_ffn_far(low, mid, midt, gout, goutt, in_three, down_three, y, dm)
    out_rows, gfirst, gfl, gft, sums_b, gi2, gd2 = run_ffn_last(
        pos2, low, image_weight, mid, midt, gout, goutt, in_two, down_two,
        y, dm, first, cotangent, vectors, count,
    )
    gft = turned_order(gft, pos2, count)
    in_far, down_far = meet(gi2, gi3), meet(gd2, gd3)
    gfl, in_sent, down_sent, _, _ = lax.optimization_barrier(
        (gfl, upper(in_far), upper(down_far), in_near[-1], down_near[-1])
    )
    in_far, down_far = fold(in_far, order1[0], in_sent), fold(down_far, order2[0], down_sent)
    gin, ga3 = run_back_far(low, gfl, xt, xt2, gft, attn_three, (s3, p3))
    gin, ga2 = run_back_far(low, gfl, xt, xt2, gft, attn_two, (s2, p2), gin)
    both = meet(ga2, ga3)
    left_far, right_far = columns(both, slice(0, half)), columns(both, slice(half, None))
    gin, left_sent, right_sent, in_sent, down_sent = lax.optimization_barrier(
        (gin, upper(left_far), upper(right_far), total(in_far).astype(BF16), total(down_far).astype(BF16))
    )
    left_far, right_far = fold(left_far, order1[0], left_sent), fold(right_far, order2[0], right_sent)
    in_grad, down_grad = join(in_near, None, in_sent), join(down_near, None, down_sent)
    gin, ga1 = run_back_near(gfl, xt, xt2, gft, attn_one, (s1, p1), gin)
    ga1, *_ = lax.optimization_barrier((ga1, left_far[-1], right_far[-1]))
    input_grad, sums_a, ga0 = run_back_last(
        gfl, xt, xt2, gft, attn_w, (s0, p0), gin, rows, gfirst, vectors
    )
    both = meet(ga0, ga1)
    left_near, right_near = columns(both, slice(0, half)), columns(both, slice(half, None))
    left_far, right_far = fold(left_far, order1[1]), fold(right_far, order2[1])
    left_near, right_near = fold(left_near, order1[0]), fold(right_near, order2[0])
    near_back, far_back = lax.optimization_barrier(
        ((left_near[-1], right_near[-1]), (left_far[-1], right_far[-1]))
    )
    left_near, right_near = left_near[:-1] + near_back[:1], right_near[:-1] + near_back[1:]
    left_far, right_far = left_far[:-1] + far_back[:1], right_far[:-1] + far_back[1:]
    left_near, right_near = fold(left_near, order1[1]), fold(right_near, order2[1])
    in_grad, down_grad = fold(in_grad, order1[1]), fold(down_grad, order2[1])
    for bit in order1[2:]:
        in_grad, down_grad = fold(in_grad, bit), fold(down_grad, bit)
        left_far, right_far = fold_two(left_far, right_far, bit)
        left_near, right_near = fold_two(left_near, right_near, bit)
    left, right = join_two(left_near, left_far, right_near, right_far)
    in_grad, down_grad, left, right = (total(terms) for terms in (in_grad, down_grad, left, right))

    down_state = (down_master.T, down_first.T, down_second.T)
    in_fn, in_sn, in_up, down_fn, down_sn, down_up, squares = run_dense_step(
        (in_grad, in_master, in_first, in_second), (down_grad,) + down_state
    )
    qkv_grad, qkv_fn, qkv_sn, qkv_up, out_grad, out_fn, out_sn, out_up, small = run_attn_step(
        left, right, (qkv_master, qkv_first, qkv_second), (out_master, out_first, out_second),
        sums_a, sums_b, squares,
    )
    new, vec_outs = run_final(
        all_sum(small), vectors, vec_first, vec_second,
        (qkv_master, out_master, in_master, down_state[0]), (qkv_up, out_up, in_up, down_up),
    )
    return (
        out_rows,
        input_grad,
        qkv_grad,
        out_grad,
        in_grad,
        down_grad.T,
        qkv_fn,
        qkv_sn,
        new[0],
        out_fn,
        out_sn,
        new[1],
        in_fn,
        in_sn,
        new[2],
        down_fn.T,
        down_sn.T,
        new[3].T,
    ) + tuple(vec_outs)


def solution(mesh):
    rows = P(("dp", "mp"), None)
    qkv_state = P(None, "dp", "mp")
    out_state = P("mp", "dp")
    in_state = P("dp", "mp")
    in_specs = (
        (rows, rows, P(("dp", "mp")), P(None, None, "mp"), P("mp", None), P(None, "mp"), P("mp", None), P())
        + (qkv_state,) * 3
        + (out_state,) * 3
        + (in_state,) * 3
        + (out_state,) * 3
        + (P(), P())
    )
    out_specs = (
        (rows, rows, qkv_state, out_state, in_state, out_state)
        + (qkv_state,) * 3
        + (out_state,) * 3
        + (in_state,) * 3
        + (out_state,) * 3
        + (P(),) * 5
    )
    return jax.shard_map(shards, mesh=mesh, in_specs=in_specs, out_specs=out_specs, check_vma=False)
```

profile of v0, /device:TPU:0, one launch (start us, length us, event | category | flops | bytes accessed | tf_op | source)
XLA Modules:
  0.0 189.8 jit_solution(12610634809877591083)
XLA Ops:
  0.7 1.4 pad_maximum_fusion.wb_ref.w_ref
  3.3 1.5 fusion
  4.8 2.7 %collective-permute-start.1 = (f32[8]{0:T(128)S(1)}, f32[8]{0:T(128)S(1)}, u32[]{:S(2)}, u32[]{:S(2)}) collective-permute-start(f32[8]{0:T(128)S(1)} %convert_reduce_fusion), channel_id=1, source_target_pairs={{0,2},{1,3},{2,0},{3,1},{4,6},{5,7},{6,4},{7,5},{8,10},{9,11},{10,... | collective-permute-start | bytes 104 | tf_op jit(solution)/shard_map/ppermute | solution.py:555
  7.5 1.2 shard_map.389
  10.0 2.0 %collective-permute-start.10 = (bf16[384,768]{1,0:T(8,128)(2,1)S(1)}, bf16[384,768]{1,0:T(8,128)(2,1)}, u32[]{:S(2)}, u32[]{:S(2)}) collective-permute-start(bf16[384,768]{1,0:T(8,128)(2,1)S(1)} %constant_dynamic-slice_fusion.1), channel_id=1, source_target_pairs={{0,2},{1,3},{2,0},{3,1},{4,6},{5,7},{6,4},{7,5},{8,10},{9,11},{10,... | collective-permute-start | bytes 1769480 | tf_op jit(solution)/shard_map/ppermute | solution.py:555
  12.0 1.5 collective-permute-start.5
  13.5 7.3 %shard_map.390 = (f32[512,768]{1,0:T(8,128)S(1)}, bf16[512,768]{1,0:T(8,128)(2,1)S(1)}, bf16[6,256,256]{2,1,0:T(8,128)(2,1)S(1)}, bf16[512,768]{1,0:T(8,128)(2,1)S(1)}, bf16[6,256,256]{2,1,0:T(8,128)(2,1)S(1)}) custom-call(bf16[512,768]{1,0:T(8,128)(2,1)S(1)} %get-tuple-element.134.x_ref.refs_2_, bf16[512,768]{1,0:T(8,128)(2,1)S(1)} %copy-done.11, ...), custom_call_target="tpu_custom_call" | custom-call | flops 70000001024 | bytes 210000000 | tf_op jit(solution)/shard_map/pallas_call | solution.py:238
  20.8 2.8 %collective-permute-done.refs_7_.h_ref = bf16[384,768]{1,0:T(8,128)(2,1)S(1)} collective-permute-done((bf16[384,768]{1,0:T(8,128)(2,1)S(1)}, bf16[384,768]{1,0:T(8,128)(2,1)S(1)}, u32[]{:S(2)}, u32[]{:S(2)}) %collective-permute-start) | collective-permute-done | bytes 589856 | tf_op jit(solution)/shard_map/ppermute | solution.py:555
  23.6 1.4 collective-permute-start.9
  25.5 1.5 collective-permute-done.6
  27.0 1.6 collective-permute-start.7
  28.6 2.0 %collective-permute-done.7 = f32[8]{0:T(128)S(1)} collective-permute-done((f32[8]{0:T(128)S(1)}, f32[8]{0:T(128)S(1)}, u32[]{:S(2)}, u32[]{:S(2)}) %collective-permute-start.7) | collective-permute-done | bytes 64 | tf_op jit(solution)/shard_map/ppermute | solution.py:555
  30.6 2.6 %collective-permute-start.8 = (f32[8]{0:T(128)S(1)}, f32[8]{0:T(128)S(1)}, u32[]{:S(2)}, u32[]{:S(2)}) collective-permute-start(f32[8]{0:T(128)S(1)} %add.277), channel_id=1, source_target_pairs={{0,16},{4,20},{8,24},{12,28},{16,0},{20,4},{24,8},{28,12},{1,17},{... | collective-permute-start | bytes 104 | tf_op jit(solution)/shard_map/ppermute | solution.py:555
  33.2 1.9 collective-permute-done.8
  39.6 7.4 %shard_map.392 = (f32[512,768]{1,0:T(8,128)S(1)}, bf16[512,768]{1,0:T(8,128)(2,1)S(1)}, bf16[8,96,512]{2,1,0:T(8,128)(2,1)S(1)}, bf16[512,768]{1,0:T(8,128)(2,1)...) custom-call(s32[8]{0:T(128)S(1)} %get-tuple-element.255.refs_0_, ...), custom_call_target="tpu_custom_call" | custom-call | flops 70000001024 | bytes 210000000 | tf_op jit(solution)/shard_map/pallas_call | solution.py:257
  47.1 6.9 %shard_map.393 = (f32[512,768]{1,0:T(8,128)S(1)}, f32[512,768]{1,0:T(8,128)S(1)}, bf16[768,768]{1,0:T(8,128)(2,1)S(1)}, bf16[768,768]{1,0:T(8,128)(2,1)S(1)}) custom-call(bf16[512,768]{1,0:T(8,128)(2,1)S(1)} %get-tuple-element.144.mid_ref.refs_3_, bf16[768,512]{1,0:T(8,128)(2,1)S(1)} %bitcast.42, bf16[512,768]{1,0:T(8,128)(2,1)S(1)} %get-tuple-element.146.g_ref.refs_5_, ...), custom_call_target="tpu_custom_call" | custom-call | flops 60000002048 | bytes 180000000 | tf_op jit(solution)/shard_map/pallas_call | solution.py:369
  54.1 1.3 collective-permute-start.15
  55.9 6.8 %shard_map.394 = (f32[512,768]{1,0:T(8,128)S(1)}, f32[512,768]{1,0:T(8,128)S(1)}, bf16[768,768]{1,0:T(8,128)(2,1)S(1)}, bf16[768,768]{1,0:T(8,128)(2,1)S(1)}) custom-call(bf16[512,768]{1,0:T(8,128)(2,1)S(1)} %get-tuple-element.144.mid_ref.refs_3_, bf16[768,512]{1,0:T(8,128)(2,1)S(1)} %bitcast.43, bf16[512,768]{1,0:T(8,128)(2,1)S(1)} %get-tuple-element.146.g_ref.refs_5_, ...), custom_call_target="tpu_custom_call" | custom-call | flops 60000002048 | bytes 180000000 | tf_op jit(solution)/shard_map/pallas_call | solution.py:369
  64.5 5.3 %collective-permute-done.15.refs_10_ = bf16[768,384]{1,0:T(8,128)(2,1)S(1)} collective-permute-done((bf16[768,384]{1,0:T(8,128)(2,1)S(1)}, bf16[768,384]{1,0:T(8,128)(2,1)S(1)}, u32[]{:S(2)}, u32[]{:S(2)}) %collective-permute-start.15) | collective-permute-done | bytes 589856 | tf_op jit(solution)/shard_map/ppermute | solution.py:555
  71.0 1.6 collective-permute-start.25
  72.6 7.0 %shard_map.395 = (f32[512,768]{1,0:T(8,128)S(1)}, f32[512,768]{1,0:T(8,128)S(1)}, bf16[768,768]{1,0:T(8,128)(2,1)S(1)}, bf16[768,768]{1,0:T(8,128)(2,1)S(1)}) custom-call(s32[1]{0:T(128)} %bitcast.refs_1_.low_ref, bf16[512,768]{1,0:T(8,128)(2,1)S(1)} %get-tuple-element.144.mid_ref.refs_3_, bf16[768,512]{1,0:T(8,128)(2,1)S(1)} %bitcast.44, ...), custom_call_target="tpu_custom_call" | custom-call | flops 60000002048 | bytes 180000000 | tf_op jit(solution)/shard_map/pallas_call | solution.py:384
  80.2 9.6 %shard_map.396 = (bf16[512,768]{1,0:T(8,128)(2,1)}, f32[512,768]{1,0:T(8,128)S(1)}, bf16[512,768]{1,0:T(8,128)(2,1)S(1)}, bf16[8,96,512]{2,1,0:T(8,128)(2,1)S(1)...) custom-call(s32[8]{0:T(128)S(1)} %copy-done.26, s32[1]{0:T(128)} %bitcast.refs_1_.low_ref, ...), custom_call_target="tpu_custom_call" | custom-call | flops 80000000000 | bytes 240000000 | tf_op jit(solution)/shard_map/pallas_call | solution.py:400
  92.3 5.6 %shard_map.397 = (f32[512,768]{1,0:T(8,128)S(1)}, bf16[768,768]{1,0:T(8,128)(2,1)S(1)}) custom-call(s32[1]{0:T(128)} %bitcast.refs_1_.low_ref, bf16[512,768]{1,0:T(8,128)(2,1)S(1)} %get-tuple-element.177.gf_ref, bf16[768,512]{1,0:T(8,128)(2,1)S(1)} %bitcast.26, bf16[768,512]{1,0:T(8,128)(2,1)S(1)} %bitcast.30, bf16[768,512]{1,0:T(8,128)(2,1)S(1)} %bitcast.38, ...), custom_call_target="tpu_custom_call" | custom-call | flops 60000002048 | bytes 180000000 | tf_op jit(solution)/shard_map/pallas_call | solution.py:510
  98.0 5.7 %shard_map.398 = (f32[512,768]{1,0:T(8,128)S(1)}, bf16[768,768]{1,0:T(8,128)(2,1)S(1)}) custom-call(s32[1]{0:T(128)} %bitcast.refs_1_.low_ref, bf16[512,768]{1,0:T(8,128)(2,1)S(1)} %get-tuple-element.177.gf_ref, bf16[768,512]{1,0:T(8,128)(2,1)S(1)} %bitcast.27, bf16[768,512]{1,0:T(8,128)(2,1)S(1)} %bitcast.31, bf16[768,512]{1,0:T(8,128)(2,1)S(1)} %bitcast.39, ...), custom_call_target="tpu_custom_call" | custom-call | flops 60000002048 | bytes 180000000 | tf_op jit(solution)/shard_map/pallas_call | solution.py:510
  103.7 1.9 %collective-permute-done.27 = bf16[384,768]{1,0:T(8,128)(2,1)S(1)} collective-permute-done((bf16[384,768]{1,0:T(8,128)(2,1)S(1)}, bf16[384,768]{1,0:T(8,128)(2,1)S(1)}, u32[]{:S(2)}, u32[]{:S(2)}) %collective-permute-start.27) | collective-permute-done | bytes 589856 | tf_op jit(solution)/shard_map/ppermute | solution.py:555
  106.6 1.3 collective-permute-start.29
  108.6 1.5 collective-permute-start.41
  110.6 7.0 %shard_map.399 = (f32[512,768]{1,0:T(8,128)S(1)}, bf16[768,768]{1,0:T(8,128)(2,1)S(1)}) custom-call(bf16[512,768]{1,0:T(8,128)(2,1)S(1)} %get-tuple-element.177.gf_ref, bf16[768,512]{1,0:T(8,128)(2,1)S(1)} %bitcast.28, bf16[768,512]{1,0:T(8,128)(2,1)S(1)} %bitcast.32, bf16[768,512]{1,0:T(8,128)(2,1)S(1)} %bitcast.40, ...), custom_call_target="tpu_custom_call" | custom-call | flops 60000002048 | bytes 180000000 | tf_op jit(solution)/shard_map/pallas_call | solution.py:510
  117.8 7.5 %shard_map.400 = (f32[512,768]{1,0:T(8,128)}, f32[8,768]{1,0:T(8,128)S(1)}, bf16[768,768]{1,0:T(8,128)(2,1)S(1)}) custom-call(bf16[512,768]{1,0:T(8,128)(2,1)S(1)} %get-tuple-element.177.gf_ref, bf16[768,512]{1,0:T(8,128)(2,1)S(1)} %bitcast.29, bf16[768,512]{1,0:T(8,128)(2,1)S(1)} %bitcast.33, bf16[768,512]{1,0:T(8,128)(2,1)S(1)} %bitcast.41, ...), custom_call_target="tpu_custom_call" | custom-call | flops 60000002048 | bytes 180000000 | tf_op jit(solution)/shard_map/pallas_call | solution.py:510
  125.5 1.3 collective-permute-start.42
  128.9 5.9 %collective-permute-done.44 = bf16[384,768]{1,0:T(8,128)(2,1)S(1)} collective-permute-done((bf16[384,768]{1,0:T(8,128)(2,1)S(1)}, bf16[384,768]{1,0:T(8,128)(2,1)S(1)}, u32[]{:S(2)}, u32[]{:S(2)}) %collective-permute-start.44) | collective-permute-done | bytes 589856 | tf_op jit(solution)/shard_map/ppermute | solution.py:555
  135.0 1.2 collective-permute-start.45
  136.4 2.7 %collective-permute-start.43 = (bf16[96,768]{1,0:T(8,128)(2,1)S(1)}, bf16[96,768]{1,0:T(8,128)(2,1)S(1)}, u32[]{:S(2)}, u32[]{:S(2)}) collective-permute-start(bf16[96,768]{1,0:T(8,128)(2,1)S(1)} %add_convert_fusion.13), channel_id=1, source_target_pairs={{0,16},{4,20},{8,24},{12,28},{16,0},{20,4},{24,8},{28,12},{1,17},{... | collective-permute-start | bytes 442376 | tf_op jit(solution)/shard_map/ppermute | solution.py:555
  140.1 2.6 %collective-permute-done.45 = bf16[192,768]{1,0:T(8,128)(2,1)S(1)} collective-permute-done((bf16[192,768]{1,0:T(8,128)(2,1)S(1)}, bf16[192,768]{1,0:T(8,128)(2,1)S(1)}, u32[]{:S(2)}, u32[]{:S(2)}) %collective-permute-start.45) | collective-permute-done | bytes 294944 | tf_op jit(solution)/shard_map/ppermute | solution.py:555
  144.0 1.8 collective-permute-done.43
  146.9 2.5 %collective-permute-done.33 = bf16[384,384]{1,0:T(8,128)(2,1)S(1)} collective-permute-done((bf16[384,384]{1,0:T(8,128)(2,1)S(1)}, bf16[384,384]{1,0:T(8,128)(2,1)S(1)}, u32[]{:S(2)}, u32[]{:S(2)}) %collective-permute-start.33) | collective-permute-done | bytes 294944 | tf_op jit(solution)/shard_map/ppermute | solution.py:555
  149.6 2.5 %collective-permute-start.39 = (bf16[192,384]{1,0:T(8,128)(2,1)S(1)}, bf16[192,384]{1,0:T(8,128)(2,1)S(1)}, u32[]{:S(2)}, u32[]{:S(2)}) collective-permute-start(bf16[192,384]{1,0:T(8,128)(2,1)S(1)} %pad_maximum_fusion.2), channel_id=1, source_target_pairs={{0,16},{4,20},{8,24},{12,28},{16,0},{20,4},{24,8},{28,12},{1,17},{... | collective-permute-start | bytes 442376 | tf_op jit(solution)/shard_map/ppermute | solution.py:555
  152.2 1.3 collective-permute-start.36
  154.3 6.2 %collective-permute-done.39 = bf16[192,384]{1,0:T(8,128)(2,1)S(1)} collective-permute-done((bf16[192,384]{1,0:T(8,128)(2,1)S(1)}, bf16[192,384]{1,0:T(8,128)(2,1)S(1)}, u32[]{:S(2)}, u32[]{:S(2)}) %collective-permute-start.39) | collective-permute-done | bytes 147488 | tf_op jit(solution)/shard_map/ppermute | solution.py:555
  160.7 1.6 collective-permute-start.40
  162.7 1.7 shard_map.401
  164.4 1.5 collective-permute-done.40
  165.9 3.7 %collective-permute-done.38 = bf16[192,384]{1,0:T(8,128)(2,1)S(1)} collective-permute-done((bf16[192,384]{1,0:T(8,128)(2,1)S(1)}, bf16[192,384]{1,0:T(8,128)(2,1)S(1)}, u32[]{:S(2)}, u32[]{:S(2)}) %collective-permute-start.38) | collective-permute-done | bytes 147488 | tf_op jit(solution)/shard_map/ppermute | solution.py:555
  169.8 1.4 shard_map.402
  173.0 3.3 %collective-permute-done.48 = f32[8,768]{1,0:T(8,128)S(1)} collective-permute-done((f32[8,768]{1,0:T(8,128)S(1)}, f32[8,768]{1,0:T(8,128)S(1)}, u32[]{:S(2)}, u32[]{:S(2)}) %collective-permute-start.48) | collective-permute-done | bytes 24608 | tf_op jit(solution)/shard_map/ppermute | solution.py:555
  177.2 3.0 %collective-permute-done.49 = f32[8,768]{1,0:T(8,128)S(1)} collective-permute-done((f32[8,768]{1,0:T(8,128)S(1)}, f32[8,768]{1,0:T(8,128)S(1)}, u32[]{:S(2)}, u32[]{:S(2)}) %collective-permute-start.49) | collective-permute-done | bytes 24608 | tf_op jit(solution)/shard_map/ppermute | solution.py:555
  180.1 3.8 %collective-permute-done.50 = f32[8,768]{1,0:T(8,128)S(1)} collective-permute-done((f32[8,768]{1,0:T(8,128)S(1)}, f32[8,768]{1,0:T(8,128)S(1)}, u32[]{:S(2)}, u32[]{:S(2)}) %collective-permute-start.50) | collective-permute-done | bytes 24608 | tf_op jit(solution)/shard_map/ppermute | solution.py:555
  185.0 3.7 %collective-permute-done.51 = f32[8,768]{1,0:T(8,128)S(1)} collective-permute-done((f32[8,768]{1,0:T(8,128)S(1)}, f32[8,768]{1,0:T(8,128)S(1)}, u32[]{:S(2)}, u32[]{:S(2)}) %collective-permute-start.51) | collective-permute-done | bytes 24608 | tf_op jit(solution)/shard_map/ppermute | solution.py:555
  (206 shorter events, 28.8 us)
Async XLA Ops:
  2.2 9.8 %collective-permute-start.2 = (bf16[768,768]{1,0:T(8,128)(2,1)S(1)}, bf16[768,768]{1,0:T(8,128)(2,1)}, u32[]{:S(2)}, u32[]{:S(2)}) collective-permute-start(bf16[768,768]{1,0:T(8,128)(2,1)S(1)} %pad_maximum_fusion.wb_ref.w_ref), channel_id=1, source_target_pairs={{0,1},{1,0},{2,3},{3,2},{4,5},{5,4},{6,7},{7,6},{8,9},{9,8},{10,11... | collective-permute-start | bytes 3538952 | tf_op jit(solution)/shard_map/ppermute | solution.py:555
  2.7 9.3 %collective-permute-start.3 = (bf16[768,768]{1,0:T(8,128)(2,1)S(1)}, bf16[768,768]{1,0:T(8,128)(2,1)}, u32[]{:S(2)}, u32[]{:S(2)}) collective-permute-start(bf16[768,768]{1,0:T(8,128)(2,1)S(1)} %copy-done.17), channel_id=1, source_target_pairs={{0,1},{1,0},{2,3},{3,2},{4,5},{5,4},{6,7},{7,6},{8,9},{9,8},{10,11... | collective-permute-start | bytes 3538952 | tf_op jit(solution)/shard_map/ppermute | solution.py:555
  2.8 9.2 %collective-permute-start.4 = (bf16[768,768]{1,0:T(8,128)(2,1)}, bf16[768,768]{1,0:T(8,128)(2,1)}, u32[]{:S(2)}, u32[]{:S(2)}) collective-permute-start(bf16[768,768]{1,0:T(8,128)(2,1)} %down_ref.1), channel_id=1, source_target_pairs={{0,1},{1,0},{2,3},{3,2},{4,5},{5,4},{6,7},{7,6},{8,9},{9,8},{10,11... | collective-permute-start | bytes 3538952 | tf_op jit(solution)/shard_map/ppermute | solution.py:555
  4.8 5.2 %collective-permute-start.1 = (f32[8]{0:T(128)S(1)}, f32[8]{0:T(128)S(1)}, u32[]{:S(2)}, u32[]{:S(2)}) collective-permute-start(f32[8]{0:T(128)S(1)} %convert_reduce_fusion), channel_id=1, source_target_pairs={{0,2},{1,3},{2,0},{3,1},{4,6},{5,7},{6,4},{7,5},{8,10},{9,11},{10,... | collective-permute-start | bytes 104 | tf_op jit(solution)/shard_map/ppermute | solution.py:555
  7.4 16.2 %collective-permute-start = (bf16[384,768]{1,0:T(8,128)(2,1)S(1)}, bf16[384,768]{1,0:T(8,128)(2,1)S(1)}, u32[]{:S(2)}, u32[]{:S(2)}) collective-permute-start(bf16[384,768]{1,0:T(8,128)(2,1)S(1)} %fusion), channel_id=1, source_target_pairs={{0,2},{1,3},{2,0},{3,1},{4,6},{5,7},{6,4},{7,5},{8,10},{9,11},{10,... | collective-permute-start | bytes 1769480 | tf_op jit(solution)/shard_map/ppermute | solution.py:555
  10.0 27.3 %collective-permute-start.10 = (bf16[384,768]{1,0:T(8,128)(2,1)S(1)}, bf16[384,768]{1,0:T(8,128)(2,1)}, u32[]{:S(2)}, u32[]{:S(2)}) collective-permute-start(bf16[384,768]{1,0:T(8,128)(2,1)S(1)} %constant_dynamic-slice_fusion.1), channel_id=1, source_target_pairs={{0,2},{1,3},{2,0},{3,1},{4,6},{5,7},{6,4},{7,5},{8,10},{9,11},{10,... | collective-permute-start | bytes 1769480 | tf_op jit(solution)/shard_map/ppermute | solution.py:555
  12.0 8.8 %collective-permute-start.5 = (f32[8]{0:T(128)S(1)}, f32[8]{0:T(128)S(1)}, u32[]{:S(2)}, u32[]{:S(2)}) collective-permute-start(f32[8]{0:T(128)S(1)} %add.272), channel_id=1, source_target_pairs={{0,4},{4,0},{8,12},{12,8},{16,20},{20,16},{24,28},{28,24},{1,5},{5... | collective-permute-start | bytes 104 | tf_op jit(solution)/shard_map/ppermute | solution.py:555
  23.6 13.8 %collective-permute-start.9 = (bf16[384,768]{1,0:T(8,128)(2,1)S(1)}, bf16[384,768]{1,0:T(8,128)(2,1)S(1)}, u32[]{:S(2)}, u32[]{:S(2)}) collective-permute-start(bf16[384,768]{1,0:T(8,128)(2,1)S(1)} %collective-permute-done.refs_7_.h_ref), channel_id=1, source_target_pairs={{0,4},{4,0},{8,12},{12,8},{16,20},{20,16},{24,28},{28,24},{1,5},{5... | collective-permute-start | bytes 1769480 | tf_op jit(solution)/shard_map/ppermute | solution.py:555
  25.0 14.5 %collective-permute-start.11 = (bf16[384,768]{1,0:T(8,128)(2,1)S(1)}, bf16[384,768]{1,0:T(8,128)(2,1)S(1)}, u32[]{:S(2)}, u32[]{:S(2)}) collective-permute-start(bf16[384,768]{1,0:T(8,128)(2,1)S(1)} %collective-permute-done.refs_7_.h_ref), channel_id=1, source_target_pairs={{0,1},{1,0},{2,3},{3,2},{4,5},{5,4},{6,7},{7,6},{8,9},{9,8},{10,11... | collective-permute-start | bytes 1769480 | tf_op jit(solution)/shard_map/ppermute | solution.py:555
  27.0 3.5 %collective-permute-start.7 = (f32[8]{0:T(128)S(1)}, f32[8]{0:T(128)S(1)}, u32[]{:S(2)}, u32[]{:S(2)}) collective-permute-start(f32[8]{0:T(128)S(1)} %add.276), channel_id=1, source_target_pairs={{0,8},{4,12},{8,0},{12,4},{16,24},{20,28},{24,16},{28,20},{1,9},{5... | collective-permute-start | bytes 104 | tf_op jit(solution)/shard_map/ppermute | solution.py:555
  30.6 4.4 %collective-permute-start.8 = (f32[8]{0:T(128)S(1)}, f32[8]{0:T(128)S(1)}, u32[]{:S(2)}, u32[]{:S(2)}) collective-permute-start(f32[8]{0:T(128)S(1)} %add.277), channel_id=1, source_target_pairs={{0,16},{4,20},{8,24},{12,28},{16,0},{20,4},{24,8},{28,12},{1,17},{... | collective-permute-start | bytes 104 | tf_op jit(solution)/shard_map/ppermute | solution.py:555
  37.4 16.5 %collective-permute-start.14 = (bf16[768,384]{1,0:T(8,128)(2,1)S(1)}, bf16[768,384]{1,0:T(8,128)(2,1)S(1)}, u32[]{:S(2)}, u32[]{:S(2)}) collective-permute-start(bf16[768,384]{1,0:T(8,128)(2,1)S(1)} %constant_dynamic-slice_fusion), channel_id=1, source_target_pairs={{0,2},{1,3},{2,0},{3,1},{4,6},{5,7},{6,4},{7,5},{8,10},{9,11},{10,... | collective-permute-start | bytes 1769480 | tf_op jit(solution)/shard_map/ppermute | solution.py:555
  38.1 32.9 %collective-permute-start.18 = (bf16[384,768]{1,0:T(8,128)(2,1)}, bf16[384,768]{1,0:T(8,128)(2,1)}, u32[]{:S(2)}, u32[]{:S(2)}) collective-permute-start(bf16[384,768]{1,0:T(8,128)(2,1)} %collective-permute-done.10.refs_7_), channel_id=1, source_target_pairs={{0,1},{1,0},{2,3},{3,2},{4,5},{5,4},{6,7},{7,6},{8,9},{9,8},{10,11... | collective-permute-start | bytes 1769480 | tf_op jit(solution)/shard_map/ppermute | solution.py:555
  38.3 15.7 %collective-permute-start.13 = (bf16[384,768]{1,0:T(8,128)(2,1)}, bf16[384,768]{1,0:T(8,128)(2,1)S(1)}, u32[]{:S(2)}, u32[]{:S(2)}) collective-permute-start(bf16[384,768]{1,0:T(8,128)(2,1)} %collective-permute-done.10.refs_7_), channel_id=1, source_target_pairs={{0,4},{4,0},{8,12},{12,8},{16,20},{20,16},{24,28},{28,24},{1,5},{5... | collective-permute-start | bytes 1769480 | tf_op jit(solution)/shard_map/ppermute | solution.py:555
  54.0 18.6 %collective-permute-start.20 = (bf16[768,384]{1,0:T(8,128)(2,1)S(1)}, bf16[768,384]{1,0:T(8,128)(2,1)S(1)}, u32[]{:S(2)}, u32[]{:S(2)}) collective-permute-start(bf16[768,384]{1,0:T(8,128)(2,1)S(1)} %collective-permute-done.14.refs_9_), channel_id=1, source_target_pairs={{0,1},{1,0},{2,3},{3,2},{4,5},{5,4},{6,7},{7,6},{8,9},{9,8},{10,11... | collective-permute-start | bytes 1769480 | tf_op jit(solution)/shard_map/ppermute | solution.py:555
  54.1 15.7 %collective-permute-start.15 = (bf16[768,384]{1,0:T(8,128)(2,1)S(1)}, bf16[768,384]{1,0:T(8,128)(2,1)S(1)}, u32[]{:S(2)}, u32[]{:S(2)}) collective-permute-start(bf16[768,384]{1,0:T(8,128)(2,1)S(1)} %collective-permute-done.14.refs_9_), channel_id=1, source_target_pairs={{0,4},{4,0},{8,12},{12,8},{16,20},{20,16},{24,28},{28,24},{1,5},{5... | collective-permute-start | bytes 1769480 | tf_op jit(solution)/shard_map/ppermute | solution.py:555
  55.4 7.3 %collective-permute-start.16 = (bf16[768,768]{1,0:T(8,128)(2,1)S(1)}, bf16[768,768]{1,0:T(8,128)(2,1)S(1)}, u32[]{:S(2)}, u32[]{:S(2)}) collective-permute-start(bf16[768,768]{1,0:T(8,128)(2,1)S(1)} %get-tuple-element.160), channel_id=1, source_target_pairs={{0,1},{1,0},{2,3},{3,2},{4,5},{5,4},{6,7},{7,6},{8,9},{9,8},{10,11... | collective-permute-start | bytes 3538952 | tf_op jit(solution)/shard_map/ppermute | solution.py:555
  55.5 7.6 %collective-permute-start.17 = (bf16[768,768]{1,0:T(8,128)(2,1)S(1)}, bf16[768,768]{1,0:T(8,128)(2,1)S(1)}, u32[]{:S(2)}, u32[]{:S(2)}) collective-permute-start(bf16[768,768]{1,0:T(8,128)(2,1)S(1)} %get-tuple-element.162), channel_id=1, source_target_pairs={{0,1},{1,0},{2,3},{3,2},{4,5},{5,4},{6,7},{7,6},{8,9},{9,8},{10,11... | collective-permute-start | bytes 3538952 | tf_op jit(solution)/shard_map/ppermute | solution.py:555
  62.8 9.8 %collective-permute-start.19 = (bf16[384,768]{1,0:T(8,128)(2,1)S(1)}, bf16[384,768]{1,0:T(8,128)(2,1)S(1)}, u32[]{:S(2)}, u32[]{:S(2)}) collective-permute-start(bf16[384,768]{1,0:T(8,128)(2,1)S(1)} %collective-permute-done.13.refs_8_), channel_id=1, source_target_pairs={{0,1},{1,0},{2,3},{3,2},{4,5},{5,4},{6,7},{7,6},{8,9},{9,8},{10,11... | collective-permute-start | bytes 1769480 | tf_op jit(solution)/shard_map/ppermute | solution.py:555
  69.8 20.4 %collective-permute-start.24 = (bf16[384,768]{1,0:T(8,128)(2,1)S(1)}, bf16[384,768]{1,0:T(8,128)(2,1)S(1)}, u32[]{:S(2)}, u32[]{:S(2)}) collective-permute-start(bf16[384,768]{1,0:T(8,128)(2,1)S(1)} %add_convert_fusion.5), channel_id=1, source_target_pairs={{0,4},{4,0},{8,12},{12,8},{16,20},{20,16},{24,28},{28,24},{1,5},{5... | collective-permute-start | bytes 1769480 | tf_op jit(solution)/shard_map/ppermute | solution.py:555
  71.0 19.2 %collective-permute-start.25 = (bf16[384,768]{1,0:T(8,128)(2,1)S(1)}, bf16[384,768]{1,0:T(8,128)(2,1)S(1)}, u32[]{:S(2)}, u32[]{:S(2)}) collective-permute-start(bf16[384,768]{1,0:T(8,128)(2,1)S(1)} %add_convert_fusion.4), channel_id=1, source_target_pairs={{0,8},{4,12},{8,0},{12,4},{16,24},{20,28},{24,16},{28,20},{1,9},{5... | collective-permute-start | bytes 1769480 | tf_op jit(solution)/shard_map/ppermute | solution.py:555
  79.6 10.2 %collective-permute-start.22 = (bf16[768,768]{1,0:T(8,128)(2,1)S(1)}, bf16[768,768]{1,0:T(8,128)(2,1)S(1)}, u32[]{:S(2)}, u32[]{:S(2)}) collective-permute-start(bf16[768,768]{1,0:T(8,128)(2,1)S(1)} %get-tuple-element.172), channel_id=1, source_target_pairs={{0,1},{1,0},{2,3},{3,2},{4,5},{5,4},{6,7},{7,6},{8,9},{9,8},{10,11... | collective-permute-start | bytes 3538952 | tf_op jit(solution)/shard_map/ppermute | solution.py:555
  79.7 10.3 %collective-permute-start.23 = (bf16[768,768]{1,0:T(8,128)(2,1)S(1)}, bf16[768,768]{1,0:T(8,128)(2,1)S(1)}, u32[]{:S(2)}, u32[]{:S(2)}) collective-permute-start(bf16[768,768]{1,0:T(8,128)(2,1)S(1)} %get-tuple-element.174), channel_id=1, source_target_pairs={{0,1},{1,0},{2,3},{3,2},{4,5},{5,4},{6,7},{7,6},{8,9},{9,8},{10,11... | collective-permute-start | bytes 3538952 | tf_op jit(solution)/shard_map/ppermute | solution.py:555
  90.2 15.4 %collective-permute-start.27 = (bf16[384,768]{1,0:T(8,128)(2,1)S(1)}, bf16[384,768]{1,0:T(8,128)(2,1)S(1)}, u32[]{:S(2)}, u32[]{:S(2)}) collective-permute-start(bf16[384,768]{1,0:T(8,128)(2,1)S(1)} %add_convert_fusion.3), channel_id=1, source_target_pairs={{0,4},{4,0},{8,12},{12,8},{16,20},{20,16},{24,28},{28,24},{1,5},{5... | collective-permute-start | bytes 1769480 | tf_op jit(solution)/shard_map/ppermute | solution.py:555
  91.1 15.0 %collective-permute-start.28 = (bf16[384,768]{1,0:T(8,128)(2,1)S(1)}, bf16[384,768]{1,0:T(8,128)(2,1)S(1)}, u32[]{:S(2)}, u32[]{:S(2)}) collective-permute-start(bf16[384,768]{1,0:T(8,128)(2,1)S(1)} %add_convert_fusion.2), channel_id=1, source_target_pairs={{0,8},{4,12},{8,0},{12,4},{16,24},{20,28},{24,16},{28,20},{1,9},{5... | collective-permute-start | bytes 1769480 | tf_op jit(solution)/shard_map/ppermute | solution.py:555
  97.9 8.5 %collective-permute-start.26 = (bf16[768,768]{1,0:T(8,128)(2,1)S(1)}, bf16[768,768]{1,0:T(8,128)(2,1)S(1)}, u32[]{:S(2)}, u32[]{:S(2)}) collective-permute-start(bf16[768,768]{1,0:T(8,128)(2,1)S(1)} %get-tuple-element.192), channel_id=1, source_target_pairs={{0,1},{1,0},{2,3},{3,2},{4,5},{5,4},{6,7},{7,6},{8,9},{9,8},{10,11... | collective-permute-start | bytes 3538952 | tf_op jit(solution)/shard_map/ppermute | solution.py:555
  106.6 11.1 %collective-permute-start.29 = (bf16[384,384]{1,0:T(8,128)(2,1)S(1)}, bf16[384,384]{1,0:T(8,128)(2,1)S(1)}, u32[]{:S(2)}, u32[]{:S(2)}) collective-permute-start(bf16[384,384]{1,0:T(8,128)(2,1)S(1)} %get-tuple-element.201), channel_id=1, source_target_pairs={{0,4},{4,0},{8,12},{12,8},{16,20},{20,16},{24,28},{28,24},{1,5},{5... | collective-permute-start | bytes 884744 | tf_op jit(solution)/shard_map/ppermute | solution.py:555
  107.8 9.8 %collective-permute-start.30 = (bf16[384,384]{1,0:T(8,128)(2,1)S(1)}, bf16[384,384]{1,0:T(8,128)(2,1)S(1)}, u32[]{:S(2)}, u32[]{:S(2)}) collective-permute-start(bf16[384,384]{1,0:T(8,128)(2,1)S(1)} %get-tuple-element.202), channel_id=1, source_target_pairs={{0,8},{4,12},{8,0},{12,4},{16,24},{20,28},{24,16},{28,20},{1,9},{5... | collective-permute-start | bytes 884744 | tf_op jit(solution)/shard_map/ppermute | solution.py:555
  108.6 16.7 %collective-permute-start.41 = (bf16[384,768]{1,0:T(8,128)(2,1)S(1)}, bf16[384,768]{1,0:T(8,128)(2,1)S(1)}, u32[]{:S(2)}, u32[]{:S(2)}) collective-permute-start(bf16[384,768]{1,0:T(8,128)(2,1)S(1)} %add_convert_fusion.1), channel_id=1, source_target_pairs={{0,2},{1,3},{2,0},{3,1},{4,6},{5,7},{6,4},{7,5},{8,10},{9,11},{10,... | collective-permute-start | bytes 1769480 | tf_op jit(solution)/shard_map/ppermute | solution.py:555
  110.1 24.7 %collective-permute-start.44 = (bf16[384,768]{1,0:T(8,128)(2,1)S(1)}, bf16[384,768]{1,0:T(8,128)(2,1)S(1)}, u32[]{:S(2)}, u32[]{:S(2)}) collective-permute-start(bf16[384,768]{1,0:T(8,128)(2,1)S(1)} %add_convert_fusion), channel_id=1, source_target_pairs={{0,2},{1,3},{2,0},{3,1},{4,6},{5,7},{6,4},{7,5},{8,10},{9,11},{10,... | collective-permute-start | bytes 1769480 | tf_op jit(solution)/shard_map/ppermute | solution.py:555
  117.6 21.4 %collective-permute-start.31 = (bf16[768,768]{1,0:T(8,128)(2,1)S(1)}, bf16[768,768]{1,0:T(8,128)(2,1)S(1)}, u32[]{:S(2)}, u32[]{:S(2)}) collective-permute-start(bf16[768,768]{1,0:T(8,128)(2,1)S(1)} %get-tuple-element.203), channel_id=1, source_target_pairs={{0,1},{1,0},{2,3},{3,2},{4,5},{5,4},{6,7},{7,6},{8,9},{9,8},{10,11... | collective-permute-start | bytes 3538952 | tf_op jit(solution)/shard_map/ppermute | solution.py:555
  125.5 10.8 %collective-permute-start.42 = (bf16[192,768]{1,0:T(8,128)(2,1)S(1)}, bf16[192,768]{1,0:T(8,128)(2,1)S(1)}, u32[]{:S(2)}, u32[]{:S(2)}) collective-permute-start(bf16[192,768]{1,0:T(8,128)(2,1)S(1)} %add_convert_fusion.7), channel_id=1, source_target_pairs={{0,8},{4,12},{8,0},{12,4},{16,24},{20,28},{24,16},{28,20},{1,9},{5... | collective-permute-start | bytes 884744 | tf_op jit(solution)/shard_map/ppermute | solution.py:555
  126.9 20.0 %collective-permute-start.35 = (bf16[192,384]{1,0:T(8,128)(2,1)S(1)}, bf16[192,384]{1,0:T(8,128)(2,1)S(1)}, u32[]{:S(2)}, u32[]{:S(2)}) collective-permute-start(bf16[192,384]{1,0:T(8,128)(2,1)S(1)} %get-tuple-element.249), channel_id=1, source_target_pairs={{0,4},{4,0},{8,12},{12,8},{16,20},{20,16},{24,28},{28,24},{1,5},{5... | collective-permute-start | bytes 442376 | tf_op jit(solution)/shard_map/ppermute | solution.py:555
  127.8 19.1 %collective-permute-start.34 = (bf16[192,384]{1,0:T(8,128)(2,1)S(1)}, bf16[192,384]{1,0:T(8,128)(2,1)S(1)}, u32[]{:S(2)}, u32[]{:S(2)}) collective-permute-start(bf16[192,384]{1,0:T(8,128)(2,1)S(1)} %get-tuple-element.250), channel_id=1, source_target_pairs={{0,8},{4,12},{8,0},{12,4},{16,24},{20,28},{24,16},{28,20},{1,9},{5... | collective-permute-start | bytes 442376 | tf_op jit(solution)/shard_map/ppermute | solution.py:555
  135.0 7.7 %collective-permute-start.45 = (bf16[192,768]{1,0:T(8,128)(2,1)S(1)}, bf16[192,768]{1,0:T(8,128)(2,1)S(1)}, u32[]{:S(2)}, u32[]{:S(2)}) collective-permute-start(bf16[192,768]{1,0:T(8,128)(2,1)S(1)} %add_convert_fusion.6), channel_id=1, source_target_pairs={{0,4},{4,0},{8,12},{12,8},{16,20},{20,16},{24,28},{28,24},{1,5},{5... | collective-permute-start | bytes 884744 | tf_op jit(solution)/shard_map/ppermute | solution.py:555
  136.4 9.5 %collective-permute-start.43 = (bf16[96,768]{1,0:T(8,128)(2,1)S(1)}, bf16[96,768]{1,0:T(8,128)(2,1)S(1)}, u32[]{:S(2)}, u32[]{:S(2)}) collective-permute-start(bf16[96,768]{1,0:T(8,128)(2,1)S(1)} %add_convert_fusion.13), channel_id=1, source_target_pairs={{0,16},{4,20},{8,24},{12,28},{16,0},{20,4},{24,8},{28,12},{1,17},{... | collective-permute-start | bytes 442376 | tf_op jit(solution)/shard_map/ppermute | solution.py:555
  139.2 10.2 %collective-permute-start.33 = (bf16[384,384]{1,0:T(8,128)(2,1)S(1)}, bf16[384,384]{1,0:T(8,128)(2,1)S(1)}, u32[]{:S(2)}, u32[]{:S(2)}) collective-permute-start(bf16[384,384]{1,0:T(8,128)(2,1)S(1)} %get-tuple-element.251), channel_id=1, source_target_pairs={{0,8},{4,12},{8,0},{12,4},{16,24},{20,28},{24,16},{28,20},{1,9},{5... | collective-permute-start | bytes 884744 | tf_op jit(solution)/shard_map/ppermute | solution.py:555
  142.7 6.7 %collective-permute-start.32 = (bf16[384,384]{1,0:T(8,128)(2,1)S(1)}, bf16[384,384]{1,0:T(8,128)(2,1)S(1)}, u32[]{:S(2)}, u32[]{:S(2)}) collective-permute-start(bf16[384,384]{1,0:T(8,128)(2,1)S(1)} %get-tuple-element.252), channel_id=1, source_target_pairs={{0,4},{4,0},{8,12},{12,8},{16,20},{20,16},{24,28},{28,24},{1,5},{5... | collective-permute-start | bytes 884744 | tf_op jit(solution)/shard_map/ppermute | solution.py:555
  145.9 16.6 %collective-permute-start.46 = (bf16[96,768]{1,0:T(8,128)(2,1)S(1)}, bf16[96,768]{1,0:T(8,128)(2,1)S(1)}, u32[]{:S(2)}, u32[]{:S(2)}) collective-permute-start(bf16[96,768]{1,0:T(8,128)(2,1)S(1)} %add_convert_fusion.12), channel_id=1, source_target_pairs={{0,16},{4,20},{8,24},{12,28},{16,0},{20,4},{24,8},{28,12},{1,17},{... | collective-permute-start | bytes 442376 | tf_op jit(solution)/shard_map/ppermute | solution.py:555
  149.6 11.0 %collective-permute-start.39 = (bf16[192,384]{1,0:T(8,128)(2,1)S(1)}, bf16[192,384]{1,0:T(8,128)(2,1)S(1)}, u32[]{:S(2)}, u32[]{:S(2)}) collective-permute-start(bf16[192,384]{1,0:T(8,128)(2,1)S(1)} %pad_maximum_fusion.2), channel_id=1, source_target_pairs={{0,16},{4,20},{8,24},{12,28},{16,0},{20,4},{24,8},{28,12},{1,17},{... | collective-permute-start | bytes 442376 | tf_op jit(solution)/shard_map/ppermute | solution.py:555
  152.2 10.1 %collective-permute-start.36 = (bf16[192,384]{1,0:T(8,128)(2,1)S(1)}, bf16[192,384]{1,0:T(8,128)(2,1)S(1)}, u32[]{:S(2)}, u32[]{:S(2)}) collective-permute-start(bf16[192,384]{1,0:T(8,128)(2,1)S(1)} %get-tuple-element.245), channel_id=1, source_target_pairs={{0,8},{4,12},{8,0},{12,4},{16,24},{20,28},{24,16},{28,20},{1,9},{5... | collective-permute-start | bytes 442376 | tf_op jit(solution)/shard_map/ppermute | solution.py:555
  153.5 8.8 %collective-permute-start.37 = (bf16[192,384]{1,0:T(8,128)(2,1)S(1)}, bf16[192,384]{1,0:T(8,128)(2,1)S(1)}, u32[]{:S(2)}, u32[]{:S(2)}) collective-permute-start(bf16[192,384]{1,0:T(8,128)(2,1)S(1)} %get-tuple-element.246), channel_id=1, source_target_pairs={{0,4},{4,0},{8,12},{12,8},{16,20},{20,16},{24,28},{28,24},{1,5},{5... | collective-permute-start | bytes 442376 | tf_op jit(solution)/shard_map/ppermute | solution.py:555
  160.7 5.2 %collective-permute-start.40 = (bf16[192,384]{1,0:T(8,128)(2,1)S(1)}, bf16[192,384]{1,0:T(8,128)(2,1)S(1)}, u32[]{:S(2)}, u32[]{:S(2)}) collective-permute-start(bf16[192,384]{1,0:T(8,128)(2,1)S(1)} %pad_maximum_fusion.3), channel_id=1, source_target_pairs={{0,2},{1,3},{2,0},{3,1},{4,6},{5,7},{6,4},{7,5},{8,10},{9,11},{10,... | collective-permute-start | bytes 442376 | tf_op jit(solution)/shard_map/ppermute | solution.py:555
  162.4 7.2 %collective-permute-start.38 = (bf16[192,384]{1,0:T(8,128)(2,1)S(1)}, bf16[192,384]{1,0:T(8,128)(2,1)S(1)}, u32[]{:S(2)}, u32[]{:S(2)}) collective-permute-start(bf16[192,384]{1,0:T(8,128)(2,1)S(1)} %pad_maximum_fusion.1), channel_id=1, source_target_pairs={{0,16},{4,20},{8,24},{12,28},{16,0},{20,4},{24,8},{28,12},{1,17},{... | collective-permute-start | bytes 442376 | tf_op jit(solution)/shard_map/ppermute | solution.py:555
  172.4 3.8 %collective-permute-start.48 = (f32[8,768]{1,0:T(8,128)S(1)}, f32[8,768]{1,0:T(8,128)S(1)}, u32[]{:S(2)}, u32[]{:S(2)}) collective-permute-start(f32[8,768]{1,0:T(8,128)S(1)} %add.353), channel_id=1, source_target_pairs={{0,2},{1,3},{2,0},{3,1},{4,6},{5,7},{6,4},{7,5},{8,10},{9,11},{10,... | collective-permute-start | bytes 73736 | tf_op jit(solution)/shard_map/ppermute | solution.py:555
  176.3 3.8 %collective-permute-start.49 = (f32[8,768]{1,0:T(8,128)S(1)}, f32[8,768]{1,0:T(8,128)S(1)}, u32[]{:S(2)}, u32[]{:S(2)}) collective-permute-start(f32[8,768]{1,0:T(8,128)S(1)} %add.354), channel_id=1, source_target_pairs={{0,4},{4,0},{8,12},{12,8},{16,20},{20,16},{24,28},{28,24},{1,5},{5... | collective-permute-start | bytes 73736 | tf_op jit(solution)/shard_map/ppermute | solution.py:555
  180.1 3.8 %collective-permute-start.50 = (f32[8,768]{1,0:T(8,128)S(1)}, f32[8,768]{1,0:T(8,128)S(1)}, u32[]{:S(2)}, u32[]{:S(2)}) collective-permute-start(f32[8,768]{1,0:T(8,128)S(1)} %add.355), channel_id=1, source_target_pairs={{0,8},{4,12},{8,0},{12,4},{16,24},{20,28},{24,16},{28,20},{1,9},{5... | collective-permute-start | bytes 73736 | tf_op jit(solution)/shard_map/ppermute | solution.py:555
  183.9 4.7 %collective-permute-start.51 = (f32[8,768]{1,0:T(8,128)S(1)}, f32[8,768]{1,0:T(8,128)S(1)}, u32[]{:S(2)}, u32[]{:S(2)}) collective-permute-start(f32[8,768]{1,0:T(8,128)S(1)} %add.356), channel_id=1, source_target_pairs={{0,16},{4,20},{8,24},{12,28},{16,0},{20,4},{24,8},{28,12},{1,17},{... | collective-permute-start | bytes 73736 | tf_op jit(solution)/shard_map/ppermute | solution.py:555
  (51 other events, 360.2 us)
where the time goes:
time: 190 us
  Pallas kernels  77.1 us (41%)
  waiting for transfers between devices  55.1 us (29%)
  starting transfers between devices  46.1 us (24%)
  other arithmetic  7.24 us (4%)
  local copies, waits for them, and re-layouts  2.73 us (1%)
    ppermute x52, waiting for transfers between devices, swap(): return lax.ppermute(value, axis, [(i, i ^ bit) for i in range(size)])  55.1 us
    ppermute x52, starting transfers between devices, swap(): return lax.ppermute(value, axis, [(i, i ^ bit) for i in range(size)])  46.1 us
    pallas_call x4, Pallas kernels, back_call(): pl.pallas_call(kernel, grid=(r // PATCHES,), out_shape=tuple(outs) + (jax...  25.8 us
    pallas_call x2, Pallas kernels, run_ffn_near(): pl.pallas_call(ffn_near_kernel, grid=(TILES,), out_shape=(jax.ShapeDtypeS...  13.7 us
    pallas_call x1, Pallas kernels, run_ffn_last(): pl.pallas_call(lambda *refs: ffn_last_kernel(*refs, count=count), grid=(T...  9.63 us
    pallas_call x1, Pallas kernels, run_attn_two(): pl.pallas_call(lambda *refs: attn_two_kernel(*refs, count=count), grid=(r...  7.45 us
    pallas_call x1, Pallas kernels, run_attn_one(): pl.pallas_call(attn_one_kernel, grid=(r // PATCHES,), out_shape=(jax.Shap...  7.28 us
    pallas_call x1, Pallas kernels, run_ffn_far(): pl.pallas_call(ffn_far_kernel, grid=(TILES,), out_shape=(jax.ShapeDtypeSt...  6.95 us
  transfers between devices with their start and end apart: 52, of which 21 were waited for; matrix products, arithmetic and copies ran while one was open for 4% of the time, Pallas kernels for 39%

commit v1 on v0

--- a/solution.py
+++ b/solution.py
@@ -103,28 +103,26 @@
 SMEM = pl.BlockSpec(memory_space=pltpu.SMEM)
 
 
-def start_kernel(pos_ref, pos2_ref, rows_ref, vec_ref, x_ref, xt_ref, xt2_ref, *, count):
+def start_kernel(pos_ref, rows_ref, vec_ref, x_ref, xt_ref, *, count):
     width, rows = rows_ref.shape[1], rows_ref.shape[0]
     for start in range(0, rows, PATCHES):
         normed, _ = layer_stats(rows_ref[start : start + PATCHES].astype(F32))
         low = (normed * vec_ref[0:1] + vec_ref[1:2]).astype(BF16)
         x_ref[start : start + PATCHES] = low
         put_turned(xt_ref, low, pos_ref, count, start)
-        put_turned(xt2_ref, low, pos2_ref, count, start)
-
-
-def run_start(pos, pos2, rows, vectors, count):
+
+
+def run_start(pos, rows, vectors, count):
     r, d = rows.shape
     return pl.pallas_call(
         lambda *refs: start_kernel(*refs, count=count),
         out_shape=(
             jax.ShapeDtypeStruct((r, d), BF16),
             jax.ShapeDtypeStruct(turned_shape(d, r, count), BF16),
-            jax.ShapeDtypeStruct(turned_shape(d, r, count), BF16),
         ),
-        in_specs=[SMEM, SMEM, pl.BlockSpec(memory_space=pltpu.VMEM), pl.BlockSpec(memory_space=pltpu.VMEM)],
-        compiler_params=params(BIG),
-    )(pos, pos2, rows, vectors)
+        in_specs=[SMEM, pl.BlockSpec(memory_space=pltpu.VMEM), pl.BlockSpec(memory_space=pltpu.VMEM)],
+        compiler_params=params(BIG),
+    )(pos, rows, vectors)
 
 
 def gout_kernel(pos_ref, weight_ref, cot_ref, g_ref, gt_ref, *, count):
@@ -159,11 +157,11 @@
         q = qkv[:, at : at + HEAD_DIM] * SCALE
         k = qkv[:, cols + at : cols + at + HEAD_DIM]
         v = qkv[:, 2 * cols + at : 2 * cols + at + HEAD_DIM]
-        scores = mm_nt(q, k)
-        expo = jnp.exp(scores - jnp.max(scores, axis=-1, keepdims=True))
-        probs = (expo * (1.0 / jnp.sum(expo, axis=-1, keepdims=True))).astype(BF16)
+        scores = mm_nt(k, q)
+        expo = jnp.exp(scores - jnp.max(scores, axis=0, keepdims=True))
+        probs = (expo * (1.0 / jnp.sum(expo, axis=0, keepdims=True))).astype(BF16)
         probs_ref[h] = probs
-        mixed.append(mm(probs, v).astype(BF16))
+        mixed.append(mm_tn(probs, v).astype(BF16))
     mixed = jnp.concatenate(mixed, axis=1)
     saved_ref[:, 3 * cols :] = mixed
     return mm(mixed, w_ref[3 * cols :])
@@ -228,7 +226,7 @@
 
 
 def cost(micros):
-    return pl.CostEstimate(flops=int(micros * 10 * 1e9), bytes_accessed=int(micros * 10 * 3e6), transcendentals=0)
+    return pl.CostEstimate(flops=int(micros * 5 * 1e9), bytes_accessed=int(micros * 5 * 3e6), transcendentals=0)
 
 
 def run_attn_one(x, rows, vectors, wa, wb):
@@ -431,41 +429,40 @@
         v = saved_ref[:, 2 * cols + at : 2 * cols + at + HEAD_DIM]
         do = dmix[:, at : at + HEAD_DIM]
         probs = probs_ref[h]
-        dv.append(mm_tn(probs, do).astype(BF16))
-        dp = mm_nt(do, v)
+        dv.append(mm(probs, do).astype(BF16))
+        dp = mm_nt(v, do)
         wide = probs.astype(F32)
-        ds = (SCALE * wide * (dp - jnp.sum(wide * dp, axis=-1, keepdims=True))).astype(BF16)
-        dq.append(mm(ds, k).astype(BF16))
-        dk.append(mm_tn(ds, q).astype(BF16))
+        ds = (SCALE * wide * (dp - jnp.sum(wide * dp, axis=0, keepdims=True))).astype(BF16)
+        dq.append(mm_tn(ds, k).astype(BF16))
+        dk.append(mm(ds, q).astype(BF16))
     dqkv = jnp.concatenate(dq + dk + dv, axis=1)
     keep_ref[pl.ds(start, PATCHES), : 3 * cols] = dqkv
     keep_ref[pl.ds(start, PATCHES), 3 * cols :] = saved_ref[:, 3 * cols :]
     return mm(dqkv, w_ref[: 3 * cols])
 
 
-def attn_grad(xt_ref, xt2_ref, gft_ref, keep_ref, g_ref):
+def attn_grad(xt_ref, gft_ref, keep_ref, g_ref):
     cols = keep_ref.shape[1] // 4
-    g_ref[:, : 2 * cols] = mm(xt_ref[...], keep_ref[:, : 2 * cols]).astype(BF16)
-    g_ref[:, 2 * cols : 3 * cols] = mm(xt2_ref[...], keep_ref[:, 2 * cols : 3 * cols]).astype(BF16)
+    g_ref[:, : 3 * cols] = mm(xt_ref[...], keep_ref[:, : 3 * cols]).astype(BF16)
     g_ref[:, 3 * cols :] = mm(gft_ref[...], keep_ref[:, 3 * cols :]).astype(BF16)
 
 
-def back_body(gf_ref, xt_ref, xt2_ref, gft_ref, w_ref, saved_ref, probs_ref, g_ref, keep_ref):
+def back_body(gf_ref, xt_ref, gft_ref, w_ref, saved_ref, probs_ref, g_ref, keep_ref):
     term = attend_back_shard(gf_ref[...], w_ref, saved_ref, probs_ref, keep_ref)
 
     @pl.when(pl.program_id(0) == pl.num_programs(0) - 1)
     def _():
-        attn_grad(xt_ref, xt2_ref, gft_ref, keep_ref, g_ref)
+        attn_grad(xt_ref, gft_ref, keep_ref, g_ref)
 
     return term
 
 
 def back_far_kernel(
-    low_ref, gf_ref, xt_ref, xt2_ref, gft_ref, saved_ref, probs_ref, h_ref, i_ref, *rest
+    low_ref, gf_ref, xt_ref, gft_ref, saved_ref, probs_ref, h_ref, i_ref, *rest
 ):
     *before, acc_ref, g_ref, keep_ref, w_ref = rest
     join_pair(low_ref, ((h_ref, i_ref),), (w_ref,))
-    term = back_body(gf_ref, xt_ref, xt2_ref, gft_ref, w_ref, saved_ref, probs_ref, g_ref, keep_ref)
+    term = back_body(gf_ref, xt_ref, gft_ref, w_ref, saved_ref, probs_ref, g_ref, keep_ref)
     if before:
         acc_ref[...] = term + before[0][...]
     else:
@@ -474,17 +471,17 @@
 
 
 def back_near_kernel(
-    gf_ref, xt_ref, xt2_ref, gft_ref, saved_ref, probs_ref, w_ref, before_ref, acc_ref, g_ref, keep_ref
+    gf_ref, xt_ref, gft_ref, saved_ref, probs_ref, w_ref, before_ref, acc_ref, g_ref, keep_ref
 ):
-    term = back_body(gf_ref, xt_ref, xt2_ref, gft_ref, w_ref, saved_ref, probs_ref, g_ref, keep_ref)
+    term = back_body(gf_ref, xt_ref, gft_ref, w_ref, saved_ref, probs_ref, g_ref, keep_ref)
     acc_ref[...] = term + before_ref[...]
 
 
 def back_last_kernel(
-    gf_ref, xt_ref, xt2_ref, gft_ref, saved_ref, probs_ref, w_ref, before_ref, rows_ref, gfirst_ref, vec_ref,
+    gf_ref, xt_ref, gft_ref, saved_ref, probs_ref, w_ref, before_ref, rows_ref, gfirst_ref, vec_ref,
     ig_ref, sums_ref, g_ref, keep_ref,
 ):
-    term = back_body(gf_ref, xt_ref, xt2_ref, gft_ref, w_ref, saved_ref, probs_ref, g_ref, keep_ref)
+    term = back_body(gf_ref, xt_ref, gft_ref, w_ref, saved_ref, probs_ref, g_ref, keep_ref)
     grad_in = before_ref[...] + term
     normed, inverse = layer_stats(rows_ref[...].astype(F32))
     ig_ref[...] = gfirst_ref[...] + norm_back(grad_in * vec_ref[0:1], normed, inverse)
@@ -511,7 +508,7 @@
         kernel,
         grid=(r // PATCHES,),
         out_shape=tuple(outs) + (jax.ShapeDtypeStruct((d, d), BF16),),
-        in_specs=([SMEM] if far else []) + [image_block(d)] + [full((d, r))] * 3 + saved_specs + specs,
+        in_specs=([SMEM] if far else []) + [image_block(d)] + [full((d, r))] * 2 + saved_specs + specs,
         out_specs=out_specs + [full((d, d))],
         scratch_shapes=[keep, whole] if far else [keep],
         compiler_params=params(BIG),
@@ -519,31 +516,31 @@
     )(*ops)
 
 
-def run_back_far(low, gfl, xt, xt2, gft, halves, saved, *acc):
+def run_back_far(low, gfl, xt, gft, halves, saved, *acc):
     r, d = gfl.shape
     return back_call(
         back_far_kernel,
-        [low, gfl, xt, xt2, gft, *saved, *halves, *acc],
+        [low, gfl, xt, gft, *saved, *halves, *acc],
         [full((d // 2, d))] * 2 + [image_block(d)] * len(acc),
         [jax.ShapeDtypeStruct((r, d), F32)], [image_block(d)], True,
     )
 
 
-def run_back_near(gfl, xt, xt2, gft, weight, saved, acc):
+def run_back_near(gfl, xt, gft, weight, saved, acc):
     r, d = gfl.shape
     return back_call(
         back_near_kernel,
-        [gfl, xt, xt2, gft, *saved, weight, acc],
+        [gfl, xt, gft, *saved, weight, acc],
         [full((d, d)), image_block(d)],
         [jax.ShapeDtypeStruct((r, d), F32)], [image_block(d)], False,
     )
 
 
-def run_back_last(gfl, xt, xt2, gft, weight, saved, acc, rows, gfirst, vectors):
+def run_back_last(gfl, xt, gft, weight, saved, acc, rows, gfirst, vectors):
     r, d = gfl.shape
     return back_call(
         back_last_kernel,
-        [gfl, xt, xt2, gft, *saved, weight, acc, rows, gfirst, vectors],
+        [gfl, xt, gft, *saved, weight, acc, rows, gfirst, vectors],
         [full((d, d))] + [image_block(d)] * 3 + [full(vectors.shape)],
         [jax.ShapeDtypeStruct((r, d), F32), jax.ShapeDtypeStruct((8, d), F32)],
         [image_block(d), full((8, d))], False,
@@ -656,13 +653,13 @@
 
 
 def attn_step_kernel(
-    left_ref, right_ref, qm_ref, qf_ref, qs_ref, om_ref, of_ref, os_ref, sums_a_ref, sums_b_ref, squares_ref,
+    sum_ref, qm_ref, qf_ref, qs_ref, om_ref, of_ref, os_ref, sums_a_ref, sums_b_ref, squares_ref,
     qg_ref, qf_out, qs_out, qu_ref, og_ref, of_out, os_out, ou_ref, small_ref,
 ):
     cols = qm_ref.shape[2]
-    left, right = left_ref[...], right_ref[...]
+    whole = sum_ref[...]
     master_square, update_square = 0.0, 0.0
-    for index, grad in enumerate((left[:, :cols], left[:, cols:], right[:, :cols])):
+    for index, grad in enumerate(whole[:, at * cols : (at + 1) * cols] for at in range(3)):
         master = qm_ref[index]
         first_new, second_new, update = lamb_step(grad, master, qf_ref[index], qs_ref[index])
         qg_ref[index] = grad
@@ -671,7 +668,7 @@
         qu_ref[index] = update
         master_square += whole_sum(master * master)
         update_square += whole_sum(update * update)
-    grad = right[:, cols:].T
+    grad = whole[:, 3 * cols :].T
     master = om_ref[...]
     first_new, second_new, update = lamb_step(grad, master, of_ref[...], os_ref[...])
     og_ref[...] = grad
@@ -689,13 +686,13 @@
     )
 
 
-def run_attn_step(left, right, qkv, out, sums_a, sums_b, squares):
+def run_attn_step(whole, qkv, out, sums_a, sums_b, squares):
     q, o = jax.ShapeDtypeStruct(qkv[0].shape, F32), jax.ShapeDtypeStruct(out[0].shape, F32)
     return pl.pallas_call(
         attn_step_kernel,
         out_shape=(q,) * 4 + (o,) * 4 + (jax.ShapeDtypeStruct(sums_a.shape, F32),),
         compiler_params=params(BIG),
-    )(left, right, *qkv, *out, sums_a, sums_b, squares)
+    )(whole, *qkv, *out, sums_a, sums_b, squares)
 
 
 def final_kernel(*refs):
@@ -798,8 +795,8 @@
     near = [swap(weight, "mp", 1) for weight in (attn_w, in_weight, down_weight)]
     counts, attn_one, in_one, down_one = lax.optimization_barrier((counts, *near))
     counts = counts + swap(counts, "dp", 1)
-    x, xt, xt2 = run_start(pos, pos2, rows, vectors, count)
-    xt, xt2 = turned_order(xt, pos, count), turned_order(xt2, pos2, count)
+    x, xt = run_start(pos, rows, vectors, count)
+    xt = turned_order(xt, pos, count)
     acc, s1, p1, s0, p0 = run_attn_one(x, rows, vectors, attn_one, attn_w)
     attn_far, counts, acc = lax.optimization_barrier((attn_far, counts, acc))
     attn_two = (attn_far, swap(attn_far, "dp", 1))
@@ -832,53 +829,46 @@
     )
     y, dm, gi3, gd3 = run_ffn_far(low, mid, midt, gout, goutt, in_three, down_three, y, dm)
     out_rows, gfirst, gfl, gft, sums_b, gi2, gd2 = run_ffn_last(
-        pos2, low, image_weight, mid, midt, gout, goutt, in_two, down_two,
+        pos, low, image_weight, mid, midt, gout, goutt, in_two, down_two,
         y, dm, first, cotangent, vectors, count,
     )
-    gft = turned_order(gft, pos2, count)
+    gft = turned_order(gft, pos, count)
     in_far, down_far = meet(gi2, gi3), meet(gd2, gd3)
     gfl, in_sent, down_sent, _, _ = lax.optimization_barrier(
         (gfl, upper(in_far), upper(down_far), in_near[-1], down_near[-1])
     )
     in_far, down_far = fold(in_far, order1[0], in_sent), fold(down_far, order2[0], down_sent)
-    gin, ga3 = run_back_far(low, gfl, xt, xt2, gft, attn_three, (s3, p3))
-    gin, ga2 = run_back_far(low, gfl, xt, xt2, gft, attn_two, (s2, p2), gin)
-    both = meet(ga2, ga3)
-    left_far, right_far = columns(both, slice(0, half)), columns(both, slice(half, None))
-    gin, left_sent, right_sent, in_sent, down_sent = lax.optimization_barrier(
-        (gin, upper(left_far), upper(right_far), total(in_far).astype(BF16), total(down_far).astype(BF16))
-    )
-    left_far, right_far = fold(left_far, order1[0], left_sent), fold(right_far, order2[0], right_sent)
+    gin, ga3 = run_back_far(low, gfl, xt, gft, attn_three, (s3, p3))
+    gin, ga2 = run_back_far(low, gfl, xt, gft, attn_two, (s2, p2), gin)
+    far = meet(ga2, ga3)
+    gin, far_sent, in_sent, down_sent = lax.optimization_barrier(
+        (gin, upper(far), total(in_far).astype(BF16), total(down_far).astype(BF16))
+    )
+    far = fold(far, order1[0], far_sent)
     in_grad, down_grad = join(in_near, None, in_sent), join(down_near, None, down_sent)
-    gin, ga1 = run_back_near(gfl, xt, xt2, gft, attn_one, (s1, p1), gin)
-    ga1, *_ = lax.optimization_barrier((ga1, left_far[-1], right_far[-1]))
+    gin, ga1 = run_back_near(gfl, xt, gft, attn_one, (s1, p1), gin)
     input_grad, sums_a, ga0 = run_back_last(
-        gfl, xt, xt2, gft, attn_w, (s0, p0), gin, rows, gfirst, vectors
-    )
-    both = meet(ga0, ga1)
-    left_near, right_near = columns(both, slice(0, half)), columns(both, slice(half, None))
-    left_far, right_far = fold(left_far, order1[1]), fold(right_far, order2[1])
-    left_near, right_near = fold(left_near, order1[0]), fold(right_near, order2[0])
-    near_back, far_back = lax.optimization_barrier(
-        ((left_near[-1], right_near[-1]), (left_far[-1], right_far[-1]))
-    )
-    left_near, right_near = left_near[:-1] + near_back[:1], right_near[:-1] + near_back[1:]
-    left_far, right_far = left_far[:-1] + far_back[:1], right_far[:-1] + far_back[1:]
-    left_near, right_near = fold(left_near, order1[1]), fold(right_near, order2[1])
-    in_grad, down_grad = fold(in_grad, order1[1]), fold(down_grad, order2[1])
+        gfl, xt, gft, attn_w, (s0, p0), gin, rows, gfirst, vectors
+    )
+    near = meet(ga0, ga1)
+    near = fold(near, order1[0])
+    far = fold(far, order1[1])
+    in_grad = fold(in_grad, order1[1])
+    near = fold(near, order1[1])
+    down_grad = fold(down_grad, order2[1])
+    near = near + (swap(total(far).astype(BF16), "mp", 2),)
     for bit in order1[2:]:
         in_grad, down_grad = fold(in_grad, bit), fold(down_grad, bit)
-        left_far, right_far = fold_two(left_far, right_far, bit)
-        left_near, right_near = fold_two(left_near, right_near, bit)
-    left, right = join_two(left_near, left_far, right_near, right_far)
-    in_grad, down_grad, left, right = (total(terms) for terms in (in_grad, down_grad, left, right))
+        near = fold(near, bit)
+    both = total(near)
+    in_grad, down_grad = total(in_grad), total(down_grad)
 
     down_state = (down_master.T, down_first.T, down_second.T)
     in_fn, in_sn, in_up, down_fn, down_sn, down_up, squares = run_dense_step(
         (in_grad, in_master, in_first, in_second), (down_grad,) + down_state
     )
     qkv_grad, qkv_fn, qkv_sn, qkv_up, out_grad, out_fn, out_sn, out_up, small = run_attn_step(
-        left, right, (qkv_master, qkv_first, qkv_second), (out_master, out_first, out_second),
+        both, (qkv_master, qkv_first, qkv_second), (out_master, out_first, out_second),
         sums_a, sums_b, squares,
     )
     new, vec_outs = run_final(

time: 190 us -> 183 us (0.963)
  waiting for transfers between devices: 55.1 us -> 51.3 us
  Pallas kernels: 77.1 us -> 74 us
    ppermute x52 -> x47, waiting for transfers between devices: 55.1 us -> 51.3 us  [swap(): return lax.ppermute(value, axis, [(i, i ^ bit) for i in range(size)])]
    ppermute x52 -> x47, starting transfers between devices: 46.1 us -> 45.5 us  [swap(): return lax.ppermute(value, axis, [(i, i ^ bit) for i in range(size)])]
  transfers between devices with their start and end apart: 52 -> 47, of which waited for: 21 -> 20; matrix products, arithmetic and copies ran while one was open for 4% -> 4% of each run, Pallas kernels for 39% -> 39%
where the time goes in v1:
time: 183 us; the launch traced here: 182 us
  Pallas kernels  74 us (40%)
  waiting for transfers between devices  51.3 us (28%)
  starting transfers between devices  45.5 us (25%)
  other arithmetic  7.12 us (4%)
  local copies, waits for them, and re-layouts  3.04 us (2%)
    ppermute x47, waiting for transfers between devices, swap(): return lax.ppermute(value, axis, [(i, i ^ bit) for i in range(size)])  51.3 us
    ppermute x47, starting transfers between devices, swap(): return lax.ppermute(value, axis, [(i, i ^ bit) for i in range(size)])  45.5 us
    pallas_call x4, Pallas kernels, back_call(): pl.pallas_call(kernel, grid=(r // PATCHES,), out_shape=tuple(outs) + (jax...  24.6 us
    pallas_call x2, Pallas kernels, run_ffn_near(): pl.pallas_call(ffn_near_kernel, grid=(TILES,), out_shape=(jax.ShapeDtypeS...  13.9 us
    pallas_call x1, Pallas kernels, run_ffn_last(): pl.pallas_call(lambda *refs: ffn_last_kernel(*refs, count=count), grid=(T...  9.3 us
    pallas_call x1, Pallas kernels, run_attn_two(): pl.pallas_call(lambda *refs: attn_two_kernel(*refs, count=count), grid=(r...  6.87 us
    pallas_call x1, Pallas kernels, run_attn_one(): pl.pallas_call(attn_one_kernel, grid=(r // PATCHES,), out_shape=(jax.Shap...  6.82 us
    pallas_call x1, Pallas kernels, run_ffn_far(): pl.pallas_call(ffn_far_kernel, grid=(TILES,), out_shape=(jax.ShapeDtypeSt...  6.23 us
  transfers between devices with their start and end apart: 47, of which 20 were waited for; matrix products, arithmetic and copies ran while one was open for 4% of the time, Pallas kernels for 39%

profile of v1, /device:TPU:0, one launch (start us, length us, event | category | flops | bytes accessed | tf_op | source)
XLA Modules:
  0.0 182.4 jit_solution(8713993145181814348)
XLA Ops:
  0.7 1.4 pad_maximum_fusion.wb_ref.w_ref
  3.3 1.5 fusion
  4.8 2.7 %collective-permute-start.1 = (f32[8]{0:T(128)S(1)}, f32[8]{0:T(128)S(1)}, u32[]{:S(2)}, u32[]{:S(2)}) collective-permute-start(f32[8]{0:T(128)S(1)} %convert_reduce_fusion), channel_id=1, source_target_pairs={{0,2},{1,3},{2,0},{3,1},{4,6},{5,7},{6,4},{7,5},{8,10},{9,11},{10,... | collective-permute-start | bytes 104 | tf_op jit(solution)/shard_map/ppermute | solution.py:552
  10.0 2.0 %collective-permute-start.10 = (bf16[384,768]{1,0:T(8,128)(2,1)S(1)}, bf16[384,768]{1,0:T(8,128)(2,1)S(1)}, u32[]{:S(2)}, u32[]{:S(2)}) collective-permute-start(bf16[384,768]{1,0:T(8,128)(2,1)S(1)} %constant_dynamic-slice_fusion.1), channel_id=1, source_target_pairs={{0,2},{1,3},{2,0},{3,1},{4,6},{5,7},{6,4},{7,5},{8,10},{9,11},{10,... | collective-permute-start | bytes 1769480 | tf_op jit(solution)/shard_map/ppermute | solution.py:552
  12.0 1.5 collective-permute-start.5
  13.5 6.8 %shard_map.390 = (f32[512,768]{1,0:T(8,128)S(1)}, bf16[512,768]{1,0:T(8,128)(2,1)S(1)}, bf16[6,256,256]{2,1,0:T(8,128)(2,1)S(1)}, bf16[512,768]{1,0:T(8,128)(2,1)S(1)}, bf16[6,256,256]{2,1,0:T(8,128)(2,1)S(1)}) custom-call(bf16[512,768]{1,0:T(8,128)(2,1)S(1)} %get-tuple-element.127.x_ref.refs_2_, bf16[512,768]{1,0:T(8,128)(2,1)S(1)} %copy-done.10, ...), custom_call_target="tpu_custom_call" | custom-call | flops 35000000512 | bytes 105000000 | tf_op jit(solution)/shard_map/pallas_call | solution.py:236
  20.3 3.3 %collective-permute-done.refs_7_.h_ref = bf16[384,768]{1,0:T(8,128)(2,1)S(1)} collective-permute-done((bf16[384,768]{1,0:T(8,128)(2,1)S(1)}, bf16[384,768]{1,0:T(8,128)(2,1)S(1)}, u32[]{:S(2)}, u32[]{:S(2)}) %collective-permute-start) | collective-permute-done | bytes 589856 | tf_op jit(solution)/shard_map/ppermute | solution.py:552
  23.6 1.4 collective-permute-start.9
  25.5 1.5 collective-permute-done.6
  27.0 1.6 collective-permute-start.7
  28.6 2.0 %collective-permute-done.7 = f32[8]{0:T(128)S(1)} collective-permute-done((f32[8]{0:T(128)S(1)}, f32[8]{0:T(128)S(1)}, u32[]{:S(2)}, u32[]{:S(2)}) %collective-permute-start.7) | collective-permute-done | bytes 64 | tf_op jit(solution)/shard_map/ppermute | solution.py:552
  30.6 2.6 %collective-permute-start.8 = (f32[8]{0:T(128)S(1)}, f32[8]{0:T(128)S(1)}, u32[]{:S(2)}, u32[]{:S(2)}) collective-permute-start(f32[8]{0:T(128)S(1)} %add.203), channel_id=1, source_target_pairs={{0,16},{4,20},{8,24},{12,28},{16,0},{20,4},{24,8},{28,12},{1,17},{... | collective-permute-start | bytes 104 | tf_op jit(solution)/shard_map/ppermute | solution.py:552
  33.2 1.9 %collective-permute-done.8 = f32[8]{0:T(128)S(1)} collective-permute-done((f32[8]{0:T(128)S(1)}, f32[8]{0:T(128)S(1)}, u32[]{:S(2)}, u32[]{:S(2)}) %collective-permute-start.8) | collective-permute-done | bytes 64 | tf_op jit(solution)/shard_map/ppermute | solution.py:552
  38.3 1.2 collective-permute-start.13
  39.5 6.9 %shard_map.392 = (f32[512,768]{1,0:T(8,128)S(1)}, bf16[512,768]{1,0:T(8,128)(2,1)S(1)}, bf16[8,96,512]{2,1,0:T(8,128)(2,1)S(1)}, bf16[512,768]{1,0:T(8,128)(2,1)...) custom-call(s32[8]{0:T(128)S(1)} %get-tuple-element.226.refs_0_, ...), custom_call_target="tpu_custom_call" | custom-call | flops 35000000512 | bytes 105000000 | tf_op jit(solution)/shard_map/pallas_call | solution.py:255
  46.4 7.0 %shard_map.393 = (f32[512,768]{1,0:T(8,128)S(1)}, f32[512,768]{1,0:T(8,128)S(1)}, bf16[768,768]{1,0:T(8,128)(2,1)S(1)}, bf16[768,768]{1,0:T(8,128)(2,1)S(1)}) custom-call(bf16[512,768]{1,0:T(8,128)(2,1)S(1)} %get-tuple-element.137.mid_ref.refs_3_, bf16[768,512]{1,0:T(8,128)(2,1)S(1)} %bitcast.33, bf16[512,768]{1,0:T(8,128)(2,1)S(1)} %get-tuple-element.139.g_ref.refs_5_, ...), custom_call_target="tpu_custom_call" | custom-call | flops 30000001024 | bytes 90000000 | tf_op jit(solution)/shard_map/pallas_call | solution.py:367
  53.8 1.2 collective-permute-start.15
  55.6 6.9 %shard_map.394 = (f32[512,768]{1,0:T(8,128)S(1)}, f32[512,768]{1,0:T(8,128)S(1)}, bf16[768,768]{1,0:T(8,128)(2,1)S(1)}, bf16[768,768]{1,0:T(8,128)(2,1)S(1)}) custom-call(bf16[512,768]{1,0:T(8,128)(2,1)S(1)} %get-tuple-element.137.mid_ref.refs_3_, bf16[768,512]{1,0:T(8,128)(2,1)S(1)} %bitcast.34, bf16[512,768]{1,0:T(8,128)(2,1)S(1)} %get-tuple-element.139.g_ref.refs_5_, ...), custom_call_target="tpu_custom_call" | custom-call | flops 30000001024 | bytes 90000000 | tf_op jit(solution)/shard_map/pallas_call | solution.py:367
  64.3 5.3 %collective-permute-done.15.refs_10_ = bf16[768,384]{1,0:T(8,128)(2,1)S(1)} collective-permute-done((bf16[768,384]{1,0:T(8,128)(2,1)S(1)}, bf16[768,384]{1,0:T(8,128)(2,1)S(1)}, u32[]{:S(2)}, u32[]{:S(2)}) %collective-permute-start.15) | collective-permute-done | bytes 589856 | tf_op jit(solution)/shard_map/ppermute | solution.py:552
  69.6 1.2 collective-permute-start.24
  70.8 1.6 collective-permute-start.25
  72.4 6.2 %shard_map.395 = (f32[512,768]{1,0:T(8,128)S(1)}, f32[512,768]{1,0:T(8,128)S(1)}, bf16[768,768]{1,0:T(8,128)(2,1)S(1)}, bf16[768,768]{1,0:T(8,128)(2,1)S(1)}) custom-call(s32[1]{0:T(128)} %bitcast.refs_1_.low_ref, bf16[512,768]{1,0:T(8,128)(2,1)S(1)} %get-tuple-element.137.mid_ref.refs_3_, bf16[768,512]{1,0:T(8,128)(2,1)S(1)} %bitcast.35, ...), custom_call_target="tpu_custom_call" | custom-call | flops 30000001024 | bytes 90000000 | tf_op jit(solution)/shard_map/pallas_call | solution.py:382
  79.2 9.3 %shard_map.396 = (bf16[512,768]{1,0:T(8,128)(2,1)}, f32[512,768]{1,0:T(8,128)S(1)}, bf16[512,768]{1,0:T(8,128)(2,1)S(1)}, bf16[8,96,512]{2,1,0:T(8,128)(2,1)S(1)...) custom-call(s32[8]{0:T(128)S(1)} %get-tuple-element.226.refs_0_, ...), custom_call_target="tpu_custom_call" | custom-call | flops 40000000000 | bytes 120000000 | tf_op jit(solution)/shard_map/pallas_call | solution.py:398
  90.7 5.3 %shard_map.397 = (f32[512,768]{1,0:T(8,128)S(1)}, bf16[768,768]{1,0:T(8,128)(2,1)S(1)}) custom-call(s32[1]{0:T(128)} %bitcast.refs_1_.low_ref, bf16[512,768]{1,0:T(8,128)(2,1)S(1)} %get-tuple-element.170.gf_ref, bf16[768,512]{1,0:T(8,128)(2,1)S(1)} %bitcast.25, bf16[768,512]{1,0:T(8,128)(2,1)S(1)} %bitcast.37, ...), custom_call_target="tpu_custom_call" | custom-call | flops 30000001024 | bytes 90000000 | tf_op jit(solution)/shard_map/pallas_call | solution.py:507
  96.1 5.4 %shard_map.398 = (f32[512,768]{1,0:T(8,128)S(1)}, bf16[768,768]{1,0:T(8,128)(2,1)S(1)}) custom-call(s32[1]{0:T(128)} %bitcast.refs_1_.low_ref, bf16[512,768]{1,0:T(8,128)(2,1)S(1)} %get-tuple-element.170.gf_ref, bf16[768,512]{1,0:T(8,128)(2,1)S(1)} %bitcast.26, bf16[768,512]{1,0:T(8,128)(2,1)S(1)} %bitcast.38, ...), custom_call_target="tpu_custom_call" | custom-call | flops 30000001024 | bytes 90000000 | tf_op jit(solution)/shard_map/pallas_call | solution.py:507
  101.5 2.7 %collective-permute-done.27 = bf16[384,768]{1,0:T(8,128)(2,1)S(1)} collective-permute-done((bf16[384,768]{1,0:T(8,128)(2,1)S(1)}, bf16[384,768]{1,0:T(8,128)(2,1)S(1)}, u32[]{:S(2)}, u32[]{:S(2)}) %collective-permute-start.27) | collective-permute-done | bytes 589856 | tf_op jit(solution)/shard_map/ppermute | solution.py:552
  105.0 1.4 collective-permute-start.32
  106.4 1.5 collective-permute-start.36
  108.4 6.6 %shard_map.399 = (f32[512,768]{1,0:T(8,128)S(1)}, bf16[768,768]{1,0:T(8,128)(2,1)S(1)}) custom-call(bf16[512,768]{1,0:T(8,128)(2,1)S(1)} %get-tuple-element.170.gf_ref, bf16[768,512]{1,0:T(8,128)(2,1)S(1)} %bitcast.27, bf16[768,512]{1,0:T(8,128)(2,1)S(1)} %bitcast.39, bf16[512,768]{1,0:T(8,128)(2,1)S(1)} %get-tuple-element.175.saved_ref, ...), custom_call_target="tpu_custom_call" | custom-call | flops 30000001024 | bytes 90000000 | tf_op jit(solution)/shard_map/pallas_call | solution.py:507
  115.2 7.3 %shard_map.400 = (f32[512,768]{1,0:T(8,128)}, f32[8,768]{1,0:T(8,128)S(1)}, bf16[768,768]{1,0:T(8,128)(2,1)S(1)}) custom-call(bf16[512,768]{1,0:T(8,128)(2,1)S(1)} %get-tuple-element.170.gf_ref, bf16[768,512]{1,0:T(8,128)(2,1)S(1)} %bitcast.28, bf16[768,512]{1,0:T(8,128)(2,1)S(1)} %bitcast.40, bf16[512,768]{1,0:T(8,128)(2,1)S(1)} %get-tuple-element.173.saved_ref, ...), custom_call_target="tpu_custom_call" | custom-call | flops 30000001024 | bytes 90000000 | tf_op jit(solution)/shard_map/pallas_call | solution.py:507
  126.1 6.9 %collective-permute-done.39 = bf16[384,768]{1,0:T(8,128)(2,1)S(1)} collective-permute-done((bf16[384,768]{1,0:T(8,128)(2,1)S(1)}, bf16[384,768]{1,0:T(8,128)(2,1)S(1)}, u32[]{:S(2)}, u32[]{:S(2)}) %collective-permute-start.39) | collective-permute-done | bytes 589856 | tf_op jit(solution)/shard_map/ppermute | solution.py:552
  134.2 1.6 collective-permute-start.34
  135.7 2.7 %collective-permute-done.37 = bf16[192,768]{1,0:T(8,128)(2,1)S(1)} collective-permute-done((bf16[192,768]{1,0:T(8,128)(2,1)S(1)}, bf16[192,768]{1,0:T(8,128)(2,1)S(1)}, u32[]{:S(2)}, u32[]{:S(2)}) %collective-permute-start.37) | collective-permute-done | bytes 294944 | tf_op jit(solution)/shard_map/ppermute | solution.py:552
  138.5 2.6 %collective-permute-start.38 = (bf16[96,768]{1,0:T(8,128)(2,1)S(1)}, bf16[96,768]{1,0:T(8,128)(2,1)S(1)}, u32[]{:S(2)}, u32[]{:S(2)}) collective-permute-start(bf16[96,768]{1,0:T(8,128)(2,1)S(1)} %add_convert_fusion.14), channel_id=1, source_target_pairs={{0,16},{4,20},{8,24},{12,28},{16,0},{20,4},{24,8},{28,12},{1,17},{... | collective-permute-start | bytes 442376 | tf_op jit(solution)/shard_map/ppermute | solution.py:552
  142.6 4.0 %collective-permute-done.40 = bf16[192,768]{1,0:T(8,128)(2,1)S(1)} collective-permute-done((bf16[192,768]{1,0:T(8,128)(2,1)S(1)}, bf16[192,768]{1,0:T(8,128)(2,1)S(1)}, u32[]{:S(2)}, u32[]{:S(2)}) %collective-permute-start.40) | collective-permute-done | bytes 294944 | tf_op jit(solution)/shard_map/ppermute | solution.py:552
  146.7 2.6 %collective-permute-start.41 = (bf16[96,768]{1,0:T(8,128)(2,1)S(1)}, bf16[96,768]{1,0:T(8,128)(2,1)S(1)}, u32[]{:S(2)}, u32[]{:S(2)}) collective-permute-start(bf16[96,768]{1,0:T(8,128)(2,1)S(1)} %add_convert_fusion.13), channel_id=1, source_target_pairs={{0,16},{4,20},{8,24},{12,28},{16,0},{20,4},{24,8},{28,12},{1,17},{... | collective-permute-start | bytes 442376 | tf_op jit(solution)/shard_map/ppermute | solution.py:552
  149.6 6.2 %collective-permute-done.31 = bf16[192,768]{1,0:T(8,128)(2,1)S(1)} collective-permute-done((bf16[192,768]{1,0:T(8,128)(2,1)S(1)}, bf16[192,768]{1,0:T(8,128)(2,1)S(1)}, u32[]{:S(2)}, u32[]{:S(2)}) %collective-permute-start.31) | collective-permute-done | bytes 294944 | tf_op jit(solution)/shard_map/ppermute | solution.py:552
  156.2 1.6 shard_map.401
  157.9 4.2 %collective-permute-done.35 = bf16[96,768]{1,0:T(8,128)(2,1)S(1)} collective-permute-done((bf16[96,768]{1,0:T(8,128)(2,1)S(1)}, bf16[96,768]{1,0:T(8,128)(2,1)S(1)}, u32[]{:S(2)}, u32[]{:S(2)}) %collective-permute-start.35) | collective-permute-done | bytes 147488 | tf_op jit(solution)/shard_map/ppermute | solution.py:552
  162.4 1.4 shard_map.402
  165.0 1.5 collective-permute-start.43
  166.6 2.3 %collective-permute-done.43 = f32[8,768]{1,0:T(8,128)S(1)} collective-permute-done((f32[8,768]{1,0:T(8,128)S(1)}, f32[8,768]{1,0:T(8,128)S(1)}, u32[]{:S(2)}, u32[]{:S(2)}) %collective-permute-start.43) | collective-permute-done | bytes 24608 | tf_op jit(solution)/shard_map/ppermute | solution.py:552
  168.9 2.0 %collective-permute-start.44 = (f32[8,768]{1,0:T(8,128)S(1)}, f32[8,768]{1,0:T(8,128)S(1)}, u32[]{:S(2)}, u32[]{:S(2)}) collective-permute-start(f32[8,768]{1,0:T(8,128)S(1)} %add.258), channel_id=1, source_target_pairs={{0,4},{4,0},{8,12},{12,8},{16,20},{20,16},{24,28},{28,24},{1,5},{5... | collective-permute-start | bytes 73736 | tf_op jit(solution)/shard_map/ppermute | solution.py:552
  170.8 1.8 %collective-permute-done.44 = f32[8,768]{1,0:T(8,128)S(1)} collective-permute-done((f32[8,768]{1,0:T(8,128)S(1)}, f32[8,768]{1,0:T(8,128)S(1)}, u32[]{:S(2)}, u32[]{:S(2)}) %collective-permute-start.44) | collective-permute-done | bytes 24608 | tf_op jit(solution)/shard_map/ppermute | solution.py:552
  172.7 1.3 collective-permute-start.45
  174.0 2.5 %collective-permute-done.45 = f32[8,768]{1,0:T(8,128)S(1)} collective-permute-done((f32[8,768]{1,0:T(8,128)S(1)}, f32[8,768]{1,0:T(8,128)S(1)}, u32[]{:S(2)}, u32[]{:S(2)}) %collective-permute-start.45) | collective-permute-done | bytes 24608 | tf_op jit(solution)/shard_map/ppermute | solution.py:552
  176.5 2.9 %collective-permute-start.46 = (f32[8,768]{1,0:T(8,128)S(1)}, f32[8,768]{1,0:T(8,128)S(1)}, u32[]{:S(2)}, u32[]{:S(2)}) collective-permute-start(f32[8,768]{1,0:T(8,128)S(1)} %add.260), channel_id=1, source_target_pairs={{0,16},{4,20},{8,24},{12,28},{16,0},{20,4},{24,8},{28,12},{1,17},{... | collective-permute-start | bytes 73736 | tf_op jit(solution)/shard_map/ppermute | solution.py:552
  179.5 1.8 collective-permute-done.46
  (166 shorter events, 23.6 us)
Async XLA Ops:
  2.2 9.8 %collective-permute-start.2 = (bf16[768,768]{1,0:T(8,128)(2,1)S(1)}, bf16[768,768]{1,0:T(8,128)(2,1)}, u32[]{:S(2)}, u32[]{:S(2)}) collective-permute-start(bf16[768,768]{1,0:T(8,128)(2,1)S(1)} %pad_maximum_fusion.wb_ref.w_ref), channel_id=1, source_target_pairs={{0,1},{1,0},{2,3},{3,2},{4,5},{5,4},{6,7},{7,6},{8,9},{9,8},{10,11... | collective-permute-start | bytes 3538952 | tf_op jit(solution)/shard_map/ppermute | solution.py:552
  2.7 9.3 %collective-permute-start.3 = (bf16[768,768]{1,0:T(8,128)(2,1)S(1)}, bf16[768,768]{1,0:T(8,128)(2,1)}, u32[]{:S(2)}, u32[]{:S(2)}) collective-permute-start(bf16[768,768]{1,0:T(8,128)(2,1)S(1)} %copy-done.16), channel_id=1, source_target_pairs={{0,1},{1,0},{2,3},{3,2},{4,5},{5,4},{6,7},{7,6},{8,9},{9,8},{10,11... | collective-permute-start | bytes 3538952 | tf_op jit(solution)/shard_map/ppermute | solution.py:552
  2.8 9.2 %collective-permute-start.4 = (bf16[768,768]{1,0:T(8,128)(2,1)}, bf16[768,768]{1,0:T(8,128)(2,1)}, u32[]{:S(2)}, u32[]{:S(2)}) collective-permute-start(bf16[768,768]{1,0:T(8,128)(2,1)} %down_ref.1), channel_id=1, source_target_pairs={{0,1},{1,0},{2,3},{3,2},{4,5},{5,4},{6,7},{7,6},{8,9},{9,8},{10,11... | collective-permute-start | bytes 3538952 | tf_op jit(solution)/shard_map/ppermute | solution.py:552
  4.8 5.2 %collective-permute-start.1 = (f32[8]{0:T(128)S(1)}, f32[8]{0:T(128)S(1)}, u32[]{:S(2)}, u32[]{:S(2)}) collective-permute-start(f32[8]{0:T(128)S(1)} %convert_reduce_fusion), channel_id=1, source_target_pairs={{0,2},{1,3},{2,0},{3,1},{4,6},{5,7},{6,4},{7,5},{8,10},{9,11},{10,... | collective-permute-start | bytes 104 | tf_op jit(solution)/shard_map/ppermute | solution.py:552
  7.4 16.2 %collective-permute-start = (bf16[384,768]{1,0:T(8,128)(2,1)S(1)}, bf16[384,768]{1,0:T(8,128)(2,1)S(1)}, u32[]{:S(2)}, u32[]{:S(2)}) collective-permute-start(bf16[384,768]{1,0:T(8,128)(2,1)S(1)} %fusion), channel_id=1, source_target_pairs={{0,2},{1,3},{2,0},{3,1},{4,6},{5,7},{6,4},{7,5},{8,10},{9,11},{10,... | collective-permute-start | bytes 1769480 | tf_op jit(solution)/shard_map/ppermute | solution.py:552
  10.0 27.3 %collective-permute-start.10 = (bf16[384,768]{1,0:T(8,128)(2,1)S(1)}, bf16[384,768]{1,0:T(8,128)(2,1)S(1)}, u32[]{:S(2)}, u32[]{:S(2)}) collective-permute-start(bf16[384,768]{1,0:T(8,128)(2,1)S(1)} %constant_dynamic-slice_fusion.1), channel_id=1, source_target_pairs={{0,2},{1,3},{2,0},{3,1},{4,6},{5,7},{6,4},{7,5},{8,10},{9,11},{10,... | collective-permute-start | bytes 1769480 | tf_op jit(solution)/shard_map/ppermute | solution.py:552
  12.0 8.3 %collective-permute-start.5 = (f32[8]{0:T(128)S(1)}, f32[8]{0:T(128)S(1)}, u32[]{:S(2)}, u32[]{:S(2)}) collective-permute-start(f32[8]{0:T(128)S(1)} %add.200), channel_id=1, source_target_pairs={{0,4},{4,0},{8,12},{12,8},{16,20},{20,16},{24,28},{28,24},{1,5},{5... | collective-permute-start | bytes 104 | tf_op jit(solution)/shard_map/ppermute | solution.py:552
  13.5 23.0 %copy-start.9 = (bf16[512,768]{1,0:T(8,128)(2,1)S(1)}, bf16[512,768]{1,0:T(8,128)(2,1)}, u32[]{:S(2)}) copy-start(bf16[512,768]{1,0:T(8,128)(2,1)} %refs_14_.1) | copy-start | bytes 2359300
  23.6 13.8 %collective-permute-start.9 = (bf16[384,768]{1,0:T(8,128)(2,1)S(1)}, bf16[384,768]{1,0:T(8,128)(2,1)S(1)}, u32[]{:S(2)}, u32[]{:S(2)}) collective-permute-start(bf16[384,768]{1,0:T(8,128)(2,1)S(1)} %collective-permute-done.refs_7_.h_ref), channel_id=1, source_target_pairs={{0,4},{4,0},{8,12},{12,8},{16,20},{20,16},{24,28},{28,24},{1,5},{5... | collective-permute-start | bytes 1769480 | tf_op jit(solution)/shard_map/ppermute | solution.py:552
  25.0 14.5 %collective-permute-start.11 = (bf16[384,768]{1,0:T(8,128)(2,1)S(1)}, bf16[384,768]{1,0:T(8,128)(2,1)S(1)}, u32[]{:S(2)}, u32[]{:S(2)}) collective-permute-start(bf16[384,768]{1,0:T(8,128)(2,1)S(1)} %collective-permute-done.refs_7_.h_ref), channel_id=1, source_target_pairs={{0,1},{1,0},{2,3},{3,2},{4,5},{5,4},{6,7},{7,6},{8,9},{9,8},{10,11... | collective-permute-start | bytes 1769480 | tf_op jit(solution)/shard_map/ppermute | solution.py:552
  25.0 2.0 %collective-permute-start.6 = (f32[8]{0:T(128)S(1)}, f32[8]{0:T(128)S(1)}, u32[]{:S(2)}, u32[]{:S(2)}) collective-permute-start(f32[8]{0:T(128)S(1)} %add.201), channel_id=1, source_target_pairs={{0,1},{1,0},{2,3},{3,2},{4,5},{5,4},{6,7},{7,6},{8,9},{9,8},{10,11... | collective-permute-start | bytes 104 | tf_op jit(solution)/shard_map/ppermute | solution.py:552
  27.0 3.5 %collective-permute-start.7 = (f32[8]{0:T(128)S(1)}, f32[8]{0:T(128)S(1)}, u32[]{:S(2)}, u32[]{:S(2)}) collective-permute-start(f32[8]{0:T(128)S(1)} %add.202), channel_id=1, source_target_pairs={{0,8},{4,12},{8,0},{12,4},{16,24},{20,28},{24,16},{28,20},{1,9},{5... | collective-permute-start | bytes 104 | tf_op jit(solution)/shard_map/ppermute | solution.py:552
  30.6 4.4 %collective-permute-start.8 = (f32[8]{0:T(128)S(1)}, f32[8]{0:T(128)S(1)}, u32[]{:S(2)}, u32[]{:S(2)}) collective-permute-start(f32[8]{0:T(128)S(1)} %add.203), channel_id=1, source_target_pairs={{0,16},{4,20},{8,24},{12,28},{16,0},{20,4},{24,8},{28,12},{1,17},{... | collective-permute-start | bytes 104 | tf_op jit(solution)/shard_map/ppermute | solution.py:552
  37.4 2.2 %collective-permute-start.12 = (bf16[384,768]{1,0:T(8,128)(2,1)S(1)}, bf16[384,768]{1,0:T(8,128)(2,1)S(1)}, u32[]{:S(2)}, u32[]{:S(2)}) collective-permute-start(bf16[384,768]{1,0:T(8,128)(2,1)S(1)} %collective-permute-done.9.refs_8_.i_ref), channel_id=1, source_target_pairs={{0,1},{1,0},{2,3},{3,2},{4,5},{5,4},{6,7},{7,6},{8,9},{9,8},{10,11... | collective-permute-start | bytes 1769480 | tf_op jit(solution)/shard_map/ppermute | solution.py:552
  37.4 16.1 %collective-permute-start.14 = (bf16[768,384]{1,0:T(8,128)(2,1)S(1)}, bf16[768,384]{1,0:T(8,128)(2,1)S(1)}, u32[]{:S(2)}, u32[]{:S(2)}) collective-permute-start(bf16[768,384]{1,0:T(8,128)(2,1)S(1)} %constant_dynamic-slice_fusion), channel_id=1, source_target_pairs={{0,2},{1,3},{2,0},{3,1},{4,6},{5,7},{6,4},{7,5},{8,10},{9,11},{10,... | collective-permute-start | bytes 1769480 | tf_op jit(solution)/shard_map/ppermute | solution.py:552
  38.1 32.7 %collective-permute-start.18 = (bf16[384,768]{1,0:T(8,128)(2,1)S(1)}, bf16[384,768]{1,0:T(8,128)(2,1)S(1)}, u32[]{:S(2)}, u32[]{:S(2)}) collective-permute-start(bf16[384,768]{1,0:T(8,128)(2,1)S(1)} %collective-permute-done.10.refs_7_), channel_id=1, source_target_pairs={{0,1},{1,0},{2,3},{3,2},{4,5},{5,4},{6,7},{7,6},{8,9},{9,8},{10,11... | collective-permute-start | bytes 1769480 | tf_op jit(solution)/shard_map/ppermute | solution.py:552
  38.3 15.5 %collective-permute-start.13 = (bf16[384,768]{1,0:T(8,128)(2,1)S(1)}, bf16[384,768]{1,0:T(8,128)(2,1)S(1)}, u32[]{:S(2)}, u32[]{:S(2)}) collective-permute-start(bf16[384,768]{1,0:T(8,128)(2,1)S(1)} %collective-permute-done.10.refs_7_), channel_id=1, source_target_pairs={{0,4},{4,0},{8,12},{12,8},{16,20},{20,16},{24,28},{28,24},{1,5},{5... | collective-permute-start | bytes 1769480 | tf_op jit(solution)/shard_map/ppermute | solution.py:552
  53.8 18.6 %collective-permute-start.20 = (bf16[768,384]{1,0:T(8,128)(2,1)S(1)}, bf16[768,384]{1,0:T(8,128)(2,1)S(1)}, u32[]{:S(2)}, u32[]{:S(2)}) collective-permute-start(bf16[768,384]{1,0:T(8,128)(2,1)S(1)} %collective-permute-done.14.refs_9_), channel_id=1, source_target_pairs={{0,1},{1,0},{2,3},{3,2},{4,5},{5,4},{6,7},{7,6},{8,9},{9,8},{10,11... | collective-permute-start | bytes 1769480 | tf_op jit(solution)/shard_map/ppermute | solution.py:552
  53.8 15.7 %collective-permute-start.15 = (bf16[768,384]{1,0:T(8,128)(2,1)S(1)}, bf16[768,384]{1,0:T(8,128)(2,1)S(1)}, u32[]{:S(2)}, u32[]{:S(2)}) collective-permute-start(bf16[768,384]{1,0:T(8,128)(2,1)S(1)} %collective-permute-done.14.refs_9_), channel_id=1, source_target_pairs={{0,4},{4,0},{8,12},{12,8},{16,20},{20,16},{24,28},{28,24},{1,5},{5... | collective-permute-start | bytes 1769480 | tf_op jit(solution)/shard_map/ppermute | solution.py:552
  55.1 7.4 %collective-permute-start.16 = (bf16[768,768]{1,0:T(8,128)(2,1)S(1)}, bf16[768,768]{1,0:T(8,128)(2,1)S(1)}, u32[]{:S(2)}, u32[]{:S(2)}) collective-permute-start(bf16[768,768]{1,0:T(8,128)(2,1)S(1)} %get-tuple-element.153), channel_id=1, source_target_pairs={{0,1},{1,0},{2,3},{3,2},{4,5},{5,4},{6,7},{7,6},{8,9},{9,8},{10,11... | collective-permute-start | bytes 3538952 | tf_op jit(solution)/shard_map/ppermute | solution.py:552
  55.3 7.7 %collective-permute-start.17 = (bf16[768,768]{1,0:T(8,128)(2,1)S(1)}, bf16[768,768]{1,0:T(8,128)(2,1)S(1)}, u32[]{:S(2)}, u32[]{:S(2)}) collective-permute-start(bf16[768,768]{1,0:T(8,128)(2,1)S(1)} %get-tuple-element.155), channel_id=1, source_target_pairs={{0,1},{1,0},{2,3},{3,2},{4,5},{5,4},{6,7},{7,6},{8,9},{9,8},{10,11... | collective-permute-start | bytes 3538952 | tf_op jit(solution)/shard_map/ppermute | solution.py:552
  62.5 9.9 %collective-permute-start.19 = (bf16[384,768]{1,0:T(8,128)(2,1)S(1)}, bf16[384,768]{1,0:T(8,128)(2,1)S(1)}, u32[]{:S(2)}, u32[]{:S(2)}) collective-permute-start(bf16[384,768]{1,0:T(8,128)(2,1)S(1)} %collective-permute-done.13.refs_8_), channel_id=1, source_target_pairs={{0,1},{1,0},{2,3},{3,2},{4,5},{5,4},{6,7},{7,6},{8,9},{9,8},{10,11... | collective-permute-start | bytes 1769480 | tf_op jit(solution)/shard_map/ppermute | solution.py:552
  69.6 2.8 %collective-permute-start.21 = (bf16[768,384]{1,0:T(8,128)(2,1)S(1)}, bf16[768,384]{1,0:T(8,128)(2,1)S(1)}, u32[]{:S(2)}, u32[]{:S(2)}) collective-permute-start(bf16[768,384]{1,0:T(8,128)(2,1)S(1)} %collective-permute-done.15.refs_10_), channel_id=1, source_target_pairs={{0,1},{1,0},{2,3},{3,2},{4,5},{5,4},{6,7},{7,6},{8,9},{9,8},{10,11... | collective-permute-start | bytes 1769480 | tf_op jit(solution)/shard_map/ppermute | solution.py:552
  69.6 19.3 %collective-permute-start.24 = (bf16[384,768]{1,0:T(8,128)(2,1)S(1)}, bf16[384,768]{1,0:T(8,128)(2,1)S(1)}, u32[]{:S(2)}, u32[]{:S(2)}) collective-permute-start(bf16[384,768]{1,0:T(8,128)(2,1)S(1)} %add_convert_fusion.7), channel_id=1, source_target_pairs={{0,4},{4,0},{8,12},{12,8},{16,20},{20,16},{24,28},{28,24},{1,5},{5... | collective-permute-start | bytes 1769480 | tf_op jit(solution)/shard_map/ppermute | solution.py:552
  70.8 18.0 %collective-permute-start.25 = (bf16[384,768]{1,0:T(8,128)(2,1)S(1)}, bf16[384,768]{1,0:T(8,128)(2,1)S(1)}, u32[]{:S(2)}, u32[]{:S(2)}) collective-permute-start(bf16[384,768]{1,0:T(8,128)(2,1)S(1)} %add_convert_fusion.6), channel_id=1, source_target_pairs={{0,8},{4,12},{8,0},{12,4},{16,24},{20,28},{24,16},{28,20},{1,9},{5... | collective-permute-start | bytes 1769480 | tf_op jit(solution)/shard_map/ppermute | solution.py:552
  78.6 9.9 %collective-permute-start.22 = (bf16[768,768]{1,0:T(8,128)(2,1)S(1)}, bf16[768,768]{1,0:T(8,128)(2,1)S(1)}, u32[]{:S(2)}, u32[]{:S(2)}) collective-permute-start(bf16[768,768]{1,0:T(8,128)(2,1)S(1)} %get-tuple-element.165), channel_id=1, source_target_pairs={{0,1},{1,0},{2,3},{3,2},{4,5},{5,4},{6,7},{7,6},{8,9},{9,8},{10,11... | collective-permute-start | bytes 3538952 | tf_op jit(solution)/shard_map/ppermute | solution.py:552
  78.7 9.9 %collective-permute-start.23 = (bf16[768,768]{1,0:T(8,128)(2,1)S(1)}, bf16[768,768]{1,0:T(8,128)(2,1)S(1)}, u32[]{:S(2)}, u32[]{:S(2)}) collective-permute-start(bf16[768,768]{1,0:T(8,128)(2,1)S(1)} %get-tuple-element.167), channel_id=1, source_target_pairs={{0,1},{1,0},{2,3},{3,2},{4,5},{5,4},{6,7},{7,6},{8,9},{9,8},{10,11... | collective-permute-start | bytes 3538952 | tf_op jit(solution)/shard_map/ppermute | solution.py:552
  88.8 15.4 %collective-permute-start.27 = (bf16[384,768]{1,0:T(8,128)(2,1)S(1)}, bf16[384,768]{1,0:T(8,128)(2,1)S(1)}, u32[]{:S(2)}, u32[]{:S(2)}) collective-permute-start(bf16[384,768]{1,0:T(8,128)(2,1)S(1)} %add_convert_fusion.5), channel_id=1, source_target_pairs={{0,4},{4,0},{8,12},{12,8},{16,20},{20,16},{24,28},{28,24},{1,5},{5... | collective-permute-start | bytes 1769480 | tf_op jit(solution)/shard_map/ppermute | solution.py:552
  89.6 15.0 %collective-permute-start.28 = (bf16[384,768]{1,0:T(8,128)(2,1)S(1)}, bf16[384,768]{1,0:T(8,128)(2,1)S(1)}, u32[]{:S(2)}, u32[]{:S(2)}) collective-permute-start(bf16[384,768]{1,0:T(8,128)(2,1)S(1)} %add_convert_fusion.4), channel_id=1, source_target_pairs={{0,8},{4,12},{8,0},{12,4},{16,24},{20,28},{24,16},{28,20},{1,9},{5... | collective-permute-start | bytes 1769480 | tf_op jit(solution)/shard_map/ppermute | solution.py:552
  96.0 8.9 %collective-permute-start.26 = (bf16[768,768]{1,0:T(8,128)(2,1)S(1)}, bf16[768,768]{1,0:T(8,128)(2,1)S(1)}, u32[]{:S(2)}, u32[]{:S(2)}) collective-permute-start(bf16[768,768]{1,0:T(8,128)(2,1)S(1)} %get-tuple-element.184), channel_id=1, source_target_pairs={{0,1},{1,0},{2,3},{3,2},{4,5},{5,4},{6,7},{7,6},{8,9},{9,8},{10,11... | collective-permute-start | bytes 3538952 | tf_op jit(solution)/shard_map/ppermute | solution.py:552
  105.0 17.5 %collective-permute-start.32 = (bf16[384,768]{1,0:T(8,128)(2,1)S(1)}, bf16[384,768]{1,0:T(8,128)(2,1)S(1)}, u32[]{:S(2)}, u32[]{:S(2)}) collective-permute-start(bf16[384,768]{1,0:T(8,128)(2,1)S(1)} %add_convert_fusion.3), channel_id=1, source_target_pairs={{0,4},{4,0},{8,12},{12,8},{16,20},{20,16},{24,28},{28,24},{1,5},{5... | collective-permute-start | bytes 1769480 | tf_op jit(solution)/shard_map/ppermute | solution.py:552
  106.4 16.8 %collective-permute-start.36 = (bf16[384,768]{1,0:T(8,128)(2,1)S(1)}, bf16[384,768]{1,0:T(8,128)(2,1)S(1)}, u32[]{:S(2)}, u32[]{:S(2)}) collective-permute-start(bf16[384,768]{1,0:T(8,128)(2,1)S(1)} %add_convert_fusion.2), channel_id=1, source_target_pairs={{0,2},{1,3},{2,0},{3,1},{4,6},{5,7},{6,4},{7,5},{8,10},{9,11},{10,... | collective-permute-start | bytes 1769480 | tf_op jit(solution)/shard_map/ppermute | solution.py:552
  107.9 25.0 %collective-permute-start.39 = (bf16[384,768]{1,0:T(8,128)(2,1)S(1)}, bf16[384,768]{1,0:T(8,128)(2,1)S(1)}, u32[]{:S(2)}, u32[]{:S(2)}) collective-permute-start(bf16[384,768]{1,0:T(8,128)(2,1)S(1)} %add_convert_fusion.1), channel_id=1, source_target_pairs={{0,2},{1,3},{2,0},{3,1},{4,6},{5,7},{6,4},{7,5},{8,10},{9,11},{10,... | collective-permute-start | bytes 1769480 | tf_op jit(solution)/shard_map/ppermute | solution.py:552
  115.1 9.9 %collective-permute-start.29 = (bf16[768,768]{1,0:T(8,128)(2,1)S(1)}, bf16[768,768]{1,0:T(8,128)(2,1)S(1)}, u32[]{:S(2)}, u32[]{:S(2)}) collective-permute-start(bf16[768,768]{1,0:T(8,128)(2,1)S(1)} %get-tuple-element.192), channel_id=1, source_target_pairs={{0,1},{1,0},{2,3},{3,2},{4,5},{5,4},{6,7},{7,6},{8,9},{9,8},{10,11... | collective-permute-start | bytes 3538952 | tf_op jit(solution)/shard_map/ppermute | solution.py:552
  122.6 11.3 %collective-permute-start.33 = (bf16[192,768]{1,0:T(8,128)(2,1)S(1)}, bf16[192,768]{1,0:T(8,128)(2,1)S(1)}, u32[]{:S(2)}, u32[]{:S(2)}) collective-permute-start(bf16[192,768]{1,0:T(8,128)(2,1)S(1)} %add_convert_fusion.11), channel_id=1, source_target_pairs={{0,8},{4,12},{8,0},{12,4},{16,24},{20,28},{24,16},{28,20},{1,9},{5... | collective-permute-start | bytes 884744 | tf_op jit(solution)/shard_map/ppermute | solution.py:552
  124.0 14.4 %collective-permute-start.37 = (bf16[192,768]{1,0:T(8,128)(2,1)S(1)}, bf16[192,768]{1,0:T(8,128)(2,1)S(1)}, u32[]{:S(2)}, u32[]{:S(2)}) collective-permute-start(bf16[192,768]{1,0:T(8,128)(2,1)S(1)} %add_convert_fusion.9), channel_id=1, source_target_pairs={{0,8},{4,12},{8,0},{12,4},{16,24},{20,28},{24,16},{28,20},{1,9},{5... | collective-permute-start | bytes 884744 | tf_op jit(solution)/shard_map/ppermute | solution.py:552
  125.1 16.3 %collective-permute-start.30 = (bf16[384,768]{1,0:T(8,128)(2,1)S(1)}, bf16[384,768]{1,0:T(8,128)(2,1)S(1)}, u32[]{:S(2)}, u32[]{:S(2)}) collective-permute-start(bf16[384,768]{1,0:T(8,128)(2,1)S(1)} %add_convert_fusion), channel_id=1, source_target_pairs={{0,4},{4,0},{8,12},{12,8},{16,20},{20,16},{24,28},{28,24},{1,5},{5... | collective-permute-start | bytes 1769480 | tf_op jit(solution)/shard_map/ppermute | solution.py:552
  133.1 13.5 %collective-permute-start.40 = (bf16[192,768]{1,0:T(8,128)(2,1)S(1)}, bf16[192,768]{1,0:T(8,128)(2,1)S(1)}, u32[]{:S(2)}, u32[]{:S(2)}) collective-permute-start(bf16[192,768]{1,0:T(8,128)(2,1)S(1)} %add_convert_fusion.8), channel_id=1, source_target_pairs={{0,4},{4,0},{8,12},{12,8},{16,20},{20,16},{24,28},{28,24},{1,5},{5... | collective-permute-start | bytes 884744 | tf_op jit(solution)/shard_map/ppermute | solution.py:552
  134.2 15.4 %collective-permute-start.34 = (bf16[192,768]{1,0:T(8,128)(2,1)S(1)}, bf16[192,768]{1,0:T(8,128)(2,1)S(1)}, u32[]{:S(2)}, u32[]{:S(2)}) collective-permute-start(bf16[192,768]{1,0:T(8,128)(2,1)S(1)} %add_convert_fusion.10), channel_id=1, source_target_pairs={{0,2},{1,3},{2,0},{3,1},{4,6},{5,7},{6,4},{7,5},{8,10},{9,11},{10,... | collective-permute-start | bytes 884744 | tf_op jit(solution)/shard_map/ppermute | solution.py:552
  138.5 10.9 %collective-permute-start.38 = (bf16[96,768]{1,0:T(8,128)(2,1)S(1)}, bf16[96,768]{1,0:T(8,128)(2,1)S(1)}, u32[]{:S(2)}, u32[]{:S(2)}) collective-permute-start(bf16[96,768]{1,0:T(8,128)(2,1)S(1)} %add_convert_fusion.14), channel_id=1, source_target_pairs={{0,16},{4,20},{8,24},{12,28},{16,0},{20,4},{24,8},{28,12},{1,17},{... | collective-permute-start | bytes 442376 | tf_op jit(solution)/shard_map/ppermute | solution.py:552
  141.5 14.3 %collective-permute-start.31 = (bf16[192,768]{1,0:T(8,128)(2,1)S(1)}, bf16[192,768]{1,0:T(8,128)(2,1)S(1)}, u32[]{:S(2)}, u32[]{:S(2)}) collective-permute-start(bf16[192,768]{1,0:T(8,128)(2,1)S(1)} %add_convert_fusion.12), channel_id=1, source_target_pairs={{0,8},{4,12},{8,0},{12,4},{16,24},{20,28},{24,16},{28,20},{1,9},{5... | collective-permute-start | bytes 884744 | tf_op jit(solution)/shard_map/ppermute | solution.py:552
  146.7 9.3 %collective-permute-start.41 = (bf16[96,768]{1,0:T(8,128)(2,1)S(1)}, bf16[96,768]{1,0:T(8,128)(2,1)S(1)}, u32[]{:S(2)}, u32[]{:S(2)}) collective-permute-start(bf16[96,768]{1,0:T(8,128)(2,1)S(1)} %add_convert_fusion.13), channel_id=1, source_target_pairs={{0,16},{4,20},{8,24},{12,28},{16,0},{20,4},{24,8},{28,12},{1,17},{... | collective-permute-start | bytes 442376 | tf_op jit(solution)/shard_map/ppermute | solution.py:552
  155.9 6.2 %collective-permute-start.35 = (bf16[96,768]{1,0:T(8,128)(2,1)S(1)}, bf16[96,768]{1,0:T(8,128)(2,1)S(1)}, u32[]{:S(2)}, u32[]{:S(2)}) collective-permute-start(bf16[96,768]{1,0:T(8,128)(2,1)S(1)} %add_convert_fusion.15), channel_id=1, source_target_pairs={{0,16},{4,20},{8,24},{12,28},{16,0},{20,4},{24,8},{28,12},{1,17},{... | collective-permute-start | bytes 442376 | tf_op jit(solution)/shard_map/ppermute | solution.py:552
  163.8 1.2 collective-permute-start.42
  165.0 3.8 %collective-permute-start.43 = (f32[8,768]{1,0:T(8,128)S(1)}, f32[8,768]{1,0:T(8,128)S(1)}, u32[]{:S(2)}, u32[]{:S(2)}) collective-permute-start(f32[8,768]{1,0:T(8,128)S(1)} %add.257), channel_id=1, source_target_pairs={{0,2},{1,3},{2,0},{3,1},{4,6},{5,7},{6,4},{7,5},{8,10},{9,11},{10,... | collective-permute-start | bytes 73736 | tf_op jit(solution)/shard_map/ppermute | solution.py:552
  168.9 3.8 %collective-permute-start.44 = (f32[8,768]{1,0:T(8,128)S(1)}, f32[8,768]{1,0:T(8,128)S(1)}, u32[]{:S(2)}, u32[]{:S(2)}) collective-permute-start(f32[8,768]{1,0:T(8,128)S(1)} %add.258), channel_id=1, source_target_pairs={{0,4},{4,0},{8,12},{12,8},{16,20},{20,16},{24,28},{28,24},{1,5},{5... | collective-permute-start | bytes 73736 | tf_op jit(solution)/shard_map/ppermute | solution.py:552
  172.7 3.8 %collective-permute-start.45 = (f32[8,768]{1,0:T(8,128)S(1)}, f32[8,768]{1,0:T(8,128)S(1)}, u32[]{:S(2)}, u32[]{:S(2)}) collective-permute-start(f32[8,768]{1,0:T(8,128)S(1)} %add.259), channel_id=1, source_target_pairs={{0,8},{4,12},{8,0},{12,4},{16,24},{20,28},{24,16},{28,20},{1,9},{5... | collective-permute-start | bytes 73736 | tf_op jit(solution)/shard_map/ppermute | solution.py:552
  176.5 4.7 %collective-permute-start.46 = (f32[8,768]{1,0:T(8,128)S(1)}, f32[8,768]{1,0:T(8,128)S(1)}, u32[]{:S(2)}, u32[]{:S(2)}) collective-permute-start(f32[8,768]{1,0:T(8,128)S(1)} %add.260), channel_id=1, source_target_pairs={{0,16},{4,20},{8,24},{12,28},{16,0},{20,4},{24,8},{28,12},{1,17},{... | collective-permute-start | bytes 73736 | tf_op jit(solution)/shard_map/ppermute | solution.py:552
  (33 other events, 222.3 us)

commit v2 on v1

--- a/solution.py
+++ b/solution.py
@@ -121,7 +121,7 @@
             jax.ShapeDtypeStruct(turned_shape(d, r, count), BF16),
         ),
         in_specs=[SMEM, pl.BlockSpec(memory_space=pltpu.VMEM), pl.BlockSpec(memory_space=pltpu.VMEM)],
-        compiler_params=params(BIG),
+        compiler_params=params(6),
     )(pos, rows, vectors)
 
 
@@ -143,7 +143,7 @@
             jax.ShapeDtypeStruct(turned_shape(d, r, count), BF16),
         ),
         in_specs=[SMEM, SMEM, pl.BlockSpec(memory_space=pltpu.VMEM)],
-        compiler_params=params(BIG),
+        compiler_params=params(4),
     )(pos, weight, cot)
 
 
@@ -226,7 +226,7 @@
 
 
 def cost(micros):
-    return pl.CostEstimate(flops=int(micros * 5 * 1e9), bytes_accessed=int(micros * 5 * 3e6), transcendentals=0)
+    return pl.CostEstimate(flops=int(micros * 3 * 1e9), bytes_accessed=int(micros * 3 * 3e6), transcendentals=0)
 
 
 def run_attn_one(x, rows, vectors, wa, wb):
@@ -239,7 +239,7 @@
         out_shape=(jax.ShapeDtypeStruct((r, d), F32),) + shapes * 2,
         in_specs=[image_block(d), image_block(d), full(vectors.shape), full((d, d)), full((d, d))],
         out_specs=[image_block(d)] + specs * 2,
-        compiler_params=params(BIG),
+        compiler_params=params(9),
         cost_estimate=cost(7),
     )(x, rows, vectors, wa, wb)
 
@@ -265,7 +265,7 @@
         + [full((d // 2, d))] * 4,
         out_specs=[image_block(d), image_block(d), tspec] + specs * 2,
         scratch_shapes=[pltpu.VMEM((d, d), BF16)] * 2,
-        compiler_params=params(BIG),
+        compiler_params=params(9),
         cost_estimate=cost(7),
     )(pos, low, x, acc, vectors, *wa, *wb)
 
@@ -330,7 +330,7 @@
 
     @pl.when(pl.program_id(0) == pl.num_programs(0) - 1)
     def _():
-        chunk = 128
+        chunk = 256
 
         def body(index, sums):
             start = pl.multiple_of(index * chunk, chunk)
@@ -370,7 +370,7 @@
         out_shape=(jax.ShapeDtypeStruct((r, d), F32),) * 2 + (grad,) * 2,
         in_specs=[full((r, d)), full((d, r)), full((r, d)), full((d, r))] + w_specs + [full((r, d))] * len(before),
         out_specs=[full((r, d))] * 2 + g_specs,
-        compiler_params=params(BIG),
+        compiler_params=params(10),
         cost_estimate=cost(6),
     )(mid, midt, g, gt, w_in, w_down, *before)
 
@@ -385,7 +385,7 @@
         out_shape=(jax.ShapeDtypeStruct((r, d), F32),) * 2 + (grad,) * 2,
         in_specs=[SMEM, full((r, d)), full((d, r)), full((r, d)), full((d, r))] + w_specs + [full((r, d))] * 2,
         out_specs=[full((r, d))] * 2 + g_specs,
-        compiler_params=params(BIG),
+        compiler_params=params(12),
         cost_estimate=cost(6),
     )(low, mid, midt, g, gt, *w_in, *w_down, y, dm)
 
@@ -412,7 +412,7 @@
         + [full(vectors.shape)],
         out_specs=[full((r, d)), full((r, d)), full((r, d)), full(tshape), full((8, d))] + g_specs,
         scratch_shapes=[pltpu.VMEM((r, d), F32)] * 2,
-        compiler_params=params(BIG),
+        compiler_params=params(14),
         cost_estimate=cost(8),
     )(pos, low, weight, mid, midt, g, gt, *w_in, *w_down, y, dm, first, cot, vectors)
 
@@ -432,9 +432,9 @@
         dv.append(mm(probs, do).astype(BF16))
         dp = mm_nt(v, do)
         wide = probs.astype(F32)
-        ds = (SCALE * wide * (dp - jnp.sum(wide * dp, axis=0, keepdims=True))).astype(BF16)
-        dq.append(mm_tn(ds, k).astype(BF16))
-        dk.append(mm(ds, q).astype(BF16))
+        ds = (wide * (dp - jnp.sum(wide * dp, axis=0, keepdims=True))).astype(BF16)
+        dq.append((SCALE * mm_tn(ds, k)).astype(BF16))
+        dk.append((SCALE * mm(ds, q)).astype(BF16))
     dqkv = jnp.concatenate(dq + dk + dv, axis=1)
     keep_ref[pl.ds(start, PATCHES), : 3 * cols] = dqkv
     keep_ref[pl.ds(start, PATCHES), 3 * cols :] = saved_ref[:, 3 * cols :]
@@ -511,7 +511,7 @@
         in_specs=([SMEM] if far else []) + [image_block(d)] + [full((d, r))] * 2 + saved_specs + specs,
         out_specs=out_specs + [full((d, d))],
         scratch_shapes=[keep, whole] if far else [keep],
-        compiler_params=params(BIG),
+        compiler_params=params(9),
         cost_estimate=cost(6),
     )(*ops)
 
@@ -648,7 +648,7 @@
     return pl.pallas_call(
         dense_step_kernel,
         out_shape=(shape,) * 6 + (jax.ShapeDtypeStruct((1, width), F32),),
-        compiler_params=params(BIG),
+        compiler_params=params(6),
     )(*in_parts, *down_parts)
 
 
@@ -691,7 +691,7 @@
     return pl.pallas_call(
         attn_step_kernel,
         out_shape=(q,) * 4 + (o,) * 4 + (jax.ShapeDtypeStruct(sums_a.shape, F32),),
-        compiler_params=params(BIG),
+        compiler_params=params(6),
     )(whole, *qkv, *out, sums_a, sums_b, squares)
 
 
@@ -729,7 +729,7 @@
         out_shape=tuple(shape(flat(m)) for m in masters)
         + (shape(vectors),) * 4
         + (jax.ShapeDtypeStruct((3, 4), F32),),
-        compiler_params=params(BIG),
+        compiler_params=params(6),
     )(small, vectors, vec_first, vec_second, *(flat(m) for m in masters), *(flat(u) for u in updates))
     new = [value.reshape(m.shape) for value, m in zip(outs[:4], masters)]
     return new, outs[4:]

time: 183 us -> 182 us (level)
  waiting for transfers between devices: 51.3 us -> 57.4 us
  starting transfers between devices: 45.5 us -> 41.2 us
    ppermute x47, waiting for transfers between devices: 51.3 us -> 57.4 us  [swap(): return lax.ppermute(value, axis, [(i, i ^ bit) for i in range(size)])]
    ppermute x47, starting transfers between devices: 45.5 us -> 41.2 us  [swap(): return lax.ppermute(value, axis, [(i, i ^ bit) for i in range(size)])]
  transfers between devices with their start and end apart: 47 -> 47, of which waited for: 20 -> 21; matrix products, arithmetic and copies ran while one was open for 4% -> 4% of each run, Pallas kernels for 39% -> 39%
where the time goes in v2:
time: 182 us
  Pallas kernels  73.5 us (40%)
  waiting for transfers between devices  57.4 us (32%)
  starting transfers between devices  41.2 us (23%)
  other arithmetic  7.09 us (4%)
    ppermute x47, waiting for transfers between devices, swap(): return lax.ppermute(value, axis, [(i, i ^ bit) for i in range(size)])  57.4 us
    ppermute x47, starting transfers between devices, swap(): return lax.ppermute(value, axis, [(i, i ^ bit) for i in range(size)])  41.2 us
    pallas_call x4, Pallas kernels, back_call(): pl.pallas_call(kernel, grid=(r // PATCHES,), out_shape=tuple(outs) + (jax...  24.7 us
    pallas_call x2, Pallas kernels, run_ffn_near(): pl.pallas_call(ffn_near_kernel, grid=(TILES,), out_shape=(jax.ShapeDtypeS...  13.8 us
    pallas_call x1, Pallas kernels, run_ffn_last(): pl.pallas_call(lambda *refs: ffn_last_kernel(*refs, count=count), grid=(T...  9.01 us
    pallas_call x1, Pallas kernels, run_attn_two(): pl.pallas_call(lambda *refs: attn_two_kernel(*refs, count=count), grid=(r...  6.87 us
    pallas_call x1, Pallas kernels, run_attn_one(): pl.pallas_call(attn_one_kernel, grid=(r // PATCHES,), out_shape=(jax.Shap...  6.82 us
    pallas_call x1, Pallas kernels, run_ffn_far(): pl.pallas_call(ffn_far_kernel, grid=(TILES,), out_shape=(jax.ShapeDtypeSt...  6.08 us
  transfers between devices with their start and end apart: 47, of which 21 were waited for; matrix products, arithmetic and copies ran while one was open for 4% of the time, Pallas kernels for 39%

profile of v2, /device:TPU:0, one launch (start us, length us, event | category | flops | bytes accessed | tf_op | source)
XLA Modules:
  0.0 181.8 jit_solution(15684445856130312963)
XLA Ops:
  0.7 1.4 pad_maximum_fusion.wb_ref.w_ref
  3.3 1.5 fusion
  4.8 2.7 %collective-permute-start.1 = (f32[8]{0:T(128)S(1)}, f32[8]{0:T(128)S(1)}, u32[]{:S(2)}, u32[]{:S(2)}) collective-permute-start(f32[8]{0:T(128)S(1)} %convert_reduce_fusion), channel_id=1, source_target_pairs={{0,2},{1,3},{2,0},{3,1},{4,6},{5,7},{6,4},{7,5},{8,10},{9,11},{10,... | collective-permute-start | bytes 104 | tf_op jit(solution)/shard_map/ppermute | solution.py:552
  10.0 2.0 %collective-permute-start.10 = (bf16[384,768]{1,0:T(8,128)(2,1)S(1)}, bf16[384,768]{1,0:T(8,128)(2,1)S(1)}, u32[]{:S(2)}, u32[]{:S(2)}) collective-permute-start(bf16[384,768]{1,0:T(8,128)(2,1)S(1)} %constant_dynamic-slice_fusion.1), channel_id=1, source_target_pairs={{0,2},{1,3},{2,0},{3,1},{4,6},{5,7},{6,4},{7,5},{8,10},{9,11},{10,... | collective-permute-start | bytes 1769480 | tf_op jit(solution)/shard_map/ppermute | solution.py:552
  12.0 1.5 collective-permute-start.5
  13.5 6.8 %shard_map.390 = (f32[512,768]{1,0:T(8,128)S(1)}, bf16[512,768]{1,0:T(8,128)(2,1)S(1)}, bf16[6,256,256]{2,1,0:T(8,128)(2,1)S(1)}, bf16[512,768]{1,0:T(8,128)(2,1)S(1)}, bf16[6,256,256]{2,1,0:T(8,128)(2,1)S(1)}) custom-call(bf16[512,768]{1,0:T(8,128)(2,1)S(1)} %get-tuple-element.127.x_ref.refs_2_, bf16[512,768]{1,0:T(8,128)(2,1)S(1)} %copy-done.6, ...), custom_call_target="tpu_custom_call" | custom-call | flops 20999999488 | bytes 63000000 | tf_op jit(solution)/shard_map/pallas_call | solution.py:236
  20.3 3.3 %collective-permute-done.refs_7_.h_ref = bf16[384,768]{1,0:T(8,128)(2,1)S(1)} collective-permute-done((bf16[384,768]{1,0:T(8,128)(2,1)S(1)}, bf16[384,768]{1,0:T(8,128)(2,1)S(1)}, u32[]{:S(2)}, u32[]{:S(2)}) %collective-permute-start) | collective-permute-done | bytes 589856 | tf_op jit(solution)/shard_map/ppermute | solution.py:552
  23.6 1.4 collective-permute-start.9
  25.5 1.5 collective-permute-done.6
  27.0 1.6 collective-permute-start.7
  28.6 2.0 %collective-permute-done.7 = f32[8]{0:T(128)S(1)} collective-permute-done((f32[8]{0:T(128)S(1)}, f32[8]{0:T(128)S(1)}, u32[]{:S(2)}, u32[]{:S(2)}) %collective-permute-start.7) | collective-permute-done | bytes 64 | tf_op jit(solution)/shard_map/ppermute | solution.py:552
  30.6 2.6 %collective-permute-start.8 = (f32[8]{0:T(128)S(1)}, f32[8]{0:T(128)S(1)}, u32[]{:S(2)}, u32[]{:S(2)}) collective-permute-start(f32[8]{0:T(128)S(1)} %add.203), channel_id=1, source_target_pairs={{0,16},{4,20},{8,24},{12,28},{16,0},{20,4},{24,8},{28,12},{1,17},{... | collective-permute-start | bytes 104 | tf_op jit(solution)/shard_map/ppermute | solution.py:552
  33.2 1.9 %collective-permute-done.8 = f32[8]{0:T(128)S(1)} collective-permute-done((f32[8]{0:T(128)S(1)}, f32[8]{0:T(128)S(1)}, u32[]{:S(2)}, u32[]{:S(2)}) %collective-permute-start.8) | collective-permute-done | bytes 64 | tf_op jit(solution)/shard_map/ppermute | solution.py:552
  38.3 1.2 collective-permute-start.13
  39.5 6.9 %shard_map.392 = (f32[512,768]{1,0:T(8,128)S(1)}, bf16[512,768]{1,0:T(8,128)(2,1)S(1)}, bf16[8,96,512]{2,1,0:T(8,128)(2,1)S(1)}, bf16[512,768]{1,0:T(8,128)(2,1)...) custom-call(s32[8]{0:T(128)S(1)} %get-tuple-element.226.refs_0_, ...), custom_call_target="tpu_custom_call" | custom-call | flops 20999999488 | bytes 63000000 | tf_op jit(solution)/shard_map/pallas_call | solution.py:255
  46.4 7.0 %shard_map.393 = (f32[512,768]{1,0:T(8,128)S(1)}, f32[512,768]{1,0:T(8,128)S(1)}, bf16[768,768]{1,0:T(8,128)(2,1)S(1)}, bf16[768,768]{1,0:T(8,128)(2,1)S(1)}) custom-call(bf16[512,768]{1,0:T(8,128)(2,1)S(1)} %get-tuple-element.137.mid_ref.refs_3_, bf16[768,512]{1,0:T(8,128)(2,1)S(1)} %bitcast.33, bf16[512,768]{1,0:T(8,128)(2,1)S(1)} %get-tuple-element.139.g_ref.refs_5_, ...), custom_call_target="tpu_custom_call" | custom-call | flops 17999998976 | bytes 54000000 | tf_op jit(solution)/shard_map/pallas_call | solution.py:367
  53.8 1.2 collective-permute-start.15
  55.6 6.8 %shard_map.394 = (f32[512,768]{1,0:T(8,128)S(1)}, f32[512,768]{1,0:T(8,128)S(1)}, bf16[768,768]{1,0:T(8,128)(2,1)S(1)}, bf16[768,768]{1,0:T(8,128)(2,1)S(1)}) custom-call(bf16[512,768]{1,0:T(8,128)(2,1)S(1)} %get-tuple-element.137.mid_ref.refs_3_, bf16[768,512]{1,0:T(8,128)(2,1)S(1)} %bitcast.34, bf16[512,768]{1,0:T(8,128)(2,1)S(1)} %get-tuple-element.139.g_ref.refs_5_, ...), custom_call_target="tpu_custom_call" | custom-call | flops 17999998976 | bytes 54000000 | tf_op jit(solution)/shard_map/pallas_call | solution.py:367
  63.0 6.6 %collective-permute-done.15.refs_10_ = bf16[768,384]{1,0:T(8,128)(2,1)S(1)} collective-permute-done((bf16[768,384]{1,0:T(8,128)(2,1)S(1)}, bf16[768,384]{1,0:T(8,128)(2,1)S(1)}, u32[]{:S(2)}, u32[]{:S(2)}) %collective-permute-start.15) | collective-permute-done | bytes 589856 | tf_op jit(solution)/shard_map/ppermute | solution.py:552
  69.6 1.2 collective-permute-start.24
  70.8 1.6 collective-permute-start.25
  72.4 6.1 %shard_map.395 = (f32[512,768]{1,0:T(8,128)S(1)}, f32[512,768]{1,0:T(8,128)S(1)}, bf16[768,768]{1,0:T(8,128)(2,1)S(1)}, bf16[768,768]{1,0:T(8,128)(2,1)S(1)}) custom-call(s32[1]{0:T(128)} %bitcast.refs_1_.low_ref, bf16[512,768]{1,0:T(8,128)(2,1)S(1)} %get-tuple-element.137.mid_ref.refs_3_, bf16[768,512]{1,0:T(8,128)(2,1)S(1)} %bitcast.35, ...), custom_call_target="tpu_custom_call" | custom-call | flops 17999998976 | bytes 54000000 | tf_op jit(solution)/shard_map/pallas_call | solution.py:382
  79.1 9.0 %shard_map.396 = (bf16[512,768]{1,0:T(8,128)(2,1)}, f32[512,768]{1,0:T(8,128)S(1)}, bf16[512,768]{1,0:T(8,128)(2,1)S(1)}, bf16[8,96,512]{2,1,0:T(8,128)(2,1)S(1)...) custom-call(s32[8]{0:T(128)S(1)} %get-tuple-element.226.refs_0_, ...), custom_call_target="tpu_custom_call" | custom-call | flops 24000000000 | bytes 72000000 | tf_op jit(solution)/shard_map/pallas_call | solution.py:398
  90.2 5.3 %shard_map.397 = (f32[512,768]{1,0:T(8,128)S(1)}, bf16[768,768]{1,0:T(8,128)(2,1)S(1)}) custom-call(s32[1]{0:T(128)} %bitcast.refs_1_.low_ref, bf16[512,768]{1,0:T(8,128)(2,1)S(1)} %get-tuple-element.170.gf_ref, bf16[768,512]{1,0:T(8,128)(2,1)S(1)} %bitcast.25, bf16[768,512]{1,0:T(8,128)(2,1)S(1)} %bitcast.37, ...), custom_call_target="tpu_custom_call" | custom-call | flops 17999998976 | bytes 54000000 | tf_op jit(solution)/shard_map/pallas_call | solution.py:507
  95.6 5.4 %shard_map.398 = (f32[512,768]{1,0:T(8,128)S(1)}, bf16[768,768]{1,0:T(8,128)(2,1)S(1)}) custom-call(s32[1]{0:T(128)} %bitcast.refs_1_.low_ref, bf16[512,768]{1,0:T(8,128)(2,1)S(1)} %get-tuple-element.170.gf_ref, bf16[768,512]{1,0:T(8,128)(2,1)S(1)} %bitcast.26, bf16[768,512]{1,0:T(8,128)(2,1)S(1)} %bitcast.38, ...), custom_call_target="tpu_custom_call" | custom-call | flops 17999998976 | bytes 54000000 | tf_op jit(solution)/shard_map/pallas_call | solution.py:507
  101.0 2.8 %collective-permute-done.27 = bf16[384,768]{1,0:T(8,128)(2,1)S(1)} collective-permute-done((bf16[384,768]{1,0:T(8,128)(2,1)S(1)}, bf16[384,768]{1,0:T(8,128)(2,1)S(1)}, u32[]{:S(2)}, u32[]{:S(2)}) %collective-permute-start.27) | collective-permute-done | bytes 589856 | tf_op jit(solution)/shard_map/ppermute | solution.py:552
  104.5 1.4 collective-permute-start.32
  105.9 1.5 collective-permute-start.36
  108.0 6.7 %shard_map.399 = (f32[512,768]{1,0:T(8,128)S(1)}, bf16[768,768]{1,0:T(8,128)(2,1)S(1)}) custom-call(bf16[512,768]{1,0:T(8,128)(2,1)S(1)} %get-tuple-element.170.gf_ref, bf16[768,512]{1,0:T(8,128)(2,1)S(1)} %bitcast.27, bf16[768,512]{1,0:T(8,128)(2,1)S(1)} %bitcast.39, bf16[512,768]{1,0:T(8,128)(2,1)S(1)} %get-tuple-element.175.saved_ref, ...), custom_call_target="tpu_custom_call" | custom-call | flops 17999998976 | bytes 54000000 | tf_op jit(solution)/shard_map/pallas_call | solution.py:507
  114.7 7.3 %shard_map.400 = (f32[512,768]{1,0:T(8,128)}, f32[8,768]{1,0:T(8,128)S(1)}, bf16[768,768]{1,0:T(8,128)(2,1)S(1)}) custom-call(bf16[512,768]{1,0:T(8,128)(2,1)S(1)} %get-tuple-element.170.gf_ref, bf16[768,512]{1,0:T(8,128)(2,1)S(1)} %bitcast.28, bf16[768,512]{1,0:T(8,128)(2,1)S(1)} %bitcast.40, bf16[512,768]{1,0:T(8,128)(2,1)S(1)} %get-tuple-element.173.saved_ref, ...), custom_call_target="tpu_custom_call" | custom-call | flops 17999998976 | bytes 54000000 | tf_op jit(solution)/shard_map/pallas_call | solution.py:507
  122.9 1.6 collective-permute-start.37
  125.4 7.1 %collective-permute-done.39 = bf16[384,768]{1,0:T(8,128)(2,1)S(1)} collective-permute-done((bf16[384,768]{1,0:T(8,128)(2,1)S(1)}, bf16[384,768]{1,0:T(8,128)(2,1)S(1)}, u32[]{:S(2)}, u32[]{:S(2)}) %collective-permute-start.39) | collective-permute-done | bytes 589856 | tf_op jit(solution)/shard_map/ppermute | solution.py:552
  133.7 1.6 collective-permute-start.34
  135.2 2.7 %collective-permute-done.37 = bf16[192,768]{1,0:T(8,128)(2,1)S(1)} collective-permute-done((bf16[192,768]{1,0:T(8,128)(2,1)S(1)}, bf16[192,768]{1,0:T(8,128)(2,1)S(1)}, u32[]{:S(2)}, u32[]{:S(2)}) %collective-permute-start.37) | collective-permute-done | bytes 294944 | tf_op jit(solution)/shard_map/ppermute | solution.py:552
  138.0 2.6 %collective-permute-start.38 = (bf16[96,768]{1,0:T(8,128)(2,1)S(1)}, bf16[96,768]{1,0:T(8,128)(2,1)S(1)}, u32[]{:S(2)}, u32[]{:S(2)}) collective-permute-start(bf16[96,768]{1,0:T(8,128)(2,1)S(1)} %add_convert_fusion.14), channel_id=1, source_target_pairs={{0,16},{4,20},{8,24},{12,28},{16,0},{20,4},{24,8},{28,12},{1,17},{... | collective-permute-start | bytes 442376 | tf_op jit(solution)/shard_map/ppermute | solution.py:552
  141.6 4.6 %collective-permute-done.40 = bf16[192,768]{1,0:T(8,128)(2,1)S(1)} collective-permute-done((bf16[192,768]{1,0:T(8,128)(2,1)S(1)}, bf16[192,768]{1,0:T(8,128)(2,1)S(1)}, u32[]{:S(2)}, u32[]{:S(2)}) %collective-permute-start.40) | collective-permute-done | bytes 294944 | tf_op jit(solution)/shard_map/ppermute | solution.py:552
  146.2 2.6 %collective-permute-start.41 = (bf16[96,768]{1,0:T(8,128)(2,1)S(1)}, bf16[96,768]{1,0:T(8,128)(2,1)S(1)}, u32[]{:S(2)}, u32[]{:S(2)}) collective-permute-start(bf16[96,768]{1,0:T(8,128)(2,1)S(1)} %add_convert_fusion.13), channel_id=1, source_target_pairs={{0,16},{4,20},{8,24},{12,28},{16,0},{20,4},{24,8},{28,12},{1,17},{... | collective-permute-start | bytes 442376 | tf_op jit(solution)/shard_map/ppermute | solution.py:552
  149.1 6.1 %collective-permute-done.31 = bf16[192,768]{1,0:T(8,128)(2,1)S(1)} collective-permute-done((bf16[192,768]{1,0:T(8,128)(2,1)S(1)}, bf16[192,768]{1,0:T(8,128)(2,1)S(1)}, u32[]{:S(2)}, u32[]{:S(2)}) %collective-permute-start.31) | collective-permute-done | bytes 294944 | tf_op jit(solution)/shard_map/ppermute | solution.py:552
  155.4 1.4 collective-permute-done.41
  157.0 1.7 shard_map.401
  158.7 2.8 %collective-permute-done.35 = bf16[96,768]{1,0:T(8,128)(2,1)S(1)} collective-permute-done((bf16[96,768]{1,0:T(8,128)(2,1)S(1)}, bf16[96,768]{1,0:T(8,128)(2,1)S(1)}, u32[]{:S(2)}, u32[]{:S(2)}) %collective-permute-start.35) | collective-permute-done | bytes 147488 | tf_op jit(solution)/shard_map/ppermute | solution.py:552
  161.7 1.5 shard_map.402
  164.3 1.5 collective-permute-start.43
  165.9 2.3 %collective-permute-done.43 = f32[8,768]{1,0:T(8,128)S(1)} collective-permute-done((f32[8,768]{1,0:T(8,128)S(1)}, f32[8,768]{1,0:T(8,128)S(1)}, u32[]{:S(2)}, u32[]{:S(2)}) %collective-permute-start.43) | collective-permute-done | bytes 24608 | tf_op jit(solution)/shard_map/ppermute | solution.py:552
  168.8 3.2 %collective-permute-done.44 = f32[8,768]{1,0:T(8,128)S(1)} collective-permute-done((f32[8,768]{1,0:T(8,128)S(1)}, f32[8,768]{1,0:T(8,128)S(1)}, u32[]{:S(2)}, u32[]{:S(2)}) %collective-permute-start.44) | collective-permute-done | bytes 24608 | tf_op jit(solution)/shard_map/ppermute | solution.py:552
  172.0 3.8 %collective-permute-done.45 = f32[8,768]{1,0:T(8,128)S(1)} collective-permute-done((f32[8,768]{1,0:T(8,128)S(1)}, f32[8,768]{1,0:T(8,128)S(1)}, u32[]{:S(2)}, u32[]{:S(2)}) %collective-permute-start.45) | collective-permute-done | bytes 24608 | tf_op jit(solution)/shard_map/ppermute | solution.py:552
  175.8 1.4 collective-permute-start.46
  177.2 3.4 %collective-permute-done.46 = f32[8,768]{1,0:T(8,128)S(1)} collective-permute-done((f32[8,768]{1,0:T(8,128)S(1)}, f32[8,768]{1,0:T(8,128)S(1)}, u32[]{:S(2)}, u32[]{:S(2)}) %collective-permute-start.46) | collective-permute-done | bytes 24608 | tf_op jit(solution)/shard_map/ppermute | solution.py:552
  (142 shorter events, 20.7 us)
Async XLA Ops:
  2.2 9.8 %collective-permute-start.2 = (bf16[768,768]{1,0:T(8,128)(2,1)S(1)}, bf16[768,768]{1,0:T(8,128)(2,1)}, u32[]{:S(2)}, u32[]{:S(2)}) collective-permute-start(bf16[768,768]{1,0:T(8,128)(2,1)S(1)} %pad_maximum_fusion.wb_ref.w_ref), channel_id=1, source_target_pairs={{0,1},{1,0},{2,3},{3,2},{4,5},{5,4},{6,7},{7,6},{8,9},{9,8},{10,11... | collective-permute-start | bytes 3538952 | tf_op jit(solution)/shard_map/ppermute | solution.py:552
  2.7 9.3 %collective-permute-start.3 = (bf16[768,768]{1,0:T(8,128)(2,1)S(1)}, bf16[768,768]{1,0:T(8,128)(2,1)}, u32[]{:S(2)}, u32[]{:S(2)}) collective-permute-start(bf16[768,768]{1,0:T(8,128)(2,1)S(1)} %copy-done.12), channel_id=1, source_target_pairs={{0,1},{1,0},{2,3},{3,2},{4,5},{5,4},{6,7},{7,6},{8,9},{9,8},{10,11... | collective-permute-start | bytes 3538952 | tf_op jit(solution)/shard_map/ppermute | solution.py:552
  2.8 9.2 %collective-permute-start.4 = (bf16[768,768]{1,0:T(8,128)(2,1)}, bf16[768,768]{1,0:T(8,128)(2,1)}, u32[]{:S(2)}, u32[]{:S(2)}) collective-permute-start(bf16[768,768]{1,0:T(8,128)(2,1)} %down_ref.1), channel_id=1, source_target_pairs={{0,1},{1,0},{2,3},{3,2},{4,5},{5,4},{6,7},{7,6},{8,9},{9,8},{10,11... | collective-permute-start | bytes 3538952 | tf_op jit(solution)/shard_map/ppermute | solution.py:552
  4.8 5.2 %collective-permute-start.1 = (f32[8]{0:T(128)S(1)}, f32[8]{0:T(128)S(1)}, u32[]{:S(2)}, u32[]{:S(2)}) collective-permute-start(f32[8]{0:T(128)S(1)} %convert_reduce_fusion), channel_id=1, source_target_pairs={{0,2},{1,3},{2,0},{3,1},{4,6},{5,7},{6,4},{7,5},{8,10},{9,11},{10,... | collective-permute-start | bytes 104 | tf_op jit(solution)/shard_map/ppermute | solution.py:552
  7.4 16.2 %collective-permute-start = (bf16[384,768]{1,0:T(8,128)(2,1)S(1)}, bf16[384,768]{1,0:T(8,128)(2,1)S(1)}, u32[]{:S(2)}, u32[]{:S(2)}) collective-permute-start(bf16[384,768]{1,0:T(8,128)(2,1)S(1)} %fusion), channel_id=1, source_target_pairs={{0,2},{1,3},{2,0},{3,1},{4,6},{5,7},{6,4},{7,5},{8,10},{9,11},{10,... | collective-permute-start | bytes 1769480 | tf_op jit(solution)/shard_map/ppermute | solution.py:552
  10.0 27.3 %collective-permute-start.10 = (bf16[384,768]{1,0:T(8,128)(2,1)S(1)}, bf16[384,768]{1,0:T(8,128)(2,1)S(1)}, u32[]{:S(2)}, u32[]{:S(2)}) collective-permute-start(bf16[384,768]{1,0:T(8,128)(2,1)S(1)} %constant_dynamic-slice_fusion.1), channel_id=1, source_target_pairs={{0,2},{1,3},{2,0},{3,1},{4,6},{5,7},{6,4},{7,5},{8,10},{9,11},{10,... | collective-permute-start | bytes 1769480 | tf_op jit(solution)/shard_map/ppermute | solution.py:552
  12.0 8.3 %collective-permute-start.5 = (f32[8]{0:T(128)S(1)}, f32[8]{0:T(128)S(1)}, u32[]{:S(2)}, u32[]{:S(2)}) collective-permute-start(f32[8]{0:T(128)S(1)} %add.200), channel_id=1, source_target_pairs={{0,4},{4,0},{8,12},{12,8},{16,20},{20,16},{24,28},{28,24},{1,5},{5... | collective-permute-start | bytes 104 | tf_op jit(solution)/shard_map/ppermute | solution.py:552
  13.5 23.0 %copy-start.5 = (bf16[512,768]{1,0:T(8,128)(2,1)S(1)}, bf16[512,768]{1,0:T(8,128)(2,1)}, u32[]{:S(2)}) copy-start(bf16[512,768]{1,0:T(8,128)(2,1)} %refs_14_.1) | copy-start | bytes 2359300
  23.6 13.8 %collective-permute-start.9 = (bf16[384,768]{1,0:T(8,128)(2,1)S(1)}, bf16[384,768]{1,0:T(8,128)(2,1)S(1)}, u32[]{:S(2)}, u32[]{:S(2)}) collective-permute-start(bf16[384,768]{1,0:T(8,128)(2,1)S(1)} %collective-permute-done.refs_7_.h_ref), channel_id=1, source_target_pairs={{0,4},{4,0},{8,12},{12,8},{16,20},{20,16},{24,28},{28,24},{1,5},{5... | collective-permute-start | bytes 1769480 | tf_op jit(solution)/shard_map/ppermute | solution.py:552
  25.0 14.5 %collective-permute-start.11 = (bf16[384,768]{1,0:T(8,128)(2,1)S(1)}, bf16[384,768]{1,0:T(8,128)(2,1)S(1)}, u32[]{:S(2)}, u32[]{:S(2)}) collective-permute-start(bf16[384,768]{1,0:T(8,128)(2,1)S(1)} %collective-permute-done.refs_7_.h_ref), channel_id=1, source_target_pairs={{0,1},{1,0},{2,3},{3,2},{4,5},{5,4},{6,7},{7,6},{8,9},{9,8},{10,11... | collective-permute-start | bytes 1769480 | tf_op jit(solution)/shard_map/ppermute | solution.py:552
  25.0 2.0 %collective-permute-start.6 = (f32[8]{0:T(128)S(1)}, f32[8]{0:T(128)S(1)}, u32[]{:S(2)}, u32[]{:S(2)}) collective-permute-start(f32[8]{0:T(128)S(1)} %add.201), channel_id=1, source_target_pairs={{0,1},{1,0},{2,3},{3,2},{4,5},{5,4},{6,7},{7,6},{8,9},{9,8},{10,11... | collective-permute-start | bytes 104 | tf_op jit(solution)/shard_map/ppermute | solution.py:552
  27.0 3.5 %collective-permute-start.7 = (f32[8]{0:T(128)S(1)}, f32[8]{0:T(128)S(1)}, u32[]{:S(2)}, u32[]{:S(2)}) collective-permute-start(f32[8]{0:T(128)S(1)} %add.202), channel_id=1, source_target_pairs={{0,8},{4,12},{8,0},{12,4},{16,24},{20,28},{24,16},{28,20},{1,9},{5... | collective-permute-start | bytes 104 | tf_op jit(solution)/shard_map/ppermute | solution.py:552
  30.6 4.4 %collective-permute-start.8 = (f32[8]{0:T(128)S(1)}, f32[8]{0:T(128)S(1)}, u32[]{:S(2)}, u32[]{:S(2)}) collective-permute-start(f32[8]{0:T(128)S(1)} %add.203), channel_id=1, source_target_pairs={{0,16},{4,20},{8,24},{12,28},{16,0},{20,4},{24,8},{28,12},{1,17},{... | collective-permute-start | bytes 104 | tf_op jit(solution)/shard_map/ppermute | solution.py:552
  37.4 2.2 %collective-permute-start.12 = (bf16[384,768]{1,0:T(8,128)(2,1)S(1)}, bf16[384,768]{1,0:T(8,128)(2,1)S(1)}, u32[]{:S(2)}, u32[]{:S(2)}) collective-permute-start(bf16[384,768]{1,0:T(8,128)(2,1)S(1)} %collective-permute-done.9.refs_8_.i_ref), channel_id=1, source_target_pairs={{0,1},{1,0},{2,3},{3,2},{4,5},{5,4},{6,7},{7,6},{8,9},{9,8},{10,11... | collective-permute-start | bytes 1769480 | tf_op jit(solution)/shard_map/ppermute | solution.py:552
  37.4 16.0 %collective-permute-start.14 = (bf16[768,384]{1,0:T(8,128)(2,1)S(1)}, bf16[768,384]{1,0:T(8,128)(2,1)S(1)}, u32[]{:S(2)}, u32[]{:S(2)}) collective-permute-start(bf16[768,384]{1,0:T(8,128)(2,1)S(1)} %constant_dynamic-slice_fusion), channel_id=1, source_target_pairs={{0,2},{1,3},{2,0},{3,1},{4,6},{5,7},{6,4},{7,5},{8,10},{9,11},{10,... | collective-permute-start | bytes 1769480 | tf_op jit(solution)/shard_map/ppermute | solution.py:552
  38.1 32.7 %collective-permute-start.18 = (bf16[384,768]{1,0:T(8,128)(2,1)S(1)}, bf16[384,768]{1,0:T(8,128)(2,1)S(1)}, u32[]{:S(2)}, u32[]{:S(2)}) collective-permute-start(bf16[384,768]{1,0:T(8,128)(2,1)S(1)} %collective-permute-done.10.refs_7_), channel_id=1, source_target_pairs={{0,1},{1,0},{2,3},{3,2},{4,5},{5,4},{6,7},{7,6},{8,9},{9,8},{10,11... | collective-permute-start | bytes 1769480 | tf_op jit(solution)/shard_map/ppermute | solution.py:552
  38.3 15.5 %collective-permute-start.13 = (bf16[384,768]{1,0:T(8,128)(2,1)S(1)}, bf16[384,768]{1,0:T(8,128)(2,1)S(1)}, u32[]{:S(2)}, u32[]{:S(2)}) collective-permute-start(bf16[384,768]{1,0:T(8,128)(2,1)S(1)} %collective-permute-done.10.refs_7_), channel_id=1, source_target_pairs={{0,4},{4,0},{8,12},{12,8},{16,20},{20,16},{24,28},{28,24},{1,5},{5... | collective-permute-start | bytes 1769480 | tf_op jit(solution)/shard_map/ppermute | solution.py:552
  53.8 18.6 %collective-permute-start.20 = (bf16[768,384]{1,0:T(8,128)(2,1)S(1)}, bf16[768,384]{1,0:T(8,128)(2,1)S(1)}, u32[]{:S(2)}, u32[]{:S(2)}) collective-permute-start(bf16[768,384]{1,0:T(8,128)(2,1)S(1)} %collective-permute-done.14.refs_9_), channel_id=1, source_target_pairs={{0,1},{1,0},{2,3},{3,2},{4,5},{5,4},{6,7},{7,6},{8,9},{9,8},{10,11... | collective-permute-start | bytes 1769480 | tf_op jit(solution)/shard_map/ppermute | solution.py:552
  53.8 15.7 %collective-permute-start.15 = (bf16[768,384]{1,0:T(8,128)(2,1)S(1)}, bf16[768,384]{1,0:T(8,128)(2,1)S(1)}, u32[]{:S(2)}, u32[]{:S(2)}) collective-permute-start(bf16[768,384]{1,0:T(8,128)(2,1)S(1)} %collective-permute-done.14.refs_9_), channel_id=1, source_target_pairs={{0,4},{4,0},{8,12},{12,8},{16,20},{20,16},{24,28},{28,24},{1,5},{5... | collective-permute-start | bytes 1769480 | tf_op jit(solution)/shard_map/ppermute | solution.py:552
  55.1 7.3 %collective-permute-start.16 = (bf16[768,768]{1,0:T(8,128)(2,1)S(1)}, bf16[768,768]{1,0:T(8,128)(2,1)S(1)}, u32[]{:S(2)}, u32[]{:S(2)}) collective-permute-start(bf16[768,768]{1,0:T(8,128)(2,1)S(1)} %get-tuple-element.153), channel_id=1, source_target_pairs={{0,1},{1,0},{2,3},{3,2},{4,5},{5,4},{6,7},{7,6},{8,9},{9,8},{10,11... | collective-permute-start | bytes 3538952 | tf_op jit(solution)/shard_map/ppermute | solution.py:552
  55.3 7.5 %collective-permute-start.17 = (bf16[768,768]{1,0:T(8,128)(2,1)S(1)}, bf16[768,768]{1,0:T(8,128)(2,1)S(1)}, u32[]{:S(2)}, u32[]{:S(2)}) collective-permute-start(bf16[768,768]{1,0:T(8,128)(2,1)S(1)} %get-tuple-element.155), channel_id=1, source_target_pairs={{0,1},{1,0},{2,3},{3,2},{4,5},{5,4},{6,7},{7,6},{8,9},{9,8},{10,11... | collective-permute-start | bytes 3538952 | tf_op jit(solution)/shard_map/ppermute | solution.py:552
  62.4 10.0 %collective-permute-start.19 = (bf16[384,768]{1,0:T(8,128)(2,1)S(1)}, bf16[384,768]{1,0:T(8,128)(2,1)S(1)}, u32[]{:S(2)}, u32[]{:S(2)}) collective-permute-start(bf16[384,768]{1,0:T(8,128)(2,1)S(1)} %collective-permute-done.13.refs_8_), channel_id=1, source_target_pairs={{0,1},{1,0},{2,3},{3,2},{4,5},{5,4},{6,7},{7,6},{8,9},{9,8},{10,11... | collective-permute-start | bytes 1769480 | tf_op jit(solution)/shard_map/ppermute | solution.py:552
  69.6 2.8 %collective-permute-start.21 = (bf16[768,384]{1,0:T(8,128)(2,1)S(1)}, bf16[768,384]{1,0:T(8,128)(2,1)S(1)}, u32[]{:S(2)}, u32[]{:S(2)}) collective-permute-start(bf16[768,384]{1,0:T(8,128)(2,1)S(1)} %collective-permute-done.15.refs_10_), channel_id=1, source_target_pairs={{0,1},{1,0},{2,3},{3,2},{4,5},{5,4},{6,7},{7,6},{8,9},{9,8},{10,11... | collective-permute-start | bytes 1769480 | tf_op jit(solution)/shard_map/ppermute | solution.py:552
  69.6 18.8 %collective-permute-start.24 = (bf16[384,768]{1,0:T(8,128)(2,1)S(1)}, bf16[384,768]{1,0:T(8,128)(2,1)S(1)}, u32[]{:S(2)}, u32[]{:S(2)}) collective-permute-start(bf16[384,768]{1,0:T(8,128)(2,1)S(1)} %add_convert_fusion.7), channel_id=1, source_target_pairs={{0,4},{4,0},{8,12},{12,8},{16,20},{20,16},{24,28},{28,24},{1,5},{5... | collective-permute-start | bytes 1769480 | tf_op jit(solution)/shard_map/ppermute | solution.py:552
  70.8 17.6 %collective-permute-start.25 = (bf16[384,768]{1,0:T(8,128)(2,1)S(1)}, bf16[384,768]{1,0:T(8,128)(2,1)S(1)}, u32[]{:S(2)}, u32[]{:S(2)}) collective-permute-start(bf16[384,768]{1,0:T(8,128)(2,1)S(1)} %add_convert_fusion.6), channel_id=1, source_target_pairs={{0,8},{4,12},{8,0},{12,4},{16,24},{20,28},{24,16},{28,20},{1,9},{5... | collective-permute-start | bytes 1769480 | tf_op jit(solution)/shard_map/ppermute | solution.py:552
  78.5 9.6 %collective-permute-start.22 = (bf16[768,768]{1,0:T(8,128)(2,1)S(1)}, bf16[768,768]{1,0:T(8,128)(2,1)S(1)}, u32[]{:S(2)}, u32[]{:S(2)}) collective-permute-start(bf16[768,768]{1,0:T(8,128)(2,1)S(1)} %get-tuple-element.165), channel_id=1, source_target_pairs={{0,1},{1,0},{2,3},{3,2},{4,5},{5,4},{6,7},{7,6},{8,9},{9,8},{10,11... | collective-permute-start | bytes 3538952 | tf_op jit(solution)/shard_map/ppermute | solution.py:552
  78.6 9.7 %collective-permute-start.23 = (bf16[768,768]{1,0:T(8,128)(2,1)S(1)}, bf16[768,768]{1,0:T(8,128)(2,1)S(1)}, u32[]{:S(2)}, u32[]{:S(2)}) collective-permute-start(bf16[768,768]{1,0:T(8,128)(2,1)S(1)} %get-tuple-element.167), channel_id=1, source_target_pairs={{0,1},{1,0},{2,3},{3,2},{4,5},{5,4},{6,7},{7,6},{8,9},{9,8},{10,11... | collective-permute-start | bytes 3538952 | tf_op jit(solution)/shard_map/ppermute | solution.py:552
  88.4 15.4 %collective-permute-start.27 = (bf16[384,768]{1,0:T(8,128)(2,1)S(1)}, bf16[384,768]{1,0:T(8,128)(2,1)S(1)}, u32[]{:S(2)}, u32[]{:S(2)}) collective-permute-start(bf16[384,768]{1,0:T(8,128)(2,1)S(1)} %add_convert_fusion.5), channel_id=1, source_target_pairs={{0,4},{4,0},{8,12},{12,8},{16,20},{20,16},{24,28},{28,24},{1,5},{5... | collective-permute-start | bytes 1769480 | tf_op jit(solution)/shard_map/ppermute | solution.py:552
  89.1 15.0 %collective-permute-start.28 = (bf16[384,768]{1,0:T(8,128)(2,1)S(1)}, bf16[384,768]{1,0:T(8,128)(2,1)S(1)}, u32[]{:S(2)}, u32[]{:S(2)}) collective-permute-start(bf16[384,768]{1,0:T(8,128)(2,1)S(1)} %add_convert_fusion.4), channel_id=1, source_target_pairs={{0,8},{4,12},{8,0},{12,4},{16,24},{20,28},{24,16},{28,20},{1,9},{5... | collective-permute-start | bytes 1769480 | tf_op jit(solution)/shard_map/ppermute | solution.py:552
  95.5 8.9 %collective-permute-start.26 = (bf16[768,768]{1,0:T(8,128)(2,1)S(1)}, bf16[768,768]{1,0:T(8,128)(2,1)S(1)}, u32[]{:S(2)}, u32[]{:S(2)}) collective-permute-start(bf16[768,768]{1,0:T(8,128)(2,1)S(1)} %get-tuple-element.184), channel_id=1, source_target_pairs={{0,1},{1,0},{2,3},{3,2},{4,5},{5,4},{6,7},{7,6},{8,9},{9,8},{10,11... | collective-permute-start | bytes 3538952 | tf_op jit(solution)/shard_map/ppermute | solution.py:552
  104.5 17.5 %collective-permute-start.32 = (bf16[384,768]{1,0:T(8,128)(2,1)S(1)}, bf16[384,768]{1,0:T(8,128)(2,1)S(1)}, u32[]{:S(2)}, u32[]{:S(2)}) collective-permute-start(bf16[384,768]{1,0:T(8,128)(2,1)S(1)} %add_convert_fusion.3), channel_id=1, source_target_pairs={{0,4},{4,0},{8,12},{12,8},{16,20},{20,16},{24,28},{28,24},{1,5},{5... | collective-permute-start | bytes 1769480 | tf_op jit(solution)/shard_map/ppermute | solution.py:552
  105.9 16.8 %collective-permute-start.36 = (bf16[384,768]{1,0:T(8,128)(2,1)S(1)}, bf16[384,768]{1,0:T(8,128)(2,1)S(1)}, u32[]{:S(2)}, u32[]{:S(2)}) collective-permute-start(bf16[384,768]{1,0:T(8,128)(2,1)S(1)} %add_convert_fusion.2), channel_id=1, source_target_pairs={{0,2},{1,3},{2,0},{3,1},{4,6},{5,7},{6,4},{7,5},{8,10},{9,11},{10,... | collective-permute-start | bytes 1769480 | tf_op jit(solution)/shard_map/ppermute | solution.py:552
  107.5 25.0 %collective-permute-start.39 = (bf16[384,768]{1,0:T(8,128)(2,1)S(1)}, bf16[384,768]{1,0:T(8,128)(2,1)S(1)}, u32[]{:S(2)}, u32[]{:S(2)}) collective-permute-start(bf16[384,768]{1,0:T(8,128)(2,1)S(1)} %add_convert_fusion.1), channel_id=1, source_target_pairs={{0,2},{1,3},{2,0},{3,1},{4,6},{5,7},{6,4},{7,5},{8,10},{9,11},{10,... | collective-permute-start | bytes 1769480 | tf_op jit(solution)/shard_map/ppermute | solution.py:552
  114.7 9.8 %collective-permute-start.29 = (bf16[768,768]{1,0:T(8,128)(2,1)S(1)}, bf16[768,768]{1,0:T(8,128)(2,1)S(1)}, u32[]{:S(2)}, u32[]{:S(2)}) collective-permute-start(bf16[768,768]{1,0:T(8,128)(2,1)S(1)} %get-tuple-element.192), channel_id=1, source_target_pairs={{0,1},{1,0},{2,3},{3,2},{4,5},{5,4},{6,7},{7,6},{8,9},{9,8},{10,11... | collective-permute-start | bytes 3538952 | tf_op jit(solution)/shard_map/ppermute | solution.py:552
  122.1 11.4 %collective-permute-start.33 = (bf16[192,768]{1,0:T(8,128)(2,1)S(1)}, bf16[192,768]{1,0:T(8,128)(2,1)S(1)}, u32[]{:S(2)}, u32[]{:S(2)}) collective-permute-start(bf16[192,768]{1,0:T(8,128)(2,1)S(1)} %add_convert_fusion.11), channel_id=1, source_target_pairs={{0,8},{4,12},{8,0},{12,4},{16,24},{20,28},{24,16},{28,20},{1,9},{5... | collective-permute-start | bytes 884744 | tf_op jit(solution)/shard_map/ppermute | solution.py:552
  122.9 15.0 %collective-permute-start.37 = (bf16[192,768]{1,0:T(8,128)(2,1)S(1)}, bf16[192,768]{1,0:T(8,128)(2,1)S(1)}, u32[]{:S(2)}, u32[]{:S(2)}) collective-permute-start(bf16[192,768]{1,0:T(8,128)(2,1)S(1)} %add_convert_fusion.9), channel_id=1, source_target_pairs={{0,8},{4,12},{8,0},{12,4},{16,24},{20,28},{24,16},{28,20},{1,9},{5... | collective-permute-start | bytes 884744 | tf_op jit(solution)/shard_map/ppermute | solution.py:552
  124.6 16.3 %collective-permute-start.30 = (bf16[384,768]{1,0:T(8,128)(2,1)S(1)}, bf16[384,768]{1,0:T(8,128)(2,1)S(1)}, u32[]{:S(2)}, u32[]{:S(2)}) collective-permute-start(bf16[384,768]{1,0:T(8,128)(2,1)S(1)} %add_convert_fusion), channel_id=1, source_target_pairs={{0,4},{4,0},{8,12},{12,8},{16,20},{20,16},{24,28},{28,24},{1,5},{5... | collective-permute-start | bytes 1769480 | tf_op jit(solution)/shard_map/ppermute | solution.py:552
  132.6 13.5 %collective-permute-start.40 = (bf16[192,768]{1,0:T(8,128)(2,1)S(1)}, bf16[192,768]{1,0:T(8,128)(2,1)S(1)}, u32[]{:S(2)}, u32[]{:S(2)}) collective-permute-start(bf16[192,768]{1,0:T(8,128)(2,1)S(1)} %add_convert_fusion.8), channel_id=1, source_target_pairs={{0,4},{4,0},{8,12},{12,8},{16,20},{20,16},{24,28},{28,24},{1,5},{5... | collective-permute-start | bytes 884744 | tf_op jit(solution)/shard_map/ppermute | solution.py:552
  133.7 15.4 %collective-permute-start.34 = (bf16[192,768]{1,0:T(8,128)(2,1)S(1)}, bf16[192,768]{1,0:T(8,128)(2,1)S(1)}, u32[]{:S(2)}, u32[]{:S(2)}) collective-permute-start(bf16[192,768]{1,0:T(8,128)(2,1)S(1)} %add_convert_fusion.10), channel_id=1, source_target_pairs={{0,2},{1,3},{2,0},{3,1},{4,6},{5,7},{6,4},{7,5},{8,10},{9,11},{10,... | collective-permute-start | bytes 884744 | tf_op jit(solution)/shard_map/ppermute | solution.py:552
  138.0 10.9 %collective-permute-start.38 = (bf16[96,768]{1,0:T(8,128)(2,1)S(1)}, bf16[96,768]{1,0:T(8,128)(2,1)S(1)}, u32[]{:S(2)}, u32[]{:S(2)}) collective-permute-start(bf16[96,768]{1,0:T(8,128)(2,1)S(1)} %add_convert_fusion.14), channel_id=1, source_target_pairs={{0,16},{4,20},{8,24},{12,28},{16,0},{20,4},{24,8},{28,12},{1,17},{... | collective-permute-start | bytes 442376 | tf_op jit(solution)/shard_map/ppermute | solution.py:552
  141.0 14.2 %collective-permute-start.31 = (bf16[192,768]{1,0:T(8,128)(2,1)S(1)}, bf16[192,768]{1,0:T(8,128)(2,1)S(1)}, u32[]{:S(2)}, u32[]{:S(2)}) collective-permute-start(bf16[192,768]{1,0:T(8,128)(2,1)S(1)} %add_convert_fusion.12), channel_id=1, source_target_pairs={{0,8},{4,12},{8,0},{12,4},{16,24},{20,28},{24,16},{28,20},{1,9},{5... | collective-permute-start | bytes 884744 | tf_op jit(solution)/shard_map/ppermute | solution.py:552
  146.2 10.6 %collective-permute-start.41 = (bf16[96,768]{1,0:T(8,128)(2,1)S(1)}, bf16[96,768]{1,0:T(8,128)(2,1)S(1)}, u32[]{:S(2)}, u32[]{:S(2)}) collective-permute-start(bf16[96,768]{1,0:T(8,128)(2,1)S(1)} %add_convert_fusion.13), channel_id=1, source_target_pairs={{0,16},{4,20},{8,24},{12,28},{16,0},{20,4},{24,8},{28,12},{1,17},{... | collective-permute-start | bytes 442376 | tf_op jit(solution)/shard_map/ppermute | solution.py:552
  155.3 6.2 %collective-permute-start.35 = (bf16[96,768]{1,0:T(8,128)(2,1)S(1)}, bf16[96,768]{1,0:T(8,128)(2,1)S(1)}, u32[]{:S(2)}, u32[]{:S(2)}) collective-permute-start(bf16[96,768]{1,0:T(8,128)(2,1)S(1)} %add_convert_fusion.15), channel_id=1, source_target_pairs={{0,16},{4,20},{8,24},{12,28},{16,0},{20,4},{24,8},{28,12},{1,17},{... | collective-permute-start | bytes 442376 | tf_op jit(solution)/shard_map/ppermute | solution.py:552
  163.1 1.2 collective-permute-start.42
  164.3 3.8 %collective-permute-start.43 = (f32[8,768]{1,0:T(8,128)S(1)}, f32[8,768]{1,0:T(8,128)S(1)}, u32[]{:S(2)}, u32[]{:S(2)}) collective-permute-start(f32[8,768]{1,0:T(8,128)S(1)} %add.257), channel_id=1, source_target_pairs={{0,2},{1,3},{2,0},{3,1},{4,6},{5,7},{6,4},{7,5},{8,10},{9,11},{10,... | collective-permute-start | bytes 73736 | tf_op jit(solution)/shard_map/ppermute | solution.py:552
  168.2 3.8 %collective-permute-start.44 = (f32[8,768]{1,0:T(8,128)S(1)}, f32[8,768]{1,0:T(8,128)S(1)}, u32[]{:S(2)}, u32[]{:S(2)}) collective-permute-start(f32[8,768]{1,0:T(8,128)S(1)} %add.258), channel_id=1, source_target_pairs={{0,4},{4,0},{8,12},{12,8},{16,20},{20,16},{24,28},{28,24},{1,5},{5... | collective-permute-start | bytes 73736 | tf_op jit(solution)/shard_map/ppermute | solution.py:552
  172.0 3.8 %collective-permute-start.45 = (f32[8,768]{1,0:T(8,128)S(1)}, f32[8,768]{1,0:T(8,128)S(1)}, u32[]{:S(2)}, u32[]{:S(2)}) collective-permute-start(f32[8,768]{1,0:T(8,128)S(1)} %add.259), channel_id=1, source_target_pairs={{0,8},{4,12},{8,0},{12,4},{16,24},{20,28},{24,16},{28,20},{1,9},{5... | collective-permute-start | bytes 73736 | tf_op jit(solution)/shard_map/ppermute | solution.py:552
  175.8 4.7 %collective-permute-start.46 = (f32[8,768]{1,0:T(8,128)S(1)}, f32[8,768]{1,0:T(8,128)S(1)}, u32[]{:S(2)}, u32[]{:S(2)}) collective-permute-start(f32[8,768]{1,0:T(8,128)S(1)} %add.260), channel_id=1, source_target_pairs={{0,16},{4,20},{8,24},{12,28},{16,0},{20,4},{24,8},{28,12},{1,17},{... | collective-permute-start | bytes 73736 | tf_op jit(solution)/shard_map/ppermute | solution.py:552
  (21 other events, 132.6 us)
